TPU v7x, 32 devices: a whole 2x2x4 slice. The times are simulated.
32 devices in a mesh: groups: 2 (over y), loop: 8 (over z, core), rep: 2 (over x).
Axes of the slice: x: 2, y: 2, z: 4, core: 2. Of those that a mesh axis runs over, the one named last changes fastest.
Arguments:
- documents: bfloat16 [16384, 1024], P(('groups', 'loop')), parts along dimension 0, may hold values from -6 to 6
- block_ids: int32 [16384, 3], P(('groups', 'loop')), parts along dimension 0, may hold values from 0 to 7, all different within a row; in each aligned block of 1024 rows (0 to 1023, 1024 to 2047, ...) at most 768 rows name the same one
- label_weight: bfloat16 [8192, 1024], P(('loop', 'rep')), may hold values from -0.1875 to 0.1875
- label_bias: bfloat16 [8192], P(('loop', 'rep')), may hold values from -2 to 1
- label_embed: bfloat16 [8192, 768], P(('loop', 'rep')), may hold values from -6 to 6
Outputs:
- pooled: bfloat16 [16384, 768], P(('groups', 'loop', 'rep')), parts along dimension 0
There are 2 independent parts, one for each index of `groups`. A program takes and returns all parts, laid end to end along the dimension named above; an argument that names none is the same for every part. Nothing has to cross between parts.
Inputs may be any that keep to these rules, and one draw needn't show every extreme that they name: `block_ids`: each row names 3 different label blocks; every block is named by some row; among the 1024 rows of one index of loop no block is named by more than 768 rows.
All inputs are finite; a program needn't handle non-finite values.
Results may differ from a plain program's by a relative error of at most 0.0048.
Values may be sent and summed in bfloat16 or wider, within the bound.
No kernel may reach another device: no remote copies, remote signals or barrier semaphores. Data moves between devices by JAX's collectives and lax.ppermute only.
A program may use at most 192 MiB of HBM per device.

v0:
```python
import jax
import jax.numpy as jnp
from jax import lax
from jax.sharding import PartitionSpec as P


def slot_layout(ids, block_count, slot_count):
    doc_count = ids.shape[0]
    blocks = jnp.arange(block_count, dtype=jnp.int32)
    member = jnp.any(ids[:, :, None] == blocks[None, None, :], axis=1).astype(jnp.int32)
    rank = jnp.cumsum(member, axis=0) - 1
    slot_ids = jnp.arange(slot_count, dtype=jnp.int32)
    hit = (member[:, :, None] > 0) & (rank[:, :, None] == slot_ids[None, None, :])
    owners = jnp.arange(doc_count, dtype=jnp.int32)[:, None, None]
    table = jnp.sum(jnp.where(hit, owners, 0), axis=0)
    empty = 1 - jnp.any(hit, axis=0).astype(jnp.int32)
    return (table + doc_count * empty, rank)


def score_rows(rows, weight_part, bias_part, embed_part):
    logits = lax.dot_general(
        rows, weight_part, (((1,), (1,)), ((), ())), preferred_element_type=jnp.float32
    )
    logits = logits + bias_part.astype(jnp.float32)[None, :]
    probs = jax.nn.sigmoid(logits)
    weights = probs.astype(jnp.bfloat16)
    mix = jnp.dot(weights, embed_part, preferred_element_type=jnp.float32)
    return (mix, jnp.sum(weights.astype(jnp.float32), axis=1))


def per_device(documents, block_ids, label_weight, label_bias, label_embed):
    doc_count = documents.shape[0]
    embed_width = label_embed.shape[1]
    shard_labels = label_weight.shape[0]
    picks = block_ids.shape[1]
    block_count = lax.axis_size("loop")
    slot_count = min(doc_count, 2 * doc_count * picks // block_count)
    table, rank = slot_layout(block_ids, block_count, slot_count)
    outgoing = jnp.take(documents, jnp.minimum(table, doc_count - 1), axis=0)

    def add_block(totals, weight_part, bias_part, embed_part, block):
        safe_block = jnp.clip(block, 0, block_count - 1)
        rows = lax.dynamic_index_in_dim(outgoing, safe_block, 0, keepdims=False)
        mix, sums = score_rows(rows, weight_part, bias_part, embed_part)
        old_mix = lax.dynamic_index_in_dim(totals[0], safe_block, 0, keepdims=True)
        old_sums = lax.dynamic_index_in_dim(totals[1], safe_block, 0, keepdims=True)
        new_mix = lax.dynamic_update_index_in_dim(totals[0], old_mix + mix[None], safe_block, 0)
        new_sums = lax.dynamic_update_index_in_dim(totals[1], old_sums + sums[None], safe_block, 0)
        return (new_mix, new_sums)

    initial = (
        jnp.zeros((block_count, slot_count, embed_width), jnp.float32),
        jnp.zeros((block_count, slot_count), jnp.float32),
    )
    weight_piece = lax.all_gather(label_weight, "loop", axis=0, tiled=True)
    bias_piece = lax.all_gather(label_bias, "loop", axis=0, tiled=True)
    embed_piece = lax.all_gather(label_embed, "loop", axis=0, tiled=True)
    count = weight_piece.shape[0]
    shards = count // shard_labels
    weight_rows = weight_piece.reshape(shards, shard_labels, weight_piece.shape[1])
    bias_rows = bias_piece.reshape(shards, shard_labels)
    embed_rows = embed_piece.reshape(shards, shard_labels, embed_piece.shape[1])

    def one_shard(index, carry):
        return add_block(carry, weight_rows[index], bias_rows[index], embed_rows[index], index)

    slot_mix, slot_sums = lax.fori_loop(0, shards, one_shard, initial)
    flat_mix = slot_mix.reshape(block_count * slot_count, embed_width)
    flat_sums = slot_sums.reshape(block_count * slot_count)
    blocks = jnp.arange(block_count, dtype=jnp.int32)
    mixture = jnp.zeros((doc_count, embed_width), jnp.float32)
    weight_sum = jnp.zeros((doc_count,), jnp.float32)
    for pick in range(picks):
        chosen_block = block_ids[:, pick]
        onehot = chosen_block[:, None] == blocks[None, :]
        position = jnp.sum(jnp.where(onehot, rank, 0), axis=1)
        flat_index = chosen_block * slot_count + position
        mixture = mixture + jnp.take(flat_mix, flat_index, axis=0)
        weight_sum = weight_sum + jnp.take(flat_sums, flat_index, axis=0)
    mixture, weight_sum = (
        lax.psum_scatter(mixture, "rep", scatter_dimension=0, tiled=True),
        lax.psum_scatter(weight_sum, "rep", scatter_dimension=0, tiled=True),
    )
    return (mixture / jnp.sqrt(1.0 + weight_sum)[:, None]).astype(jnp.bfloat16)


def solution(mesh):
    return jax.shard_map(
        per_device,
        mesh=mesh,
        in_specs=(
            P(("groups", "loop"), None),
            P(("groups", "loop"), None),
            P(("loop", "rep"), None),
            P(("loop", "rep")),
            P(("loop", "rep"), None),
        ),
        out_specs=P(("groups", "loop", "rep"), None),
        check_vma=False,
    )
```

profile of v0, /device:TPU:0, one launch (start us, length us, event | category | flops | bytes accessed | tf_op | source)
XLA Modules:
  0.0 336.6 jit_solution(10775033497560686792)
XLA Ops:
  16.1 5.7 %select_reduce_fusion = s32[8,768]{1,0:T(8,128)S(1)} fusion(s32[1024,8]{1,0:T(8,128)S(1)} %copy.20, pred[1024,8]{1,0:T(8,128)(4,1)S(1)} %copy.19), kind=kLoop, calls=%fused_computation.22 | loop fusion | flops 25159680 | bytes 65536 | tf_op jit(solution)/shard_map/reduce_sum | solution.py:15
  21.8 14.6 %all-gather = bf16[8,1,512]{2,1,0:T(2,128)(2,1)S(1)} all-gather(bf16[1,1,512]{2,1,0:T(2,128)(2,1)S(1)} %reshape.164), channel_id=1, replica_groups=mesh['groups'=2,'loop'=8,'rep'=2] {'loop'}, dimensions={0}, use_global_device_ids=true | all-gather | bytes 9216 | tf_op jit(solution)/shard_map/all_gather | solution.py:56
  36.5 26.9 %gather_fusion = bf16[6144,1024]{1,0:T(8,128)(2,1)} fusion(bf16[1024,1024]{1,0:T(8,128)(2,1)S(1)} %copy-done, s32[6144]{0:T(1024)S(1)} %broadcast_clamp_fusion), kind=kCustom, calls=%fused_computation.6 | custom fusion | bytes 25190400 | tf_op jit(solution)/shard_map/jit(_take)/gather | solution.py:39
  63.5 10.9 %broadcast_select_fusion = bf16[8,768,1024]{2,1,0:T(8,128)(2,1)} fusion(bf16[8,768,1024]{2,1,0:T(8,128)(2,1)} %bitcast.76, pred[8,768]{1,0:T(8,128)(4,1)S(1)} %compare_and_fusion), kind=kLoop, calls=%fused_computation.26 | loop fusion | flops 6291456 | bytes 25171968 | tf_op jit(solution)/shard_map/jit(_take)/select_n | solution.py:39
  76.7 82.3 %all-gather.4.cloned.1.call-done = bf16[4096,1024]{1,0:T(8,128)(2,1)} async-done(((bf16[512,1024]{1,0:T(8,128)(2,1)}), bf16[4096,1024]{1,0:T(8,128)(2,1)}) %all-gather.4.cloned.1.call-update) | async-done | bytes 8388624 | tf_op jit(solution)/shard_map/all_gather | solution.py:55
  159.0 8.1 %broadcast_in_dim.74 = f32[8,768,768]{2,1,0:T(8,128)} broadcast(f32[]{:T(128)} %constant.109.clone.1), dimensions={} | broadcast | bytes 18874372 | tf_op jit(solution)/shard_map/broadcast_in_dim | solution.py:52
  167.1 57.6 %while.15 = (s32[]{:T(128)}, f32[8,768,768]{2,1,0:T(8,128)}, f32[8,768]{1,0:T(8,128)S(1)}, bf16[8,768,1024]{2,1,0:T(8,128)(2,1)}, bf16[8,512,1024]{2,1,0:T(8,128...) while((s32[]{:T(128)}, f32[8,768,768]{2,1,0:T(8,128)}, ...), condition=%wide.region_7.8_spmd, body=%wide.region_5.7_spmd.sunk | while | flops 1412628992 | bytes 9724049 | solution.py:67
  170.0 4.1 %fusion.23 = f32[8,768,768]{2,1,0:T(8,128)} fusion(f32[8,768,768]{2,1,0:T(8,128)} %get-tuple-element.222, s32[]{:T(128)S(6)} %min.40, bf16[768,512]{0,1:T(8,128)(2,1)S(1)} %get-tuple-element.209, bf16[8,512,768]{2,1,0:T(8,128)(2,1)} %get-tuple-element.237, s32[]{:T(128)} %get-tuple-element.221), kind=kOutput, calls=%fused_computation.8.clone.1 | convolution fusion | flops 604569600 | bytes 6291972 | tf_op jit(solution)/shard_map/while/body/eval_jaxpr/dot_general | solution.py:27
  177.2 4.1 %fusion.23 = f32[8,768,768]{2,1,0:T(8,128)} fusion(f32[8,768,768]{2,1,0:T(8,128)} %get-tuple-element.222, s32[]{:T(128)S(6)} %min.40, bf16[768,512]{0,1:T(8,128)(2,1)S(1)} %get-tuple-element.209, bf16[8,512,768]{2,1,0:T(8,128)(2,1)} %get-tuple-element.237, s32[]{:T(128)} %get-tuple-element.221), kind=kOutput, calls=%fused_computation.8.clone.1 | convolution fusion | flops 604569600 | bytes 6291972 | tf_op jit(solution)/shard_map/while/body/eval_jaxpr/dot_general | solution.py:27
  184.4 4.2 %fusion.23 = f32[8,768,768]{2,1,0:T(8,128)} fusion(f32[8,768,768]{2,1,0:T(8,128)} %get-tuple-element.222, s32[]{:T(128)S(6)} %min.40, bf16[768,512]{0,1:T(8,128)(2,1)S(1)} %get-tuple-element.209, bf16[8,512,768]{2,1,0:T(8,128)(2,1)} %get-tuple-element.237, s32[]{:T(128)} %get-tuple-element.221), kind=kOutput, calls=%fused_computation.8.clone.1 | convolution fusion | flops 604569600 | bytes 6291972 | tf_op jit(solution)/shard_map/while/body/eval_jaxpr/dot_general | solution.py:27
  191.6 4.2 %fusion.23 = f32[8,768,768]{2,1,0:T(8,128)} fusion(f32[8,768,768]{2,1,0:T(8,128)} %get-tuple-element.222, s32[]{:T(128)S(6)} %min.40, bf16[768,512]{0,1:T(8,128)(2,1)S(1)} %get-tuple-element.209, bf16[8,512,768]{2,1,0:T(8,128)(2,1)} %get-tuple-element.237, s32[]{:T(128)} %get-tuple-element.221), kind=kOutput, calls=%fused_computation.8.clone.1 | convolution fusion | flops 604569600 | bytes 6291972 | tf_op jit(solution)/shard_map/while/body/eval_jaxpr/dot_general | solution.py:27
  198.8 4.1 %fusion.23 = f32[8,768,768]{2,1,0:T(8,128)} fusion(f32[8,768,768]{2,1,0:T(8,128)} %get-tuple-element.222, s32[]{:T(128)S(6)} %min.40, bf16[768,512]{0,1:T(8,128)(2,1)S(1)} %get-tuple-element.209, bf16[8,512,768]{2,1,0:T(8,128)(2,1)} %get-tuple-element.237, s32[]{:T(128)} %get-tuple-element.221), kind=kOutput, calls=%fused_computation.8.clone.1 | convolution fusion | flops 604569600 | bytes 6291972 | tf_op jit(solution)/shard_map/while/body/eval_jaxpr/dot_general | solution.py:27
  206.0 4.2 %fusion.23 = f32[8,768,768]{2,1,0:T(8,128)} fusion(f32[8,768,768]{2,1,0:T(8,128)} %get-tuple-element.222, s32[]{:T(128)S(6)} %min.40, bf16[768,512]{0,1:T(8,128)(2,1)S(1)} %get-tuple-element.209, bf16[8,512,768]{2,1,0:T(8,128)(2,1)} %get-tuple-element.237, s32[]{:T(128)} %get-tuple-element.221), kind=kOutput, calls=%fused_computation.8.clone.1 | convolution fusion | flops 604569600 | bytes 6291972 | tf_op jit(solution)/shard_map/while/body/eval_jaxpr/dot_general | solution.py:27
  213.3 4.1 %fusion.23 = f32[8,768,768]{2,1,0:T(8,128)} fusion(f32[8,768,768]{2,1,0:T(8,128)} %get-tuple-element.222, s32[]{:T(128)S(6)} %min.40, bf16[768,512]{0,1:T(8,128)(2,1)S(1)} %get-tuple-element.209, bf16[8,512,768]{2,1,0:T(8,128)(2,1)} %get-tuple-element.237, s32[]{:T(128)} %get-tuple-element.221), kind=kOutput, calls=%fused_computation.8.clone.1 | convolution fusion | flops 604569600 | bytes 6291972 | tf_op jit(solution)/shard_map/while/body/eval_jaxpr/dot_general | solution.py:27
  220.5 4.2 %fusion.23 = f32[8,768,768]{2,1,0:T(8,128)} fusion(f32[8,768,768]{2,1,0:T(8,128)} %get-tuple-element.222, s32[]{:T(128)S(6)} %min.40, bf16[768,512]{0,1:T(8,128)(2,1)S(1)} %get-tuple-element.209, bf16[8,512,768]{2,1,0:T(8,128)(2,1)} %get-tuple-element.237, s32[]{:T(128)} %get-tuple-element.221), kind=kOutput, calls=%fused_computation.8.clone.1 | convolution fusion | flops 604569600 | bytes 6291972 | tf_op jit(solution)/shard_map/while/body/eval_jaxpr/dot_general | solution.py:27
  224.7 6.2 %gather_fusion.5 = f32[1024]{0:T(1024)S(1)} fusion(f32[6144]{0:T(1024)S(1)} %reshape.96, s32[1024]{0:T(1024)S(1)} %get-tuple-element.163), kind=kCustom, calls=%fused_computation.4.clone | custom fusion | bytes 12288 | tf_op jit(solution)/shard_map/jit(_take)/gather | solution.py:79
  230.9 6.2 %gather_fusion.6 = f32[1024]{0:T(1024)S(1)} fusion(f32[6144]{0:T(1024)S(1)} %reshape.96, s32[1024]{0:T(1024)S(1)} %get-tuple-element.162), kind=kCustom, calls=%fused_computation.5.clone | custom fusion | bytes 12288 | tf_op jit(solution)/shard_map/jit(_take)/gather | solution.py:79
  237.1 12.2 %gather_fusion.2 = f32[1024,768]{1,0:T(8,128)} fusion(f32[6144,768]{1,0:T(8,128)} %bitcast.73, s32[1024]{0:T(1024)S(1)} %get-tuple-element.163), kind=kCustom, calls=%fused_computation.2.clone | custom fusion | bytes 6295552 | tf_op jit(solution)/shard_map/jit(_take)/gather | solution.py:78
  249.3 12.3 %gather_fusion.3 = f32[1024,768]{1,0:T(8,128)} fusion(f32[6144,768]{1,0:T(8,128)} %bitcast.74, s32[1024]{0:T(1024)S(1)} %get-tuple-element.162), kind=kCustom, calls=%fused_computation.3.clone | custom fusion | bytes 6295552 | tf_op jit(solution)/shard_map/jit(_take)/gather | solution.py:78
  261.6 6.1 %gather_fusion.4 = f32[1024]{0:T(1024)S(1)} fusion(f32[6144]{0:T(1024)S(1)} %reshape.96, s32[1024]{0:T(1024)S(1)} %broadcast_clamp_fusion.3), kind=kCustom, calls=%fused_computation.1.clone | custom fusion | bytes 12288 | tf_op jit(solution)/shard_map/jit(_take)/gather | solution.py:79
  267.7 12.2 %gather_fusion.1 = f32[1024,768]{1,0:T(8,128)} fusion(f32[6144,768]{1,0:T(8,128)} %bitcast.75, s32[1024]{0:T(1024)S(1)} %broadcast_clamp_fusion.3), kind=kCustom, calls=%fused_computation.clone | custom fusion | bytes 6295552 | tf_op jit(solution)/shard_map/jit(_take)/gather | solution.py:78
  280.0 5.5 %select_add_fusion = f32[1024,768]{1,0:T(8,128)} fusion(f32[1024,768]{1,0:T(8,128)} %gather_fusion.3, f32[1024,768]{1,0:T(8,128)} %gather_fusion.2, f32[1024,768]{1,0:T(8,128)} %gather_fusion.1, pred[1024]{0:T(1024)(128)(4,1)S(1)} %get-tuple-element.154, pred[1024]{0:T(1024)(128)(4,1)S(1)} %get-tuple-element.153, pred[1024]{0:T(1024)(128)(4,1)S(1)} %get-tuple-element.152), kind=kLoop, calls=%fused_computation.27 | loop fusion | flops 3932160 | bytes 12585984 | tf_op jit(solution)/shard_map/add | solution.py:78
  287.4 5.0 %all-reduce = f32[1024]{0:T(1024)S(1)} all-reduce(f32[1024]{0:T(1024)S(1)} %get-tuple-element.151), channel_id=3, replica_groups=mesh['groups'=2,'loop'=8,'rep'=2] {'rep'}, use_global_device_ids=true, to_apply=%region_12.15.clone | all-reduce | flops 1024 | bytes 8192
  292.4 35.2 %reduce-scatter.2.cloned.1.call-done = f32[512,768]{1,0:T(8,128)} async-done(((f32[1024,768]{1,0:T(8,128)}), f32[512,768]{1,0:T(8,128)}) %reduce-scatter.2.cloned.1.call-update) | async-done | bytes 1572880 | tf_op jit(solution)/shard_map/reduce_scatter | solution.py:81
  (76 shorter events, 39.6 us)
Async XLA Ops:
  6.5 29.9 %copy-start = (bf16[1024,1024]{1,0:T(8,128)(2,1)S(1)}, bf16[1024,1024]{1,0:T(8,128)(2,1)}, u32[]{:S(2)}) copy-start(bf16[1024,1024]{1,0:T(8,128)(2,1)} %param.11) | copy-start | bytes 6291460
  6.5 15.3 %copy-start.3 = (bf16[512]{0:T(512)(128)(2,1)S(1)}, bf16[512]{0:T(512)(128)(2,1)}, u32[]{:S(2)}) copy-start(bf16[512]{0:T(512)(128)(2,1)} %param.14) | copy-start | bytes 3076
  6.5 70.1 %all-gather.6.cloned.1.call-start = ((), (), s32[]{:S(2)}) async-start(), calls=%async_computation.2 | async-start | bytes 7077888 | tf_op jit(solution)/shard_map/all_gather | solution.py:57
  7.3 151.7 %all-gather.4.cloned.1.call-start = ((), (), s32[]{:S(2)}) async-start(), calls=%async_computation.1 | async-start | bytes 9437184 | tf_op jit(solution)/shard_map/all_gather | solution.py:55
  8.0 319.6 %reduce-scatter.2.cloned.1.call-start = ((), (), s32[]{:S(2)}) async-start(), calls=%async_computation.3 | async-start | bytes 4718592 | tf_op jit(solution)/shard_map/reduce_scatter | solution.py:81
  36.5 26.9 %copy-start.2 = (s32[1024,3]{0,1:T(4,128)S(1)}, s32[1024,3]{0,1:T(4,128)}, u32[]{:S(2)}) copy-start(s32[1024,3]{0,1:T(4,128)} %param.12) | copy-start | bytes 36868
  279.9 50.1 %copy-start.1 = (bf16[1024,1024]{1,0:T(8,128)(2,1)S(1)}, bf16[1024,1024]{1,0:T(8,128)(2,1)}, u32[]{:S(2)}) copy-start(bf16[1024,1024]{1,0:T(8,128)(2,1)} %param.11) | copy-start | bytes 6291460
  285.5 0.7 copy-start.4
Sparse Core Ops, SparseCore 0:
  9.0 67.6 all-gather.5
  78.3 80.6 all-gather.3
  285.6 41.9 reduce-scatter.1
where the time goes:
time: 337 us
  waiting for transfers between devices  121 us (36%)
  local copies, waits for them, and re-layouts  92.8 us (28%)
  matrix products  56.5 us (17%)
  other arithmetic  32.1 us (10%)
  blocking collectives  19.6 us (6%)
  between operations  14 us (4%)
    all_gather x1, waiting for transfers between devices, per_device(): weight_piece = lax.all_gather(label_weight, 'loop', axis=0, tiled=True)  82.3 us
    gather x3, local copies, waits for them, and re-layouts, per_device(): mixture = mixture + jnp.take(flat_mix, flat_index, axis=0)  36.7 us
    reduce_scatter x1, waiting for transfers between devices, per_device(): lax.psum_scatter(mixture, 'rep', scatter_dimension=0, tiled=True)  35.2 us
    dot_general x8, matrix products, score_rows(): mix = jnp.dot(weights, embed_part, preferred_element_type=jnp.float32)  33.3 us
    gather x1, local copies, waits for them, and re-layouts, per_device(): outgoing = jnp.take(documents, jnp.minimum(table, doc_count - 1), axis=0)  26.9 us
    dot_general x8, matrix products, score_rows(): lax.dot_general(rows, weight_part, (((1,), (1,)), ((), ())), preferred_el...  23.1 us
    gather x3, local copies, waits for them, and re-layouts, per_device(): weight_sum = weight_sum + jnp.take(flat_sums, flat_index, axis=0)  18.5 us
    all_gather x1, blocking collectives, per_device(): bias_piece = lax.all_gather(label_bias, 'loop', axis=0, tiled=True)  14.6 us
  transfers between devices with their start and end apart: 3, of which 3 were waited for; matrix products, arithmetic and copies ran while one was open for 16% of the time, Pallas kernels for 0%

commit v1 on v0

v1 whole, which is shorter than its diff:
```python
import functools

import jax
import jax.numpy as jnp
from jax import lax
from jax.experimental import pallas as pl
from jax.experimental.pallas import tpu as pltpu
from jax.sharding import PartitionSpec as P

AXES = ("groups", "loop", "rep")
DOC_TILE = 256


def accumulate(spec, table, *refs):
    step, packed, pieces, parts, part_rows, offset, first, final, groups = spec
    docs_ref, ids_ref, bias_ref = refs[:3]
    at = 3
    weight_rows, embed_rows = [], []
    for _ in range(pieces):
        if packed:
            width = docs_ref.shape[1]
            weight_rows.append(refs[at][:, :width])
            embed_rows.append(refs[at][:, width:])
            at += 1
        else:
            weight_rows.append(refs[at][...])
            embed_rows.append(refs[at + 1][...])
            at += 2
    if not first:
        mix_in, sum_in = refs[at], refs[at + 1]
        at += 2
    mix_out, sum_out = refs[at], refs[at + 1]
    group = table[0]
    cores = pieces // parts
    biases, masks = [], []
    ids = ids_ref[...]
    for core in range(cores):
        block = table[1 + 2 * step + core]
        chosen = jnp.max((ids == block).astype(jnp.float32), axis=1, keepdims=True)
        for part in range(parts):
            row = bias_ref[core : core + 1, :]
            rows = weight_rows[core * parts + part].shape[0]
            if parts == 1:
                piece = row
            else:
                owner = lax.rem(group + groups - part, groups)
                piece = row[:, offset : offset + rows]
                for other in range(1, groups):
                    start = other * part_rows + offset
                    piece = jnp.where(owner == other, row[:, start : start + rows], piece)
            biases.append(piece)
            masks.append(jnp.broadcast_to(chosen, (chosen.shape[0], rows)))
    joined = lambda xs, axis: xs[0] if len(xs) == 1 else jnp.concatenate(xs, axis=axis)
    logits = lax.dot_general(
        docs_ref[...],
        joined(weight_rows, 0),
        (((1,), (1,)), ((), ())),
        preferred_element_type=jnp.float32,
    )
    logits = logits + joined(biases, 1)
    weights = (joined(masks, 1) * jax.nn.sigmoid(logits)).astype(jnp.bfloat16)
    mix = jnp.dot(weights, joined(embed_rows, 0), preferred_element_type=jnp.float32)
    sums = jnp.sum(weights.astype(jnp.float32), axis=1, keepdims=True)
    if not first:
        mix = mix + mix_in[...]
        sums = sums + sum_in[...]
    mix_out[...] = mix.astype(mix_out.dtype)
    sum_out[...] = sums


def add_labels(table, docs, ids, bias, pieces, totals, *, step, packed, parts, part_rows, offset, groups, rows_of=None, out_dtype=jnp.float32):
    doc_count, width = docs.shape
    embed_width = pieces[0].shape[1] - width if packed else pieces[1].shape[1]
    first = totals is None
    final = rows_of is not None
    if final:
        tile_of, tiles, tile = rows_of
    else:
        tile = min(DOC_TILE, doc_count)
        tiles = doc_count // tile
        tile_of = lambda i, t: i
    moving = lambda i, t: (tile_of(i, t), 0)
    still = lambda i, t: (0, 0)
    count = len(pieces) if packed else len(pieces) // 2
    spec = (step, packed, count, parts, part_rows, offset, first, final, groups)
    labels = sum(p.shape[0] for p in pieces) // (1 if packed else 2)
    in_specs = [
        pl.BlockSpec((tile, width), moving),
        pl.BlockSpec((tile, ids.shape[1]), moving),
        pl.BlockSpec(bias.shape, still),
    ] + [pl.BlockSpec(p.shape, still) for p in pieces]
    operands = [docs, ids, bias, *pieces]
    aliases = {}
    if not first:
        in_specs += [pl.BlockSpec((tile, embed_width), moving), pl.BlockSpec((tile, 1), moving)]
        operands += list(totals)
        if not final:
            aliases = {len(operands) - 1: 0, len(operands): 1}
    out_map = (lambda i, t: (i, 0)) if final else moving
    return pl.pallas_call(
        functools.partial(accumulate, spec),
        grid_spec=pltpu.PrefetchScalarGridSpec(
            num_scalar_prefetch=1,
            grid=(tiles,),
            in_specs=in_specs,
            out_specs=[pl.BlockSpec((tile, embed_width), out_map), pl.BlockSpec((tile, 1), out_map)],
        ),
        out_shape=[
            jax.ShapeDtypeStruct((tiles * tile, embed_width), out_dtype),
            jax.ShapeDtypeStruct((tiles * tile, 1), jnp.float32),
        ],
        input_output_aliases=aliases,
        compiler_params=pltpu.CompilerParams(vmem_limit_bytes=40 * 1024 * 1024),
        cost_estimate=pl.CostEstimate(
            flops=2 * tiles * tile * labels * (width + embed_width),
            bytes_accessed=2 * tiles * tile * (width + 4 * embed_width) + 2 * labels * (width + embed_width),
            transcendentals=tiles * tile * labels,
        ),
    )(table, *operands)


def per_device(sizes, documents, block_ids, label_weight, label_bias, label_embed):
    groups, loop, reps = sizes
    cores = 2 if loop % 2 == 0 else 1
    chips = loop // cores
    doc_count, width = documents.shape
    shard = label_weight.shape[0]
    part_rows = shard // groups

    def moved(x, to):
        pairs = []
        for g in range(groups):
            for l in range(loop):
                for r in range(reps):
                    g2, z2, c2, r2 = to(g, l // cores, l % cores, r)
                    there = (g2 % groups, (z2 % chips) * cores + c2 % cores, r2 % reps)
                    number = lambda a: (a[0] * loop + a[1]) * reps + a[2]
                    pairs.append((number((g, l, r)), number(there)))
        return lax.ppermute(x, AXES, pairs)

    along = lambda x: moved(x, lambda g, z, c, r: (g, z + 1, c, r))
    across = lambda x, k: moved(x, lambda g, z, c, r: (g + k, z, c, r))
    other_core = lambda x: moved(x, lambda g, z, c, r: (g, z, c + 1, r))
    other_rep = lambda x, k: moved(x, lambda g, z, c, r: (g, z, c, r + k))

    group = lax.axis_index("groups")
    place = lax.axis_index("loop")
    rep = lax.axis_index("rep")
    chip, core = place // cores, place % cores
    entries = [group]
    for step in range(chips):
        for k in range(2):
            entries.append(((chip - step) % chips) * cores + (core + k) % cores)
    entries.append(rep)
    table = jnp.stack(entries).astype(jnp.int32)

    small = max(16, part_rows // 4 // 16 * 16)
    chunks = [(0, part_rows - small), (part_rows - small, small)]
    flying = []
    for offset, rows in chunks:
        start = group * part_rows + offset
        flying.append(
            jnp.concatenate(
                [
                    lax.dynamic_slice_in_dim(label_weight, start, rows, 0),
                    lax.dynamic_slice_in_dim(label_embed, start, rows, 0),
                ],
                axis=1,
            )
        )
    bias_row = label_bias.astype(jnp.float32)[None, :]
    bias = jnp.concatenate([bias_row, other_core(bias_row)], axis=0) if cores == 2 else bias_row

    own = [label_weight, label_embed]
    if cores == 2:
        own += [other_core(label_weight), other_core(label_embed)]
    call = functools.partial(add_labels, table, documents, block_ids)
    common = dict(part_rows=part_rows, groups=groups)
    totals = call(bias, own, None, step=0, packed=False, parts=1, offset=0, **common)
    for step in range(1, chips):
        bias = along(bias)
        for index, (offset, rows) in enumerate(chunks):
            flying[index] = along(flying[index])
            pieces = [flying[index]] + [across(flying[index], k) for k in range(1, groups)]
            if cores == 2:
                pieces += [other_core(p) for p in pieces]
            here = dict(step=step, packed=True, parts=groups, offset=offset, **common)
            if step < chips - 1 or index < len(chunks) - 1:
                totals = call(bias, pieces, totals, **here)
    tile_docs = doc_count // reps
    tile = min(DOC_TILE, tile_docs)
    subs = tile_docs // tile
    last = table.shape[0] - 1
    away_of = lambda i, t: lax.rem(t[last] + 1 + i // subs, reps) * subs + i % subs
    home_of = lambda i, t: t[last] * subs + i
    away_mix, away_sum = call(
        bias, pieces, totals, rows_of=(away_of, (reps - 1) * subs, tile), out_dtype=jnp.bfloat16, **here
    )
    home_mix, home_sum = call(bias, pieces, totals, rows_of=(home_of, subs, tile), **here)
    mixture, weight_sum = home_mix, home_sum
    for k in range(1, reps):
        part = slice((k - 1) * tile_docs, k * tile_docs)
        mixture = mixture + other_rep(away_mix[part], k).astype(jnp.float32)
        weight_sum = weight_sum + other_rep(away_sum[part].reshape(-1, 128), k).reshape(-1, 1)
    return (mixture / jnp.sqrt(1.0 + weight_sum)).astype(jnp.bfloat16)


def solution(mesh):
    sizes = tuple(mesh.shape[axis] for axis in AXES)
    return jax.shard_map(
        functools.partial(per_device, sizes),
        mesh=mesh,
        in_specs=(
            P(("groups", "loop"), None),
            P(("groups", "loop"), None),
            P(("loop", "rep"), None),
            P(("loop", "rep")),
            P(("loop", "rep"), None),
        ),
        out_specs=P(("groups", "loop", "rep"), None),
        check_vma=False,
    )
```

time: 337 us -> 179 us (0.53)
  local copies, waits for them, and re-layouts: 92.8 us -> 25.3 us
  matrix products: 56.5 us -> 0 us
  Pallas kernels: 0 us -> 37 us
  waiting for transfers between devices: 121 us -> 93.4 us
  other arithmetic: 32.1 us -> 5 us
  blocking collectives: 19.6 us -> 0 us
  starting transfers between devices: 0.08 us -> 16.6 us
  between operations: 14 us -> 0.4 us
    ppermute x0 -> x32, waiting for transfers between devices: none -> 93.4 us  [moved(): return lax.ppermute(x, AXES, pairs)]
    all_gather x2 -> x0, waiting for transfers between devices: 84.6 us -> none  [the longest x1 82.3 us: per_device(): weight_piece = lax.all_gather(label_weight, 'loop', axis=0, tiled=True)]
    gather x7 -> x0, local copies, waits for them, and re-layouts: 82 us -> none  [the longest x3 36.7 us: per_device(): mixture = mixture + jnp.take(flat_mix, flat_index, axis=0)]
    dot_general x16 -> x0, matrix products: 56.5 us -> none  [the longest x8 33.3 us: score_rows(): mix = jnp.dot(weights, embed_part, preferred_element_type=jnp.float32)]
    pallas_call x0 -> x8, Pallas kernels: none -> 37 us  [add_labels(): pl.pallas_call(functools.partial(accumulate, spec), grid_spec=pltpu.Prefe...]
    reduce_scatter x1 -> x0, waiting for transfers between devices: 35.2 us -> none  [per_device(): lax.psum_scatter(mixture, 'rep', scatter_dimension=0, tiled=True)]
    unnamed x14 -> x75, local copies, waits for them, and re-layouts: 1.25 us -> 22.9 us
    ppermute x0 -> x32, starting transfers between devices: none -> 16.6 us  [moved(): return lax.ppermute(x, AXES, pairs)]
  transfers between devices with their start and end apart: 3 -> 32, of which waited for: 3 -> 9; matrix products, arithmetic and copies ran while one was open for 16% -> 2% of each run, Pallas kernels for 0% -> 19%
where the time goes in v1:
time: 179 us; the launch traced here: 178 us
  waiting for transfers between devices  93.4 us (52%)
  Pallas kernels  37 us (21%)
  local copies, waits for them, and re-layouts  25.3 us (14%)
  starting transfers between devices  16.6 us (9%)
  other arithmetic  5 us (3%)
    ppermute x32, waiting for transfers between devices, moved(): return lax.ppermute(x, AXES, pairs)  93.4 us
    pallas_call x8, Pallas kernels, add_labels(): pl.pallas_call(functools.partial(accumulate, spec), grid_spec=pltpu.Prefe...  37 us
    unnamed x75, local copies, waits for them, and re-layouts  22.9 us
    ppermute x32, starting transfers between devices, moved(): return lax.ppermute(x, AXES, pairs)  16.6 us
  transfers between devices with their start and end apart: 32, of which 9 were waited for; matrix products, arithmetic and copies ran while one was open for 2% of the time, Pallas kernels for 19%

profile of v1, /device:TPU:0, one launch (start us, length us, event | category | flops | bytes accessed | tf_op | source)
XLA Modules:
  0.0 177.8 jit_solution(14404650867275924412)
XLA Ops:
  2.2 3.1 %collective-permute-start.10 = (bf16[192,1792]{1,0:T(8,128)(2,1)S(1)}, bf16[192,1792]{1,0:T(8,128)(2,1)}, u32[]{:S(2)}, u32[]{:S(2)}) collective-permute-start(bf16[192,1792]{1,0:T(8,128)(2,1)S(1)} %pad_maximum_fusion), channel_id=1, source_target_pairs={{0,4},{1,5},{2,6},{3,7},{4,8},{5,9},{6,10},{7,11},{8,12},{9,13},{1... | collective-permute-start | bytes 2064392 | tf_op jit(solution)/shard_map/ppermute | solution.py:139
  5.4 17.5 %collective-permute-done.10.refs_3_ = bf16[192,1792]{1,0:T(8,128)(2,1)} collective-permute-done((bf16[192,1792]{1,0:T(8,128)(2,1)S(1)}, bf16[192,1792]{1,0:T(8,128)(2,1)}, u32[]{:S(2)}, u32[]{:S(2)}) %collective-permute-start.10) | collective-permute-done | bytes 688160 | tf_op jit(solution)/shard_map/ppermute | solution.py:139
  22.9 1.3 collective-permute-start.4
  24.2 22.2 %collective-permute-done.4.refs_3_ = bf16[64,1792]{1,0:T(8,128)(2,1)S(1)} collective-permute-done((bf16[64,1792]{1,0:T(8,128)(2,1)S(1)}, bf16[64,1792]{1,0:T(8,128)(2,1)S(1)}, u32[]{:S(2)}, u32[]{:S(2)}) %collective-permute-start.4) | collective-permute-done | bytes 229408 | tf_op jit(solution)/shard_map/ppermute | solution.py:139
  49.0 3.5 %collective-permute-done.22.refs_4_ = bf16[64,1792]{1,0:T(8,128)(2,1)S(1)} collective-permute-done((bf16[64,1792]{1,0:T(8,128)(2,1)S(1)}, bf16[64,1792]{1,0:T(8,128)(2,1)S(1)}, u32[]{:S(2)}, u32[]{:S(2)}) %collective-permute-start.22) | collective-permute-done | bytes 229408 | tf_op jit(solution)/shard_map/ppermute | solution.py:139
  53.2 5.4 %collective-permute-done.1.refs_2_ = f32[2,512]{1,0:T(2,128)S(1)} collective-permute-done((f32[2,512]{1,0:T(2,128)S(1)}, f32[2,512]{1,0:T(2,128)S(1)}, u32[]{:S(2)}, u32[]{:S(2)}) %collective-permute-start.1) | collective-permute-done | bytes 4128 | tf_op jit(solution)/shard_map/ppermute | solution.py:139
  58.6 5.4 %collective-permute-done.2.refs_2_ = f32[2,512]{1,0:T(2,128)S(1)} collective-permute-done((f32[2,512]{1,0:T(2,128)S(1)}, f32[2,512]{1,0:T(2,128)S(1)}, u32[]{:S(2)}, u32[]{:S(2)}) %collective-permute-start.2) | collective-permute-done | bytes 4128 | tf_op jit(solution)/shard_map/ppermute | solution.py:139
  68.0 19.8 %collective-permute-done.16.refs_4_ = bf16[64,1792]{1,0:T(8,128)(2,1)S(1)} collective-permute-done((bf16[64,1792]{1,0:T(8,128)(2,1)S(1)}, bf16[64,1792]{1,0:T(8,128)(2,1)S(1)}, u32[]{:S(2)}, u32[]{:S(2)}) %collective-permute-start.16) | collective-permute-done | bytes 229408 | tf_op jit(solution)/shard_map/ppermute | solution.py:139
  94.1 13.1 %collective-permute-done.19.refs_4_ = bf16[192,1792]{1,0:T(8,128)(2,1)} collective-permute-done((bf16[192,1792]{1,0:T(8,128)(2,1)}, bf16[192,1792]{1,0:T(8,128)(2,1)}, u32[]{:S(2)}, u32[]{:S(2)}) %collective-permute-start.19) | collective-permute-done | bytes 688160 | tf_op jit(solution)/shard_map/ppermute | solution.py:139
  107.2 1.6 copy-done
  114.5 5.8 %shard_map.55 = (f32[1024,768]{1,0:T(8,128)S(1)}, f32[1024,1]{1,0:T(8,128)S(1)}) custom-call(s32[10]{0:T(128)S(1)} %stack.43.table, bf16[1024,1024]{1,0:T(8,128)(2,1)S(1)} %copy-done, s32[1024,3]{1,0:T(8,128)S(1)} %copy-done.2, f32[2,512]{1,0:T(2,128)S(1)} %pad_maximum_fusion.2.refs_2_, bf16[512,1024]{1,0:T(8,128)(2,1)S(1)} %copy-done.16, ...), custom_call_target="tpu_custom_call" | custom-call | flops 3758096384 | bytes 12058624 | tf_op jit(solution)/shard_map/pallas_call | solution.py:100
  121.1 6.6 %shard_map.56 = (f32[1024,768]{1,0:T(8,128)S(1)}, f32[1024,1]{1,0:T(8,128)S(1)}) custom-call(s32[10]{0:T(128)S(1)} %stack.43.table, bf16[1024,1024]{1,0:T(8,128)(2,1)S(1)} %copy-done, s32[1024,3]{1,0:T(8,128)S(1)} %copy-done.2, f32[2,512]{1,0:T(2,128)S(1)} %collective-permute-done.1.refs_2_, ...), custom_call_target="tpu_custom_call", output_to_operand_aliasing={{0}: (8, {}), {1}: (9, {})} | custom-call | flops 2818572288 | bytes 11141120 | tf_op jit(solution)/shard_map/pallas_call | solution.py:100
  127.8 3.5 %shard_map.57 = (f32[1024,768]{1,0:T(8,128)S(1)}, f32[1024,1]{1,0:T(8,128)S(1)}) custom-call(s32[10]{0:T(128)S(1)} %stack.43.table, bf16[1024,1024]{1,0:T(8,128)(2,1)S(1)} %copy-done, s32[1024,3]{1,0:T(8,128)S(1)} %copy-done.2, f32[2,512]{1,0:T(2,128)S(1)} %collective-permute-done.1.refs_2_, ...), custom_call_target="tpu_custom_call", output_to_operand_aliasing={{0}: (8, {}), {1}: (9, {})} | custom-call | flops 939524096 | bytes 9306112 | tf_op jit(solution)/shard_map/pallas_call | solution.py:100
  131.9 1.3 collective-permute-start.7
  133.2 6.4 %shard_map.58 = (f32[1024,768]{1,0:T(8,128)S(1)}, f32[1024,1]{1,0:T(8,128)S(1)}) custom-call(s32[10]{0:T(128)S(1)} %stack.43.table, bf16[1024,1024]{1,0:T(8,128)(2,1)S(1)} %copy-done, s32[1024,3]{1,0:T(8,128)S(1)} %copy-done.2, f32[2,512]{1,0:T(2,128)S(1)} %collective-permute-done.2.refs_2_, ...), custom_call_target="tpu_custom_call", output_to_operand_aliasing={{0}: (8, {}), {1}: (9, {})} | custom-call | flops 2818572288 | bytes 11141120 | tf_op jit(solution)/shard_map/pallas_call | solution.py:100
  140.3 3.5 %shard_map.59 = (f32[1024,768]{1,0:T(8,128)S(1)}, f32[1024,1]{1,0:T(8,128)S(1)}) custom-call(s32[10]{0:T(128)S(1)} %stack.43.table, bf16[1024,1024]{1,0:T(8,128)(2,1)S(1)} %copy-done, s32[1024,3]{1,0:T(8,128)S(1)} %copy-done.2, f32[2,512]{1,0:T(2,128)S(1)} %collective-permute-done.2.refs_2_, ...), custom_call_target="tpu_custom_call", output_to_operand_aliasing={{0}: (8, {}), {1}: (9, {})} | custom-call | flops 939524096 | bytes 9306112 | tf_op jit(solution)/shard_map/pallas_call | solution.py:100
  143.8 1.3 collective-permute-done.3.refs_2_
  145.1 6.4 %shard_map.60 = (f32[1024,768]{1,0:T(8,128)S(1)}, f32[1024,1]{1,0:T(8,128)S(1)}) custom-call(s32[10]{0:T(128)S(1)} %stack.43.table, bf16[1024,1024]{1,0:T(8,128)(2,1)S(1)} %copy-done, s32[1024,3]{1,0:T(8,128)S(1)} %copy-done.2, f32[2,512]{1,0:T(2,128)S(1)} %collective-permute-done.3.refs_2_, ...), custom_call_target="tpu_custom_call", output_to_operand_aliasing={{0}: (8, {}), {1}: (9, {})} | custom-call | flops 2818572288 | bytes 11141120 | tf_op jit(solution)/shard_map/pallas_call | solution.py:100
  151.5 2.8 %shard_map.62 = (bf16[512,768]{1,0:T(8,128)(2,1)}, f32[512,1]{1,0:T(8,128)S(1)}) custom-call(s32[10]{0:T(128)S(1)} %stack.43.table, bf16[1024,1024]{1,0:T(8,128)(2,1)S(1)} %copy-done, s32[1024,3]{1,0:T(8,128)S(1)} %copy-done.2, f32[2,512]{1,0:T(2,128)S(1)} %collective-permute-done.3.refs_2_, bf16[64,1792]{1,0:T(8,128)(2,1)S(1)} %collective-permute-done.6.refs_3_, ...), custom_call_target="tpu_custom_call" | custom-call | flops 469762048 | bytes 5111808 | tf_op jit(solution)/shard_map/pallas_call | solution.py:100
  155.0 1.5 collective-permute-start.30
  158.2 1.6 copy-done.1
  164.7 2.0 %shard_map.61 = (f32[512,768]{1,0:T(8,128)S(1)}, f32[512,1]{1,0:T(8,128)S(1)}) custom-call(s32[10]{0:T(128)S(1)} %stack.43.table, bf16[1024,1024]{1,0:T(8,128)(2,1)S(1)} %copy-done.1, s32[1024,3]{1,0:T(8,128)S(1)} %copy-done.3, f32[2,512]{1,0:T(2,128)S(1)} %collective-permute-done.3.refs_2_, bf16[64,1792]{1,0:T(8,128)(2,1)S(1)} %collective-permute-done.6.refs_3_, ...), custom_call_target="tpu_custom_call" | custom-call | flops 469762048 | bytes 5111808 | tf_op jit(solution)/shard_map/pallas_call | solution.py:100
  168.6 5.2 %collective-permute-done.31 = f32[4,128]{1,0:T(4,128)S(1)} collective-permute-done((f32[4,128]{1,0:T(4,128)S(1)}, f32[4,128]{1,0:T(4,128)S(1)}, u32[]{:S(2)}, u32[]{:S(2)}) %collective-permute-start.31) | collective-permute-done | bytes 2080 | tf_op jit(solution)/shard_map/ppermute | solution.py:139
  175.1 2.7 %divide_convert_fusion = bf16[512,768]{1,0:T(8,128)(2,1)} fusion(f32[512,768]{1,0:T(8,128)} %copy-done.6, bf16[512,768]{1,0:T(8,128)(2,1)} %collective-permute-done.30, f32[512]{0:T(512)S(1)} %sqrt_reduce_fusion), kind=kLoop, calls=%fused_computation | loop fusion | flops 1572864 | bytes 3147776 | tf_op jit(solution)/shard_map/convert_element_type | solution.py:205
  (136 shorter events, 33.9 us)
Async XLA Ops:
  2.2 20.6 %collective-permute-start.10 = (bf16[192,1792]{1,0:T(8,128)(2,1)S(1)}, bf16[192,1792]{1,0:T(8,128)(2,1)}, u32[]{:S(2)}, u32[]{:S(2)}) collective-permute-start(bf16[192,1792]{1,0:T(8,128)(2,1)S(1)} %pad_maximum_fusion), channel_id=1, source_target_pairs={{0,4},{1,5},{2,6},{3,7},{4,8},{5,9},{6,10},{7,11},{8,12},{9,13},{1... | collective-permute-start | bytes 2064392 | tf_op jit(solution)/shard_map/ppermute | solution.py:139
  22.9 43.6 %collective-permute-start.11 = (bf16[192,1792]{1,0:T(8,128)(2,1)}, bf16[192,1792]{1,0:T(8,128)(2,1)}, u32[]{:S(2)}, u32[]{:S(2)}) collective-permute-start(bf16[192,1792]{1,0:T(8,128)(2,1)} %collective-permute-done.10.refs_3_), channel_id=1, source_target_pairs={{0,4},{1,5},{2,6},{3,7},{4,8},{5,9},{6,10},{7,11},{8,12},{9,13},{1... | collective-permute-start | bytes 2064392 | tf_op jit(solution)/shard_map/ppermute | solution.py:139
  22.9 23.5 %collective-permute-start.4 = (bf16[64,1792]{1,0:T(8,128)(2,1)S(1)}, bf16[64,1792]{1,0:T(8,128)(2,1)S(1)}, u32[]{:S(2)}, u32[]{:S(2)}) collective-permute-start(bf16[64,1792]{1,0:T(8,128)(2,1)S(1)} %pad_maximum_fusion.1), channel_id=1, source_target_pairs={{0,4},{1,5},{2,6},{3,7},{4,8},{5,9},{6,10},{7,11},{8,12},{9,13},{1... | collective-permute-start | bytes 688136 | tf_op jit(solution)/shard_map/ppermute | solution.py:139
  47.7 16.3 %collective-permute-start.23 = (bf16[64,1792]{1,0:T(8,128)(2,1)S(1)}, bf16[64,1792]{1,0:T(8,128)(2,1)S(1)}, u32[]{:S(2)}, u32[]{:S(2)}) collective-permute-start(bf16[64,1792]{1,0:T(8,128)(2,1)S(1)} %collective-permute-done.4.refs_3_), channel_id=1, source_target_pairs={{0,2},{1,3},{2,0},{3,1},{4,6},{5,7},{6,4},{7,5},{8,10},{9,11},{10,... | collective-permute-start | bytes 688136 | tf_op jit(solution)/shard_map/ppermute | solution.py:139
  47.7 17.5 %collective-permute-start.5 = (bf16[64,1792]{1,0:T(8,128)(2,1)S(1)}, bf16[64,1792]{1,0:T(8,128)(2,1)S(1)}, u32[]{:S(2)}, u32[]{:S(2)}) collective-permute-start(bf16[64,1792]{1,0:T(8,128)(2,1)S(1)} %collective-permute-done.4.refs_3_), channel_id=1, source_target_pairs={{0,4},{1,5},{2,6},{3,7},{4,8},{5,9},{6,10},{7,11},{8,12},{9,13},{1... | collective-permute-start | bytes 688136 | tf_op jit(solution)/shard_map/ppermute | solution.py:139
  52.4 14.1 %collective-permute-start.24 = (bf16[64,1792]{1,0:T(8,128)(2,1)S(1)}, bf16[64,1792]{1,0:T(8,128)(2,1)S(1)}, u32[]{:S(2)}, u32[]{:S(2)}) collective-permute-start(bf16[64,1792]{1,0:T(8,128)(2,1)S(1)} %collective-permute-done.22.refs_4_), channel_id=1, source_target_pairs={{0,2},{1,3},{2,0},{3,1},{4,6},{5,7},{6,4},{7,5},{8,10},{9,11},{10,... | collective-permute-start | bytes 688136 | tf_op jit(solution)/shard_map/ppermute | solution.py:139
  64.0 25.7 %collective-permute-start.29 = (bf16[512,768]{1,0:T(8,128)(2,1)S(1)}, bf16[512,768]{1,0:T(8,128)(2,1)S(1)}, u32[]{:S(2)}, u32[]{:S(2)}) collective-permute-start(bf16[512,768]{1,0:T(8,128)(2,1)S(1)} %copy-done.29), channel_id=1, source_target_pairs={{0,2},{1,3},{2,0},{3,1},{4,6},{5,7},{6,4},{7,5},{8,10},{9,11},{10,... | collective-permute-start | bytes 2359304 | tf_op jit(solution)/shard_map/ppermute | solution.py:139
  64.7 28.3 %collective-permute-start.28 = (bf16[512,1024]{1,0:T(8,128)(2,1)S(1)}, bf16[512,1024]{1,0:T(8,128)(2,1)S(1)}, u32[]{:S(2)}, u32[]{:S(2)}) collective-permute-start(bf16[512,1024]{1,0:T(8,128)(2,1)S(1)} %copy-done.15), channel_id=1, source_target_pairs={{0,2},{1,3},{2,0},{3,1},{4,6},{5,7},{6,4},{7,5},{8,10},{9,11},{10,... | collective-permute-start | bytes 3145736 | tf_op jit(solution)/shard_map/ppermute | solution.py:139
  65.2 25.4 %collective-permute-start.25 = (bf16[192,1792]{1,0:T(8,128)(2,1)}, bf16[192,1792]{1,0:T(8,128)(2,1)}, u32[]{:S(2)}, u32[]{:S(2)}) collective-permute-start(bf16[192,1792]{1,0:T(8,128)(2,1)} %collective-permute-done.10.refs_3_), channel_id=1, source_target_pairs={{0,16},{1,17},{2,18},{3,19},{4,20},{5,21},{6,22},{7,23},{8,24},{9,... | collective-permute-start | bytes 2064392 | tf_op jit(solution)/shard_map/ppermute | solution.py:139
  66.5 24.6 %collective-permute-start.12 = (bf16[192,1792]{1,0:T(8,128)(2,1)}, bf16[192,1792]{1,0:T(8,128)(2,1)}, u32[]{:S(2)}, u32[]{:S(2)}) collective-permute-start(bf16[192,1792]{1,0:T(8,128)(2,1)} %collective-permute-done.11.refs_3_), channel_id=1, source_target_pairs={{0,4},{1,5},{2,6},{3,7},{4,8},{5,9},{6,10},{7,11},{8,12},{9,13},{1... | collective-permute-start | bytes 2064392 | tf_op jit(solution)/shard_map/ppermute | solution.py:139
  67.2 20.5 %collective-permute-start.16 = (bf16[64,1792]{1,0:T(8,128)(2,1)S(1)}, bf16[64,1792]{1,0:T(8,128)(2,1)S(1)}, u32[]{:S(2)}, u32[]{:S(2)}) collective-permute-start(bf16[64,1792]{1,0:T(8,128)(2,1)S(1)} %collective-permute-done.5.refs_3_), channel_id=1, source_target_pairs={{0,16},{1,17},{2,18},{3,19},{4,20},{5,21},{6,22},{7,23},{8,24},{9,... | collective-permute-start | bytes 688136 | tf_op jit(solution)/shard_map/ppermute | solution.py:139
  88.5 18.7 %collective-permute-start.19 = (bf16[192,1792]{1,0:T(8,128)(2,1)}, bf16[192,1792]{1,0:T(8,128)(2,1)}, u32[]{:S(2)}, u32[]{:S(2)}) collective-permute-start(bf16[192,1792]{1,0:T(8,128)(2,1)} %collective-permute-done.11.refs_3_), channel_id=1, source_target_pairs={{0,16},{1,17},{2,18},{3,19},{4,20},{5,21},{6,22},{7,23},{8,24},{9,... | collective-permute-start | bytes 2064392 | tf_op jit(solution)/shard_map/ppermute | solution.py:139
  90.6 29.7 %collective-permute-start.26 = (bf16[192,1792]{1,0:T(8,128)(2,1)}, bf16[192,1792]{1,0:T(8,128)(2,1)}, u32[]{:S(2)}, u32[]{:S(2)}) collective-permute-start(bf16[192,1792]{1,0:T(8,128)(2,1)} %collective-permute-done.10.refs_3_), channel_id=1, source_target_pairs={{0,2},{1,3},{2,0},{3,1},{4,6},{5,7},{6,4},{7,5},{8,10},{9,11},{10,... | collective-permute-start | bytes 2064392 | tf_op jit(solution)/shard_map/ppermute | solution.py:139
  90.6 29.8 %collective-permute-start.27 = (bf16[192,1792]{1,0:T(8,128)(2,1)}, bf16[192,1792]{1,0:T(8,128)(2,1)}, u32[]{:S(2)}, u32[]{:S(2)}) collective-permute-start(bf16[192,1792]{1,0:T(8,128)(2,1)} %collective-permute-done.25.refs_4_), channel_id=1, source_target_pairs={{0,2},{1,3},{2,0},{3,1},{4,6},{5,7},{6,4},{7,5},{8,10},{9,11},{10,... | collective-permute-start | bytes 2064392 | tf_op jit(solution)/shard_map/ppermute | solution.py:139
  91.2 29.9 %collective-permute-start.13 = (bf16[192,1792]{1,0:T(8,128)(2,1)}, bf16[192,1792]{1,0:T(8,128)(2,1)}, u32[]{:S(2)}, u32[]{:S(2)}) collective-permute-start(bf16[192,1792]{1,0:T(8,128)(2,1)} %collective-permute-done.12.refs_3_), channel_id=1, source_target_pairs={{0,16},{1,17},{2,18},{3,19},{4,20},{5,21},{6,22},{7,23},{8,24},{9,... | collective-permute-start | bytes 2064392 | tf_op jit(solution)/shard_map/ppermute | solution.py:139
  94.1 37.8 %collective-permute-start.20 = (bf16[192,1792]{1,0:T(8,128)(2,1)}, bf16[192,1792]{1,0:T(8,128)(2,1)S(1)}, u32[]{:S(2)}, u32[]{:S(2)}) collective-permute-start(bf16[192,1792]{1,0:T(8,128)(2,1)} %collective-permute-done.11.refs_3_), channel_id=1, source_target_pairs={{0,2},{1,3},{2,0},{3,1},{4,6},{5,7},{6,4},{7,5},{8,10},{9,11},{10,... | collective-permute-start | bytes 2064392 | tf_op jit(solution)/shard_map/ppermute | solution.py:139
  107.2 24.8 %collective-permute-start.21 = (bf16[192,1792]{1,0:T(8,128)(2,1)}, bf16[192,1792]{1,0:T(8,128)(2,1)S(1)}, u32[]{:S(2)}, u32[]{:S(2)}) collective-permute-start(bf16[192,1792]{1,0:T(8,128)(2,1)} %collective-permute-done.19.refs_4_), channel_id=1, source_target_pairs={{0,2},{1,3},{2,0},{3,1},{4,6},{5,7},{6,4},{7,5},{8,10},{9,11},{10,... | collective-permute-start | bytes 2064392 | tf_op jit(solution)/shard_map/ppermute | solution.py:139
  120.4 10.9 %collective-permute-start.6 = (bf16[64,1792]{1,0:T(8,128)(2,1)S(1)}, bf16[64,1792]{1,0:T(8,128)(2,1)S(1)}, u32[]{:S(2)}, u32[]{:S(2)}) collective-permute-start(bf16[64,1792]{1,0:T(8,128)(2,1)S(1)} %copy-done.18), channel_id=1, source_target_pairs={{0,4},{1,5},{2,6},{3,7},{4,8},{5,9},{6,10},{7,11},{8,12},{9,13},{1... | collective-permute-start | bytes 688136 | tf_op jit(solution)/shard_map/ppermute | solution.py:139
  120.5 24.6 %collective-permute-start.14 = (bf16[192,1792]{1,0:T(8,128)(2,1)}, bf16[192,1792]{1,0:T(8,128)(2,1)S(1)}, u32[]{:S(2)}, u32[]{:S(2)}) collective-permute-start(bf16[192,1792]{1,0:T(8,128)(2,1)} %collective-permute-done.12.refs_3_), channel_id=1, source_target_pairs={{0,2},{1,3},{2,0},{3,1},{4,6},{5,7},{6,4},{7,5},{8,10},{9,11},{10,... | collective-permute-start | bytes 2064392 | tf_op jit(solution)/shard_map/ppermute | solution.py:139
  121.0 24.1 %collective-permute-start.15 = (bf16[192,1792]{1,0:T(8,128)(2,1)}, bf16[192,1792]{1,0:T(8,128)(2,1)S(1)}, u32[]{:S(2)}, u32[]{:S(2)}) collective-permute-start(bf16[192,1792]{1,0:T(8,128)(2,1)} %collective-permute-done.13.refs_4_), channel_id=1, source_target_pairs={{0,2},{1,3},{2,0},{3,1},{4,6},{5,7},{6,4},{7,5},{8,10},{9,11},{10,... | collective-permute-start | bytes 2064392 | tf_op jit(solution)/shard_map/ppermute | solution.py:139
  139.7 11.8 %collective-permute-start.8 = (bf16[64,1792]{1,0:T(8,128)(2,1)S(1)}, bf16[64,1792]{1,0:T(8,128)(2,1)S(1)}, u32[]{:S(2)}, u32[]{:S(2)}) collective-permute-start(bf16[64,1792]{1,0:T(8,128)(2,1)S(1)} %collective-permute-done.6.refs_3_), channel_id=1, source_target_pairs={{0,2},{1,3},{2,0},{3,1},{4,6},{5,7},{6,4},{7,5},{8,10},{9,11},{10,... | collective-permute-start | bytes 688136 | tf_op jit(solution)/shard_map/ppermute | solution.py:139
  139.9 11.6 %collective-permute-start.9 = (bf16[64,1792]{1,0:T(8,128)(2,1)S(1)}, bf16[64,1792]{1,0:T(8,128)(2,1)S(1)}, u32[]{:S(2)}, u32[]{:S(2)}) collective-permute-start(bf16[64,1792]{1,0:T(8,128)(2,1)S(1)} %collective-permute-done.7.refs_4_), channel_id=1, source_target_pairs={{0,2},{1,3},{2,0},{3,1},{4,6},{5,7},{6,4},{7,5},{8,10},{9,11},{10,... | collective-permute-start | bytes 688136 | tf_op jit(solution)/shard_map/ppermute | solution.py:139
  155.0 20.1 %collective-permute-start.30 = (bf16[512,768]{1,0:T(8,128)(2,1)}, bf16[512,768]{1,0:T(8,128)(2,1)}, u32[]{:S(2)}, u32[]{:S(2)}) collective-permute-start(bf16[512,768]{1,0:T(8,128)(2,1)} %get-tuple-element.34), channel_id=1, source_target_pairs={{0,1},{1,0},{2,3},{3,2},{4,5},{5,4},{6,7},{7,6},{8,9},{9,8},{10,11... | collective-permute-start | bytes 2359304 | tf_op jit(solution)/shard_map/ppermute | solution.py:139
  157.6 16.2 %collective-permute-start.31 = (f32[4,128]{1,0:T(4,128)S(1)}, f32[4,128]{1,0:T(4,128)S(1)}, u32[]{:S(2)}, u32[]{:S(2)}) collective-permute-start(f32[4,128]{1,0:T(4,128)S(1)} %bitcast.15), channel_id=1, source_target_pairs={{0,1},{1,0},{2,3},{3,2},{4,5},{5,4},{6,7},{7,6},{8,9},{9,8},{10,11... | collective-permute-start | bytes 6152 | tf_op jit(solution)/shard_map/ppermute | solution.py:139
  (45 other events, 279.6 us)

commit v2 on v0

v2 whole, which is shorter than its diff:
```python
import functools

import jax
import jax.numpy as jnp
from jax import lax
from jax.experimental import pallas as pl
from jax.experimental.pallas import tpu as pltpu
from jax.sharding import PartitionSpec as P

AXES = ("groups", "loop", "rep")
DOC_TILE = 256
VMEM_LIMIT = 24 * 1024 * 1024
SHARES = (1, 1)
TIES = {("first", 1): 1, ("mid", 1): 1, ("last", 1): 1}
BIAS_ROWS = 8
COST_NEXT = 4400000000


def joined(xs, axis):
    return xs[0] if len(xs) == 1 else jnp.concatenate(xs, axis=axis)


def column(row):
    return jnp.transpose(jnp.broadcast_to(row[:1], (128, row.shape[1])))[:, :1]


def accumulate(spec, table, bias_ref, *refs):
    step, offsets, parts, part_rows, sets, first, where, reps, received = spec
    count = max(1, len(offsets)) * parts
    labels, refs = refs[: 2 if not offsets else count], refs[2 if not offsets else count :]
    if offsets:
        lead, bias_rows, weight_rows, embed_rows = len(offsets), [], [], []
        for k, ref in enumerate(labels):
            offset = offsets[k % lead]
            rows = ref.shape[0] - (0 if offset else BIAS_ROWS)
            width = sets_width(refs)
            weight_rows.append(ref[:rows, :width])
            embed_rows.append(ref[:rows, width:])
            source = labels[k - k % lead]
            row = source[source.shape[0] - BIAS_ROWS :, :part_rows].astype(jnp.float32)[:1]
            bias_rows.append(row[:, offset : offset + rows])
        bias = joined(bias_rows, 1)
        weight_rows, embed_rows = joined(weight_rows, 0), joined(embed_rows, 0)
    else:
        weight_rows, embed_rows, bias = labels[0][...], labels[1][...], bias_ref[...]
    block, rep = table[1 + step], table[table.shape[0] - 1]
    per_set = 2 + (0 if first else 2) + (2 if received else 0)
    for k in range(sets):
        docs_ref, ids_ref, *rest = refs[k * per_set : (k + 1) * per_set]
        mix_out, sum_out = refs[sets * per_set + 2 * k : sets * per_set + 2 * k + 2]
        held = docs_ref.shape[0] if where == "all" else docs_ref.shape[0] // reps
        tile = min(DOC_TILE, held)
        subs = held // tile

        @pl.loop(0, mix_out.shape[0] // tile)
        def _(i):
            if where == "all":
                source = i
            elif where == "home":
                source = rep * subs + i
            else:
                source = lax.rem(rep + 1 + i // subs, reps) * subs + lax.rem(i, subs)
            from_rows = pl.ds(pl.multiple_of(source * tile, tile), tile)
            to_rows = pl.ds(pl.multiple_of(i * tile, tile), tile)
            chosen = jnp.max((ids_ref[from_rows, :] == block).astype(jnp.float32), axis=1, keepdims=True)
            logits = lax.dot_general(
                docs_ref[from_rows, :], weight_rows, (((1,), (1,)), ((), ())), preferred_element_type=jnp.float32
            )
            weights = (chosen * jax.nn.sigmoid(logits + bias)).astype(jnp.bfloat16)
            mix = jnp.dot(weights, embed_rows, preferred_element_type=jnp.float32)
            sums = jnp.sum(weights.astype(jnp.float32), axis=1, keepdims=True)
            if not first:
                mix = mix + rest[0][from_rows, :]
                sums = sums + rest[1][from_rows, :]
            if received:
                mix = mix + rest[2][to_rows, :].astype(jnp.float32)
                sums = sums + column(rest[3][:, to_rows])
            mix_out[to_rows, :] = mix.astype(mix_out.dtype)
            if sum_out.shape[0] == 8:
                sum_out[:, to_rows] = jnp.transpose(jnp.broadcast_to(sums, (tile, 128)))[:8]
            else:
                sum_out[to_rows, :] = sums


def sets_width(refs):
    return refs[0].shape[1]


def add_labels(table, bias, labels, sets, *, step, offsets, parts, part_rows, reps, where="all", out=jnp.float32):
    embed_width = labels[1].shape[1] if not offsets else labels[0].shape[1] - sets[0][0].shape[1]
    first, received = len(sets[0]) == 2, len(sets[0]) > 4
    spec = (step, offsets, parts, part_rows, len(sets), first, where, reps, received)
    operands = [bias, *labels]
    aliases, out_shape = {}, []
    for k, one in enumerate(sets):
        docs = one[0]
        rows = {"all": docs.shape[0], "home": docs.shape[0] // reps, "away": docs.shape[0] // reps * (reps - 1)}[where]
        if where == "all" and not first:
            aliases[1 + len(operands) + 2] = 2 * k
            aliases[1 + len(operands) + 3] = 2 * k + 1
        operands += one
        out_shape.append(jax.ShapeDtypeStruct((rows, embed_width), out))
        out_shape.append(jax.ShapeDtypeStruct((rows, 1) if out == jnp.float32 else (8, rows), jnp.float32))
    outs = pl.pallas_call(
        functools.partial(accumulate, spec),
        in_specs=[pl.BlockSpec(memory_space=pltpu.SMEM)] + [pl.BlockSpec(memory_space=pltpu.VMEM)] * len(operands),
        out_specs=[pl.BlockSpec(memory_space=pltpu.VMEM)] * len(out_shape),
        out_shape=out_shape,
        input_output_aliases=aliases,
        compiler_params=pltpu.CompilerParams(vmem_limit_bytes=VMEM_LIMIT),
        cost_estimate=pl.CostEstimate(flops=0, bytes_accessed=0, transcendentals=0),
    )(table, *operands)
    return [list(outs[2 * k : 2 * k + 2]) for k in range(len(sets))]


def combine(mix_ref, sum_ref, *refs):
    out_ref, others = refs[-1], list(refs[:-1])
    mix, sums = mix_ref[...], sum_ref[...]
    while others:
        parts, rows = [], 0
        while rows < mix.shape[0]:
            parts.append(others.pop(0)[...].astype(jnp.float32))
            rows += parts[-1].shape[0]
        mix = mix + joined(parts, 0)
        sums = sums + column(others.pop(0)[...])
    out_ref[...] = (mix / jnp.sqrt(1.0 + sums)).astype(out_ref.dtype)


def combined(mix, sums, others):
    return pl.pallas_call(
        combine,
        in_specs=[pl.BlockSpec(memory_space=pltpu.VMEM)] * (2 + len(others)),
        out_specs=pl.BlockSpec(memory_space=pltpu.VMEM),
        out_shape=jax.ShapeDtypeStruct(mix.shape, jnp.bfloat16),
        compiler_params=pltpu.CompilerParams(vmem_limit_bytes=VMEM_LIMIT),
        cost_estimate=pl.CostEstimate(flops=0, bytes_accessed=0, transcendentals=0),
    )(mix, sums, *others)


def pack(spec, table, weight, embed, bias, out, sems):
    offset, rows, part_rows, groups = spec
    width = weight.shape[1]
    group = table[0]
    source = pl.ds(pl.multiple_of(group * part_rows + offset, 16), rows)
    copies = [
        pltpu.make_async_copy(weight.at[source, :], out.at[pl.ds(0, rows), pl.ds(0, width)], sems.at[0]),
        pltpu.make_async_copy(embed.at[source, :], out.at[pl.ds(0, rows), pl.ds(width, embed.shape[1])], sems.at[1]),
    ]
    for copy in copies:
        copy.start()
    if offset == 0:
        row = bias[:, :part_rows]
        for other in range(1, groups):
            row = jnp.where(group == other, bias[:, other * part_rows : (other + 1) * part_rows], row)
        out[rows:, :part_rows] = jnp.broadcast_to(row, (BIAS_ROWS, part_rows)).astype(out.dtype)
        out[rows:, part_rows:] = jnp.zeros((BIAS_ROWS, out.shape[1] - part_rows), out.dtype)
    for copy in copies:
        copy.wait()


def packed_part(table, weight, embed, bias, offset, rows, part_rows, groups, cost):
    width = weight.shape[1] + embed.shape[1]
    return pl.pallas_call(
        functools.partial(pack, (offset, rows, part_rows, groups)),
        in_specs=[pl.BlockSpec(memory_space=pltpu.SMEM)]
        + [pl.BlockSpec(memory_space=pl.ANY)] * 2
        + [pl.BlockSpec(memory_space=pltpu.VMEM)],
        out_specs=pl.BlockSpec(memory_space=pltpu.VMEM),
        out_shape=jax.ShapeDtypeStruct((rows + (0 if offset else BIAS_ROWS), width), weight.dtype),
        scratch_shapes=[pltpu.SemaphoreType.DMA((2,))],
        compiler_params=pltpu.CompilerParams(vmem_limit_bytes=VMEM_LIMIT),
        cost_estimate=pl.CostEstimate(flops=cost, bytes_accessed=0, transcendentals=0),
    )(table, weight, embed, bias)


def per_device(sizes, documents, block_ids, label_weight, label_bias, label_embed):
    groups, loop, reps = sizes
    cores = 2 if loop % 2 == 0 else 1
    chips = loop // cores
    doc_count = documents.shape[0]
    part_rows = label_weight.shape[0] // groups

    def moved(x, to):
        pairs = []
        for g in range(groups):
            for l in range(loop):
                for r in range(reps):
                    g2, z2, c2, r2 = to(g, l // cores, l % cores, r)
                    there = (g2 % groups, (z2 % chips) * cores + c2 % cores, r2 % reps)
                    number = lambda a: (a[0] * loop + a[1]) * reps + a[2]
                    pairs.append((number((g, l, r)), number(there)))
        return lax.ppermute(x, AXES, pairs)

    along = lambda x: moved(x, lambda g, z, c, r: (g, z + 1, c, r))
    across = lambda x, k: moved(x, lambda g, z, c, r: (g + k, z, c, r))
    other_core = lambda x: moved(x, lambda g, z, c, r: (g, z, c + 1, r))
    other_rep = lambda x, k: moved(x, lambda g, z, c, r: (g, z, c, r + k))

    place = lax.axis_index("loop")
    chip, core = place // cores, place % cores
    entries = [lax.axis_index("groups")]
    entries += [((chip - step) % chips) * cores + core for step in range(chips)]
    entries.append(lax.axis_index("rep"))
    table = jnp.stack(entries).astype(jnp.int32)

    total = sum(SHARES)
    cuts = [part_rows * sum(SHARES[:k]) // total // 16 * 16 for k in range(len(SHARES))] + [part_rows]
    chunks = [(a, b - a) for a, b in zip(cuts, cuts[1:])]
    bias = label_bias.astype(jnp.float32)[None, :]
    flying = [
        packed_part(table, label_weight, label_embed, bias, offset, rows, part_rows, groups, COST_NEXT if offset else 0)
        for offset, rows in chunks
    ]
    sets = [[documents, block_ids]]
    if cores == 2:
        sets.append([other_core(documents), other_core(block_ids)])
    call = functools.partial(add_labels, table, bias)
    common = dict(part_rows=part_rows, reps=reps)
    history = [call([label_weight, label_embed], sets, step=0, offsets=(), parts=1, **common)]

    def after(x, step, index):
        back = TIES.get(("last" if step + 1 == chips else "first" if step == 1 else "mid", index))
        if back is None or back > step:
            return x
        x, history[step - back] = lax.optimization_barrier((x, history[step - back]))
        return x

    for step in range(1, chips):
        arrived = []
        for index in range(len(chunks)):
            flying[index] = after(along(flying[index]), step, index)
            arrived.append([flying[index]] + [across(flying[index], k) for k in range(1, groups)])
        labels = [pieces[part] for part in range(groups) for pieces in arrived]
        here = dict(step=step, offsets=tuple(offset for offset, _ in chunks), parts=groups, **common)
        if step + 1 < chips:
            history.append(call(labels, [one + t for one, t in zip(sets, history[-1])], **here))
    held = [one + t for one, t in zip(sets, history[-1])]

    narrow = dict(out=jnp.bfloat16, **here)
    tile_docs = doc_count // reps
    others = []
    away = [held[0]]
    if cores == 2:
        (share,) = call(labels, [held[1]], where="away", **narrow)
        away = [held[0] + [other_core(x) for x in share]]
    (away,) = call(labels, away, where="away", **narrow)
    if cores == 2:
        away, held[1] = lax.optimization_barrier((away, held[1]))
        (share,) = call(labels, [held[1]], where="home", **narrow)
        half = tile_docs // 2
        others += [other_core(share[0][:half]), other_core(share[0][half:]), other_core(share[1])]
    ((home_mix, home_sum),) = call(labels, [held[0]], where="home", **here)
    for k in range(1, reps):
        part = slice((k - 1) * tile_docs, k * tile_docs)
        others += [other_rep(away[0][part], k), other_rep(away[1][:, part], k)]
    return combined(home_mix, home_sum, others)


def solution(mesh):
    sizes = tuple(mesh.shape[axis] for axis in AXES)
    return jax.shard_map(
        functools.partial(per_device, sizes),
        mesh=mesh,
        in_specs=(
            P(("groups", "loop"), None),
            P(("groups", "loop"), None),
            P(("loop", "rep"), None),
            P(("loop", "rep")),
            P(("loop", "rep"), None),
        ),
        out_specs=P(("groups", "loop", "rep"), None),
        check_vma=False,
    )
```

time: 337 us -> 118 us (0.35)
  local copies, waits for them, and re-layouts: 92.8 us -> 3.95 us
  waiting for transfers between devices: 121 us -> 55.1 us
  matrix products: 56.5 us -> 0 us
  Pallas kernels: 0 us -> 40.4 us
  other arithmetic: 32.1 us -> 0.68 us
  blocking collectives: 19.6 us -> 0 us
  starting transfers between devices: 0.08 us -> 17.4 us
  between operations: 14 us -> 0.2 us
    all_gather x2 -> x0, waiting for transfers between devices: 84.6 us -> none  [the longest x1 82.3 us: per_device(): weight_piece = lax.all_gather(label_weight, 'loop', axis=0, tiled=True)]
    gather x7 -> x0, local copies, waits for them, and re-layouts: 82 us -> none  [the longest x3 36.7 us: per_device(): mixture = mixture + jnp.take(flat_mix, flat_index, axis=0)]
    dot_general x16 -> x0, matrix products: 56.5 us -> none  [the longest x8 33.3 us: score_rows(): mix = jnp.dot(weights, embed_part, preferred_element_type=jnp.float32)]
    ppermute x0 -> x21, waiting for transfers between devices: none -> 55.1 us  [moved(): return lax.ppermute(x, AXES, pairs)]
    pallas_call x0 -> x10, Pallas kernels: none -> 40.4 us  [the longest x7 37 us: add_labels(): pl.pallas_call(functools.partial(accumulate, spec), in_specs=[pl.BlockSpe...]
    reduce_scatter x1 -> x0, waiting for transfers between devices: 35.2 us -> none  [per_device(): lax.psum_scatter(mixture, 'rep', scatter_dimension=0, tiled=True)]
    ppermute x0 -> x21, starting transfers between devices: none -> 17.4 us  [moved(): return lax.ppermute(x, AXES, pairs)]
    all_gather x1 -> x0, blocking collectives: 14.6 us -> none  [per_device(): bias_piece = lax.all_gather(label_bias, 'loop', axis=0, tiled=True)]
  transfers between devices with their start and end apart: 3 -> 21, of which waited for: 3 -> 10; matrix products, arithmetic and copies ran while one was open for 16% -> 1% of each run, Pallas kernels for 0% -> 28%
where the time goes in v2:
time: 118 us
  waiting for transfers between devices  55.1 us (47%)
  Pallas kernels  40.4 us (34%)
  starting transfers between devices  17.4 us (15%)
  local copies, waits for them, and re-layouts  3.95 us (3%)
    ppermute x21, waiting for transfers between devices, moved(): return lax.ppermute(x, AXES, pairs)  55.1 us
    pallas_call x7, Pallas kernels, add_labels(): pl.pallas_call(functools.partial(accumulate, spec), in_specs=[pl.BlockSpe...  37 us
    ppermute x21, starting transfers between devices, moved(): return lax.ppermute(x, AXES, pairs)  17.4 us
    unnamed x13, local copies, waits for them, and re-layouts  3.82 us
  transfers between devices with their start and end apart: 21, of which 10 were waited for; matrix products, arithmetic and copies ran while one was open for 1% of the time, Pallas kernels for 28%

profile of v2, /device:TPU:0, one launch (start us, length us, event | category | flops | bytes accessed | tf_op | source)
XLA Modules:
  0.0 117.8 jit_solution(10551473795393461694)
XLA Ops:
  4.2 2.6 %collective-permute-start = (bf16[136,1792]{1,0:T(8,128)(2,1)S(1)}, bf16[136,1792]{1,0:T(8,128)(2,1)}, u32[]{:S(2)}, u32[]{:S(2)}) collective-permute-start(bf16[136,1792]{1,0:T(8,128)(2,1)S(1)} %shard_map.55), channel_id=1, source_target_pairs={{0,4},{1,5},{2,6},{3,7},{4,8},{5,9},{6,10},{7,11},{8,12},{9,13},{1... | collective-permute-start | bytes 1462280 | tf_op jit(solution)/shard_map/ppermute | solution.py:192
  8.2 1.6 %collective-permute-start.3 = (bf16[128,1792]{1,0:T(8,128)(2,1)}, bf16[128,1792]{1,0:T(8,128)(2,1)}, u32[]{:S(2)}, u32[]{:S(2)}) collective-permute-start(bf16[128,1792]{1,0:T(8,128)(2,1)} %shard_map.56), channel_id=1, source_target_pairs={{0,4},{1,5},{2,6},{3,7},{4,8},{5,9},{6,10},{7,11},{8,12},{9,13},{1... | collective-permute-start | bytes 1376264 | tf_op jit(solution)/shard_map/ppermute | solution.py:192
  9.9 11.1 %collective-permute-done.refs_0_ = bf16[136,1792]{1,0:T(8,128)(2,1)} collective-permute-done((bf16[136,1792]{1,0:T(8,128)(2,1)S(1)}, bf16[136,1792]{1,0:T(8,128)(2,1)}, u32[]{:S(2)}, u32[]{:S(2)}) %collective-permute-start) | collective-permute-done | bytes 487456 | tf_op jit(solution)/shard_map/ppermute | solution.py:192
  21.0 1.6 %collective-permute-start.7 = (bf16[136,1792]{1,0:T(8,128)(2,1)}, bf16[136,1792]{1,0:T(8,128)(2,1)}, u32[]{:S(2)}, u32[]{:S(2)}) collective-permute-start(bf16[136,1792]{1,0:T(8,128)(2,1)} %collective-permute-done.refs_0_), channel_id=1, source_target_pairs={{0,16},{1,17},{2,18},{3,19},{4,20},{5,21},{6,22},{7,23},{8,24},{9,... | collective-permute-start | bytes 1462280 | tf_op jit(solution)/shard_map/ppermute | solution.py:192
  22.9 1.9 %collective-permute-done.5.refs_5_.refs_9_ = s32[1024,3]{1,0:T(8,128)S(1)} collective-permute-done((s32[1024,3]{1,0:T(8,128)S(1)}, s32[1024,3]{1,0:T(8,128)S(1)}, u32[]{:S(2)}, u32[]{:S(2)}) %collective-permute-start.5) | collective-permute-done | bytes 12320 | tf_op jit(solution)/shard_map/ppermute | solution.py:192
  26.1 8.3 %shard_map.57 = (f32[1024,768]{1,0:T(8,128)S(1)}, f32[1024,1]{1,0:T(8,128)S(1)}, f32[1024,768]{1,0:T(8,128)S(1)}, f32[1024,1]{1,0:T(8,128)S(1)}) custom-call(s32[6]{0:T(128)S(1)} %stack.27.table, f32[1,512]{1,0:T(1,128)S(1)} %bitcast.9, bf16[512,1024]{1,0:T(8,128)(2,1)S(1)} %copy-done.2, bf16[512,768]{1,0:T(8,128)(2,1)S(1)} %copy-done.4, ...), custom_call_target="tpu_custom_call" | custom-call | tf_op jit(solution)/shard_map/pallas_call | solution.py:104
  34.8 1.5 %collective-permute-start.6 = (bf16[128,1792]{1,0:T(8,128)(2,1)}, bf16[128,1792]{1,0:T(8,128)(2,1)S(1)}, u32[]{:S(2)}, u32[]{:S(2)}) collective-permute-start(bf16[128,1792]{1,0:T(8,128)(2,1)} %collective-permute-done.3.refs_1_), channel_id=1, source_target_pairs={{0,4},{1,5},{2,6},{3,7},{4,8},{5,9},{6,10},{7,11},{8,12},{9,13},{1... | collective-permute-start | bytes 1376264 | tf_op jit(solution)/shard_map/ppermute | solution.py:192
  36.3 4.9 %collective-permute-done.1.refs_0_ = bf16[136,1792]{1,0:T(8,128)(2,1)} collective-permute-done((bf16[136,1792]{1,0:T(8,128)(2,1)}, bf16[136,1792]{1,0:T(8,128)(2,1)}, u32[]{:S(2)}, u32[]{:S(2)}) %collective-permute-start.1) | collective-permute-done | bytes 487456 | tf_op jit(solution)/shard_map/ppermute | solution.py:192
  41.3 1.6 %collective-permute-start.10 = (bf16[136,1792]{1,0:T(8,128)(2,1)}, bf16[136,1792]{1,0:T(8,128)(2,1)S(1)}, u32[]{:S(2)}, u32[]{:S(2)}) collective-permute-start(bf16[136,1792]{1,0:T(8,128)(2,1)} %collective-permute-done.1.refs_0_), channel_id=1, source_target_pairs={{0,16},{1,17},{2,18},{3,19},{4,20},{5,21},{6,22},{7,23},{8,24},{9,... | collective-permute-start | bytes 1462280 | tf_op jit(solution)/shard_map/ppermute | solution.py:192
  42.9 5.1 %collective-permute-done.8.refs_3_ = bf16[128,1792]{1,0:T(8,128)(2,1)S(1)} collective-permute-done((bf16[128,1792]{1,0:T(8,128)(2,1)}, bf16[128,1792]{1,0:T(8,128)(2,1)S(1)}, u32[]{:S(2)}, u32[]{:S(2)}) %collective-permute-start.8) | collective-permute-done | bytes 458784 | tf_op jit(solution)/shard_map/ppermute | solution.py:192
  48.0 8.7 %shard_map.58 = (f32[1024,768]{1,0:T(8,128)S(1)}, f32[1024,1]{1,0:T(8,128)S(1)}, f32[1024,768]{1,0:T(8,128)S(1)}, f32[1024,1]{1,0:T(8,128)S(1)}) custom-call(s32[6]{0:T(128)S(1)} %stack.27.table, f32[1,512]{1,0:T(1,128)S(1)} %bitcast.10, ...), custom_call_target="tpu_custom_call", output_to_operand_aliasing={{0}: (8, {}), {1}: (9, {}), {2}: (12, {}), {3}: (13, {})} | custom-call | tf_op jit(solution)/shard_map/pallas_call | solution.py:104
  57.2 1.5 %collective-permute-start.9 = (bf16[128,1792]{1,0:T(8,128)(2,1)S(1)}, bf16[128,1792]{1,0:T(8,128)(2,1)S(1)}, u32[]{:S(2)}, u32[]{:S(2)}) collective-permute-start(bf16[128,1792]{1,0:T(8,128)(2,1)S(1)} %collective-permute-done.6.refs_1_), channel_id=1, source_target_pairs={{0,4},{1,5},{2,6},{3,7},{4,8},{5,9},{6,10},{7,11},{8,12},{9,13},{1... | collective-permute-start | bytes 1376264 | tf_op jit(solution)/shard_map/ppermute | solution.py:192
  58.7 2.7 %collective-permute-done.2.refs_0_ = bf16[136,1792]{1,0:T(8,128)(2,1)S(1)} collective-permute-done((bf16[136,1792]{1,0:T(8,128)(2,1)}, bf16[136,1792]{1,0:T(8,128)(2,1)S(1)}, u32[]{:S(2)}, u32[]{:S(2)}) %collective-permute-start.2) | collective-permute-done | bytes 487456 | tf_op jit(solution)/shard_map/ppermute | solution.py:192
  61.4 1.6 %collective-permute-start.12 = (bf16[136,1792]{1,0:T(8,128)(2,1)S(1)}, bf16[136,1792]{1,0:T(8,128)(2,1)S(1)}, u32[]{:S(2)}, u32[]{:S(2)}) collective-permute-start(bf16[136,1792]{1,0:T(8,128)(2,1)S(1)} %collective-permute-done.2.refs_0_), channel_id=1, source_target_pairs={{0,16},{1,17},{2,18},{3,19},{4,20},{5,21},{6,22},{7,23},{8,24},{9,... | collective-permute-start | bytes 1462280 | tf_op jit(solution)/shard_map/ppermute | solution.py:192
  63.1 7.2 %collective-permute-done.11.refs_3_ = bf16[128,1792]{1,0:T(8,128)(2,1)S(1)} collective-permute-done((bf16[128,1792]{1,0:T(8,128)(2,1)S(1)}, bf16[128,1792]{1,0:T(8,128)(2,1)S(1)}, u32[]{:S(2)}, u32[]{:S(2)}) %collective-permute-start.11) | collective-permute-done | bytes 458784 | tf_op jit(solution)/shard_map/ppermute | solution.py:192
  70.3 8.5 %shard_map.59 = (f32[1024,768]{1,0:T(8,128)S(1)}, f32[1024,1]{1,0:T(8,128)S(1)}, f32[1024,768]{1,0:T(8,128)S(1)}, f32[1024,1]{1,0:T(8,128)S(1)}) custom-call(s32[6]{0:T(128)S(1)} %stack.27.table, f32[1,512]{1,0:T(1,128)S(1)} %bitcast.11, ...), custom_call_target="tpu_custom_call", output_to_operand_aliasing={{0}: (8, {}), {1}: (9, {}), {2}: (12, {}), {3}: (13, {})} | custom-call | tf_op jit(solution)/shard_map/pallas_call | solution.py:104
  79.9 8.2 %collective-permute-done.13.refs_3_ = bf16[128,1792]{1,0:T(8,128)(2,1)S(1)} collective-permute-done((bf16[128,1792]{1,0:T(8,128)(2,1)S(1)}, bf16[128,1792]{1,0:T(8,128)(2,1)S(1)}, u32[]{:S(2)}, u32[]{:S(2)}) %collective-permute-start.13) | collective-permute-done | bytes 458784 | tf_op jit(solution)/shard_map/ppermute | solution.py:192
  88.1 3.4 %shard_map.61 = (bf16[512,768]{1,0:T(8,128)(2,1)S(1)}, f32[8,512]{1,0:T(8,128)S(1)}) custom-call(s32[6]{0:T(128)S(1)} %stack.27.table, f32[1,512]{1,0:T(1,128)S(1)} %bitcast.12, bf16[136,1792]{1,0:T(8,128)(2,1)S(1)} %collective-permute-done.2.refs_0_, bf16[128,1792]{1,0:T(8,128)(2,1)S(1)} %collective-permute-done.9.refs_1_, ...), custom_call_target="tpu_custom_call" | custom-call | tf_op jit(solution)/shard_map/pallas_call | solution.py:104
  92.1 1.8 %collective-permute-done.15.refs_9_ = f32[8,512]{1,0:T(8,128)S(1)} collective-permute-done((f32[8,512]{1,0:T(8,128)S(1)}, f32[8,512]{1,0:T(8,128)S(1)}, u32[]{:S(2)}, u32[]{:S(2)}) %collective-permute-start.15) | collective-permute-done | bytes 16416 | tf_op jit(solution)/shard_map/ppermute | solution.py:192
  93.9 2.4 %shard_map.62 = (bf16[512,768]{1,0:T(8,128)(2,1)S(1)}, f32[8,512]{1,0:T(8,128)S(1)}) custom-call(s32[6]{0:T(128)S(1)} %stack.27.table, f32[1,512]{1,0:T(1,128)S(1)} %bitcast.13, bf16[136,1792]{1,0:T(8,128)(2,1)S(1)} %collective-permute-done.2.refs_0_, bf16[128,1792]{1,0:T(8,128)(2,1)S(1)} %collective-permute-done.9.refs_1_, ...), custom_call_target="tpu_custom_call" | custom-call | tf_op jit(solution)/shard_map/pallas_call | solution.py:104
  96.3 1.5 %collective-permute-start.19 = (bf16[512,768]{1,0:T(8,128)(2,1)S(1)}, bf16[512,768]{1,0:T(8,128)(2,1)S(1)}, u32[]{:S(2)}, u32[]{:S(2)}) collective-permute-start(bf16[512,768]{1,0:T(8,128)(2,1)S(1)} %get-tuple-element.85), channel_id=1, source_target_pairs={{0,1},{1,0},{2,3},{3,2},{4,5},{5,4},{6,7},{7,6},{8,9},{9,8},{10,11... | collective-permute-start | bytes 2359304 | tf_op jit(solution)/shard_map/ppermute | solution.py:192
  97.8 3.4 %shard_map.63 = (bf16[512,768]{1,0:T(8,128)(2,1)S(1)}, f32[8,512]{1,0:T(8,128)S(1)}) custom-call(s32[6]{0:T(128)S(1)} %stack.27.table, f32[1,512]{1,0:T(1,128)S(1)} %bitcast.14, bf16[136,1792]{1,0:T(8,128)(2,1)S(1)} %collective-permute-done.2.refs_0_, bf16[128,1792]{1,0:T(8,128)(2,1)S(1)} %collective-permute-done.9.refs_1_, ...), custom_call_target="tpu_custom_call" | custom-call | tf_op jit(solution)/shard_map/pallas_call | solution.py:104
  102.6 2.3 %shard_map.60 = (f32[512,768]{1,0:T(8,128)S(1)}, f32[512,1]{1,0:T(8,128)S(1)}) custom-call(s32[6]{0:T(128)S(1)} %stack.27.table, f32[1,512]{1,0:T(1,128)S(1)} %bitcast.15, bf16[136,1792]{1,0:T(8,128)(2,1)S(1)} %collective-permute-done.2.refs_0_, bf16[128,1792]{1,0:T(8,128)(2,1)S(1)} %collective-permute-done.9.refs_1_, ...), custom_call_target="tpu_custom_call" | custom-call | tf_op jit(solution)/shard_map/pallas_call | solution.py:104
  104.9 11.4 %collective-permute-done.20.refs_4_ = f32[8,512]{1,0:T(8,128)S(1)} collective-permute-done((f32[8,512]{1,0:T(8,128)S(1)}, f32[8,512]{1,0:T(8,128)S(1)}, u32[]{:S(2)}, u32[]{:S(2)}) %collective-permute-start.20) | collective-permute-done | bytes 16416 | tf_op jit(solution)/shard_map/ppermute | solution.py:192
  (44 shorter events, 12.4 us)
Async XLA Ops:
  0.0 24.8 %collective-permute-start.4 = (bf16[1024,1024]{1,0:T(8,128)(2,1)}, bf16[1024,1024]{1,0:T(8,128)(2,1)}, u32[]{:S(2)}, u32[]{:S(2)}) collective-permute-start(bf16[1024,1024]{1,0:T(8,128)(2,1)} %refs_4_.7), channel_id=1, source_target_pairs={{0,2},{1,3},{2,0},{3,1},{4,6},{5,7},{6,4},{7,5},{8,10},{9,11},{10,... | collective-permute-start | bytes 6291464 | tf_op jit(solution)/shard_map/ppermute | solution.py:192
  4.2 18.4 %copy-start.5 = (s32[1024,3]{0,1:T(4,128)S(1)}, s32[1024,3]{0,1:T(4,128)}, u32[]{:S(2)}) copy-start(s32[1024,3]{0,1:T(4,128)} %param.6) | copy-start | bytes 36868
  4.2 20.6 %copy-start = (bf16[1024,1024]{1,0:T(8,128)(2,1)S(1)}, bf16[1024,1024]{1,0:T(8,128)(2,1)}, u32[]{:S(2)}) copy-start(bf16[1024,1024]{1,0:T(8,128)(2,1)} %refs_4_.7) | copy-start | bytes 6291460
  4.2 20.6 %copy-start.4 = (bf16[512,768]{1,0:T(8,128)(2,1)S(1)}, bf16[512,768]{1,0:T(8,128)(2,1)}, u32[]{:S(2)}) copy-start(bf16[512,768]{1,0:T(8,128)(2,1)} %refs_1_.1) | copy-start | bytes 2359300
  4.2 16.7 %collective-permute-start = (bf16[136,1792]{1,0:T(8,128)(2,1)S(1)}, bf16[136,1792]{1,0:T(8,128)(2,1)}, u32[]{:S(2)}, u32[]{:S(2)}) collective-permute-start(bf16[136,1792]{1,0:T(8,128)(2,1)S(1)} %shard_map.55), channel_id=1, source_target_pairs={{0,4},{1,5},{2,6},{3,7},{4,8},{5,9},{6,10},{7,11},{8,12},{9,13},{1... | collective-permute-start | bytes 1462280 | tf_op jit(solution)/shard_map/ppermute | solution.py:192
  8.2 26.2 %collective-permute-start.3 = (bf16[128,1792]{1,0:T(8,128)(2,1)}, bf16[128,1792]{1,0:T(8,128)(2,1)}, u32[]{:S(2)}, u32[]{:S(2)}) collective-permute-start(bf16[128,1792]{1,0:T(8,128)(2,1)} %shard_map.56), channel_id=1, source_target_pairs={{0,4},{1,5},{2,6},{3,7},{4,8},{5,9},{6,10},{7,11},{8,12},{9,13},{1... | collective-permute-start | bytes 1376264 | tf_op jit(solution)/shard_map/ppermute | solution.py:192
  21.0 20.3 %collective-permute-start.1 = (bf16[136,1792]{1,0:T(8,128)(2,1)}, bf16[136,1792]{1,0:T(8,128)(2,1)}, u32[]{:S(2)}, u32[]{:S(2)}) collective-permute-start(bf16[136,1792]{1,0:T(8,128)(2,1)} %collective-permute-done.refs_0_), channel_id=1, source_target_pairs={{0,4},{1,5},{2,6},{3,7},{4,8},{5,9},{6,10},{7,11},{8,12},{9,13},{1... | collective-permute-start | bytes 1462280 | tf_op jit(solution)/shard_map/ppermute | solution.py:192
  21.0 21.9 %collective-permute-start.7 = (bf16[136,1792]{1,0:T(8,128)(2,1)}, bf16[136,1792]{1,0:T(8,128)(2,1)}, u32[]{:S(2)}, u32[]{:S(2)}) collective-permute-start(bf16[136,1792]{1,0:T(8,128)(2,1)} %collective-permute-done.refs_0_), channel_id=1, source_target_pairs={{0,16},{1,17},{2,18},{3,19},{4,20},{5,21},{6,22},{7,23},{8,24},{9,... | collective-permute-start | bytes 1462280 | tf_op jit(solution)/shard_map/ppermute | solution.py:192
  22.9 2.0 %collective-permute-start.5 = (s32[1024,3]{1,0:T(8,128)S(1)}, s32[1024,3]{1,0:T(8,128)S(1)}, u32[]{:S(2)}, u32[]{:S(2)}) collective-permute-start(s32[1024,3]{1,0:T(8,128)S(1)} %copy.15.refs_3_.refs_5_), channel_id=1, source_target_pairs={{0,2},{1,3},{2,0},{3,1},{4,6},{5,7},{6,4},{7,5},{8,10},{9,11},{10,... | collective-permute-start | bytes 36872 | tf_op jit(solution)/shard_map/ppermute | solution.py:192
  34.4 13.6 %collective-permute-start.8 = (bf16[128,1792]{1,0:T(8,128)(2,1)}, bf16[128,1792]{1,0:T(8,128)(2,1)S(1)}, u32[]{:S(2)}, u32[]{:S(2)}) collective-permute-start(bf16[128,1792]{1,0:T(8,128)(2,1)} %collective-permute-done.3.refs_1_), channel_id=1, source_target_pairs={{0,16},{1,17},{2,18},{3,19},{4,20},{5,21},{6,22},{7,23},{8,24},{9,... | collective-permute-start | bytes 1376264 | tf_op jit(solution)/shard_map/ppermute | solution.py:192
  34.8 22.0 %collective-permute-start.6 = (bf16[128,1792]{1,0:T(8,128)(2,1)}, bf16[128,1792]{1,0:T(8,128)(2,1)S(1)}, u32[]{:S(2)}, u32[]{:S(2)}) collective-permute-start(bf16[128,1792]{1,0:T(8,128)(2,1)} %collective-permute-done.3.refs_1_), channel_id=1, source_target_pairs={{0,4},{1,5},{2,6},{3,7},{4,8},{5,9},{6,10},{7,11},{8,12},{9,13},{1... | collective-permute-start | bytes 1376264 | tf_op jit(solution)/shard_map/ppermute | solution.py:192
  41.3 20.2 %collective-permute-start.2 = (bf16[136,1792]{1,0:T(8,128)(2,1)}, bf16[136,1792]{1,0:T(8,128)(2,1)S(1)}, u32[]{:S(2)}, u32[]{:S(2)}) collective-permute-start(bf16[136,1792]{1,0:T(8,128)(2,1)} %collective-permute-done.1.refs_0_), channel_id=1, source_target_pairs={{0,4},{1,5},{2,6},{3,7},{4,8},{5,9},{6,10},{7,11},{8,12},{9,13},{1... | collective-permute-start | bytes 1462280 | tf_op jit(solution)/shard_map/ppermute | solution.py:192
  41.3 21.8 %collective-permute-start.10 = (bf16[136,1792]{1,0:T(8,128)(2,1)}, bf16[136,1792]{1,0:T(8,128)(2,1)S(1)}, u32[]{:S(2)}, u32[]{:S(2)}) collective-permute-start(bf16[136,1792]{1,0:T(8,128)(2,1)} %collective-permute-done.1.refs_0_), channel_id=1, source_target_pairs={{0,16},{1,17},{2,18},{3,19},{4,20},{5,21},{6,22},{7,23},{8,24},{9,... | collective-permute-start | bytes 1462280 | tf_op jit(solution)/shard_map/ppermute | solution.py:192
  56.8 13.5 %collective-permute-start.11 = (bf16[128,1792]{1,0:T(8,128)(2,1)S(1)}, bf16[128,1792]{1,0:T(8,128)(2,1)S(1)}, u32[]{:S(2)}, u32[]{:S(2)}) collective-permute-start(bf16[128,1792]{1,0:T(8,128)(2,1)S(1)} %collective-permute-done.6.refs_1_), channel_id=1, source_target_pairs={{0,16},{1,17},{2,18},{3,19},{4,20},{5,21},{6,22},{7,23},{8,24},{9,... | collective-permute-start | bytes 1376264 | tf_op jit(solution)/shard_map/ppermute | solution.py:192
  57.2 21.6 %collective-permute-start.9 = (bf16[128,1792]{1,0:T(8,128)(2,1)S(1)}, bf16[128,1792]{1,0:T(8,128)(2,1)S(1)}, u32[]{:S(2)}, u32[]{:S(2)}) collective-permute-start(bf16[128,1792]{1,0:T(8,128)(2,1)S(1)} %collective-permute-done.6.refs_1_), channel_id=1, source_target_pairs={{0,4},{1,5},{2,6},{3,7},{4,8},{5,9},{6,10},{7,11},{8,12},{9,13},{1... | collective-permute-start | bytes 1376264 | tf_op jit(solution)/shard_map/ppermute | solution.py:192
  61.4 18.4 %collective-permute-start.12 = (bf16[136,1792]{1,0:T(8,128)(2,1)S(1)}, bf16[136,1792]{1,0:T(8,128)(2,1)S(1)}, u32[]{:S(2)}, u32[]{:S(2)}) collective-permute-start(bf16[136,1792]{1,0:T(8,128)(2,1)S(1)} %collective-permute-done.2.refs_0_), channel_id=1, source_target_pairs={{0,16},{1,17},{2,18},{3,19},{4,20},{5,21},{6,22},{7,23},{8,24},{9,... | collective-permute-start | bytes 1462280 | tf_op jit(solution)/shard_map/ppermute | solution.py:192
  78.8 9.3 %collective-permute-start.13 = (bf16[128,1792]{1,0:T(8,128)(2,1)S(1)}, bf16[128,1792]{1,0:T(8,128)(2,1)S(1)}, u32[]{:S(2)}, u32[]{:S(2)}) collective-permute-start(bf16[128,1792]{1,0:T(8,128)(2,1)S(1)} %collective-permute-done.9.refs_1_), channel_id=1, source_target_pairs={{0,16},{1,17},{2,18},{3,19},{4,20},{5,21},{6,22},{7,23},{8,24},{9,... | collective-permute-start | bytes 1376264 | tf_op jit(solution)/shard_map/ppermute | solution.py:192
  91.5 2.4 %collective-permute-start.14 = (bf16[512,768]{1,0:T(8,128)(2,1)S(1)}, bf16[512,768]{1,0:T(8,128)(2,1)S(1)}, u32[]{:S(2)}, u32[]{:S(2)}) collective-permute-start(bf16[512,768]{1,0:T(8,128)(2,1)S(1)} %get-tuple-element.75), channel_id=1, source_target_pairs={{0,2},{1,3},{2,0},{3,1},{4,6},{5,7},{6,4},{7,5},{8,10},{9,11},{10,... | collective-permute-start | bytes 2359304 | tf_op jit(solution)/shard_map/ppermute | solution.py:192
  91.6 2.3 %collective-permute-start.15 = (f32[8,512]{1,0:T(8,128)S(1)}, f32[8,512]{1,0:T(8,128)S(1)}, u32[]{:S(2)}, u32[]{:S(2)}) collective-permute-start(f32[8,512]{1,0:T(8,128)S(1)} %get-tuple-element.76), channel_id=1, source_target_pairs={{0,2},{1,3},{2,0},{3,1},{4,6},{5,7},{6,4},{7,5},{8,10},{9,11},{10,... | collective-permute-start | bytes 49160 | tf_op jit(solution)/shard_map/ppermute | solution.py:192
  96.3 20.0 %collective-permute-start.19 = (bf16[512,768]{1,0:T(8,128)(2,1)S(1)}, bf16[512,768]{1,0:T(8,128)(2,1)S(1)}, u32[]{:S(2)}, u32[]{:S(2)}) collective-permute-start(bf16[512,768]{1,0:T(8,128)(2,1)S(1)} %get-tuple-element.85), channel_id=1, source_target_pairs={{0,1},{1,0},{2,3},{3,2},{4,5},{5,4},{6,7},{7,6},{8,9},{9,8},{10,11... | collective-permute-start | bytes 2359304 | tf_op jit(solution)/shard_map/ppermute | solution.py:192
  101.3 15.0 %collective-permute-start.16 = (bf16[256,768]{1,0:T(8,128)(2,1)S(1)}, bf16[256,768]{1,0:T(8,128)(2,1)S(1)}, u32[]{:S(2)}, u32[]{:S(2)}) collective-permute-start(bf16[256,768]{1,0:T(8,128)(2,1)S(1)} %get-tuple-element.88), channel_id=1, source_target_pairs={{0,2},{1,3},{2,0},{3,1},{4,6},{5,7},{6,4},{7,5},{8,10},{9,11},{10,... | collective-permute-start | bytes 1179656 | tf_op jit(solution)/shard_map/ppermute | solution.py:192
  101.3 15.0 %collective-permute-start.17 = (bf16[256,768]{1,0:T(8,128)(2,1)S(1)}, bf16[256,768]{1,0:T(8,128)(2,1)S(1)}, u32[]{:S(2)}, u32[]{:S(2)}) collective-permute-start(bf16[256,768]{1,0:T(8,128)(2,1)S(1)} %get-tuple-element.87), channel_id=1, source_target_pairs={{0,2},{1,3},{2,0},{3,1},{4,6},{5,7},{6,4},{7,5},{8,10},{9,11},{10,... | collective-permute-start | bytes 1179656 | tf_op jit(solution)/shard_map/ppermute | solution.py:192
  101.8 3.0 %collective-permute-start.18 = (f32[8,512]{1,0:T(8,128)S(1)}, f32[8,512]{1,0:T(8,128)S(1)}, u32[]{:S(2)}, u32[]{:S(2)}) collective-permute-start(f32[8,512]{1,0:T(8,128)S(1)} %get-tuple-element.84), channel_id=1, source_target_pairs={{0,2},{1,3},{2,0},{3,1},{4,6},{5,7},{6,4},{7,5},{8,10},{9,11},{10,... | collective-permute-start | bytes 49160 | tf_op jit(solution)/shard_map/ppermute | solution.py:192
  101.9 14.4 %collective-permute-start.20 = (f32[8,512]{1,0:T(8,128)S(1)}, f32[8,512]{1,0:T(8,128)S(1)}, u32[]{:S(2)}, u32[]{:S(2)}) collective-permute-start(f32[8,512]{1,0:T(8,128)S(1)} %get-tuple-element.86), channel_id=1, source_target_pairs={{0,1},{1,0},{2,3},{3,2},{4,5},{5,4},{6,7},{7,6},{8,9},{9,8},{10,11... | collective-permute-start | bytes 49160 | tf_op jit(solution)/shard_map/ppermute | solution.py:192
  (3 other events, 3.6 us)

commit v3 on v2

--- a/solution.py
+++ b/solution.py
@@ -8,12 +8,13 @@
 from jax.sharding import PartitionSpec as P
 
 AXES = ("groups", "loop", "rep")
-DOC_TILE = 256
+DOC_TILE = 1024
 VMEM_LIMIT = 24 * 1024 * 1024
 SHARES = (1, 1)
-TIES = {("first", 1): 1, ("mid", 1): 1, ("last", 1): 1}
+TIES = {("first", 0): 1, ("mid", 1): 1, ("last", 1): 1}
 BIAS_ROWS = 8
-COST_NEXT = 4400000000
+NEAR = 64
+COST_NEXT = 13200000000
 
 
 def joined(xs, axis):
@@ -25,19 +26,24 @@
 
 
 def accumulate(spec, table, bias_ref, *refs):
-    step, offsets, parts, part_rows, sets, first, where, reps, received = spec
-    count = max(1, len(offsets)) * parts
-    labels, refs = refs[: 2 if not offsets else count], refs[2 if not offsets else count :]
-    if offsets:
-        lead, bias_rows, weight_rows, embed_rows = len(offsets), [], [], []
-        for k, ref in enumerate(labels):
-            offset = offsets[k % lead]
+    step, pieces, part_rows, sets, first, where, reps, received = spec
+    count = max(2, len(pieces))
+    labels, refs = refs[:count], refs[count:]
+    if pieces:
+        width = refs[0].shape[1]
+        leads = {part: ref for (part, offset), ref in zip(pieces, labels) if offset == 0}
+        bias_rows, weight_rows, embed_rows = [], [], []
+        for (part, offset), ref in zip(pieces, labels):
             rows = ref.shape[0] - (0 if offset else BIAS_ROWS)
-            width = sets_width(refs)
             weight_rows.append(ref[:rows, :width])
             embed_rows.append(ref[:rows, width:])
-            source = labels[k - k % lead]
-            row = source[source.shape[0] - BIAS_ROWS :, :part_rows].astype(jnp.float32)[:1]
+            if leads:
+                lead = leads[part]
+                row = lead[lead.shape[0] - BIAS_ROWS :, :part_rows].astype(jnp.float32)[:1]
+            else:
+                row = bias_ref[:1, part * part_rows : (part + 1) * part_rows]
+            if where == "all" and offset == 0:
+                refs[-1][:, part * part_rows : (part + 1) * part_rows] = jnp.broadcast_to(row, (8, part_rows))
             bias_rows.append(row[:, offset : offset + rows])
         bias = joined(bias_rows, 1)
         weight_rows, embed_rows = joined(weight_rows, 0), joined(embed_rows, 0)
@@ -82,14 +88,10 @@
                 sum_out[to_rows, :] = sums
 
 
-def sets_width(refs):
-    return refs[0].shape[1]
-
-
-def add_labels(table, bias, labels, sets, *, step, offsets, parts, part_rows, reps, where="all", out=jnp.float32):
-    embed_width = labels[1].shape[1] if not offsets else labels[0].shape[1] - sets[0][0].shape[1]
+def add_labels(table, bias, labels, sets, *, step, pieces, parts, part_rows, reps, where="all", out=jnp.float32):
+    embed_width = labels[0].shape[1] - sets[0][0].shape[1] if pieces else labels[1].shape[1]
     first, received = len(sets[0]) == 2, len(sets[0]) > 4
-    spec = (step, offsets, parts, part_rows, len(sets), first, where, reps, received)
+    spec = (step, pieces, part_rows, len(sets), first, where, reps, received)
     operands = [bias, *labels]
     aliases, out_shape = {}, []
     for k, one in enumerate(sets):
@@ -101,6 +103,8 @@
         operands += one
         out_shape.append(jax.ShapeDtypeStruct((rows, embed_width), out))
         out_shape.append(jax.ShapeDtypeStruct((rows, 1) if out == jnp.float32 else (8, rows), jnp.float32))
+    if pieces and where == "all":
+        out_shape.append(jax.ShapeDtypeStruct((8, parts * part_rows), jnp.float32))
     outs = pl.pallas_call(
         functools.partial(accumulate, spec),
         in_specs=[pl.BlockSpec(memory_space=pltpu.SMEM)] + [pl.BlockSpec(memory_space=pltpu.VMEM)] * len(operands),
@@ -110,7 +114,8 @@
         compiler_params=pltpu.CompilerParams(vmem_limit_bytes=VMEM_LIMIT),
         cost_estimate=pl.CostEstimate(flops=0, bytes_accessed=0, transcendentals=0),
     )(table, *operands)
-    return [list(outs[2 * k : 2 * k + 2]) for k in range(len(sets))]
+    totals = [list(outs[2 * k : 2 * k + 2]) for k in range(len(sets))]
+    return (totals, outs[-1]) if len(outs) > 2 * len(sets) else totals
 
 
 def combine(mix_ref, sum_ref, *refs):
@@ -170,7 +175,7 @@
         scratch_shapes=[pltpu.SemaphoreType.DMA((2,))],
         compiler_params=pltpu.CompilerParams(vmem_limit_bytes=VMEM_LIMIT),
         cost_estimate=pl.CostEstimate(flops=cost, bytes_accessed=0, transcendentals=0),
-    )(table, weight, embed, bias)
+    )(table, *[pltpu.with_memory_space_constraint(x, pltpu.HBM) for x in (weight, embed)], bias)
 
 
 def per_device(sizes, documents, block_ids, label_weight, label_bias, label_embed):
@@ -214,9 +219,9 @@
     sets = [[documents, block_ids]]
     if cores == 2:
         sets.append([other_core(documents), other_core(block_ids)])
-    call = functools.partial(add_labels, table, bias)
-    common = dict(part_rows=part_rows, reps=reps)
-    history = [call([label_weight, label_embed], sets, step=0, offsets=(), parts=1, **common)]
+    call = functools.partial(add_labels, table)
+    common = dict(parts=groups, part_rows=part_rows, reps=reps)
+    history = [call(bias, [label_weight, label_embed], sets, step=0, pieces=(), **common)]
 
     def after(x, step, index):
         back = TIES.get(("last" if step + 1 == chips else "first" if step == 1 else "mid", index))
@@ -225,16 +230,30 @@
         x, history[step - back] = lax.optimization_barrier((x, history[step - back]))
         return x
 
+    def kernel(pieces, bias, step):
+        arrays = [x for _, x in pieces]
+        one = [s + t for s, t in zip(sets, history[-1])]
+        return call(bias, arrays, one, step=step, pieces=tuple(place for place, _ in pieces), **common)
+
+    final = len(chunks) - 1
     for step in range(1, chips):
-        arrived = []
-        for index in range(len(chunks)):
+        earlier, arrived = (arrived if step > 1 else None), []
+        for index, (offset, rows) in enumerate(chunks):
+            near = rows * NEAR // 128 // 16 * 16 if step + 1 == chips and index == final and step > 1 else rows
             flying[index] = after(along(flying[index]), step, index)
-            arrived.append([flying[index]] + [across(flying[index], k) for k in range(1, groups)])
-        labels = [pieces[part] for part in range(groups) for pieces in arrived]
-        here = dict(step=step, offsets=tuple(offset for offset, _ in chunks), parts=groups, **common)
+            pieces = [((0, offset), flying[index])]
+            for k in range(1, groups):
+                pieces.append(((k, offset), across(flying[index][:near] if near < rows else flying[index], k)))
+                if near < rows:
+                    pieces.append(((k, offset + near), along(earlier[index][k][1][near:])))
+            arrived.append(pieces)
         if step + 1 < chips:
-            history.append(call(labels, [one + t for one, t in zip(sets, history[-1])], **here))
-    held = [one + t for one, t in zip(sets, history[-1])]
+            history.append(kernel(sum(arrived, []), bias, step)[0])
+    totals, bias = kernel(sum(arrived[:final], []), bias, chips - 1)
+    held = [one + t for one, t in zip(sets, totals)]
+    labels = [x for _, x in arrived[final]]
+    here = dict(step=chips - 1, pieces=tuple(place for place, _ in arrived[final]), **common)
+    call = functools.partial(call, bias)
 
     narrow = dict(out=jnp.bfloat16, **here)
     tile_docs = doc_count // reps

time: 118 us -> 108 us (0.915)
  Pallas kernels: 40.4 us -> 34.5 us
  waiting for transfers between devices: 55.1 us -> 50.2 us
  starting transfers between devices: 17.4 us -> 19.5 us
    pallas_call x7 -> x8, Pallas kernels: 37 us -> 28.3 us  [add_labels(): pl.pallas_call(functools.partial(accumulate, spec), in_specs=[pl.BlockSpe...]
    ppermute x21 -> x22, waiting for transfers between devices: 55.1 us -> 50.2 us  [moved(): return lax.ppermute(x, AXES, pairs)]
    pallas_call x2, Pallas kernels: 1.98 us -> 4.68 us  [packed_part(): pl.pallas_call(functools.partial(pack, (offset, rows, part_rows, groups))...]
    ppermute x21 -> x22, starting transfers between devices: 17.4 us -> 19.5 us  [moved(): return lax.ppermute(x, AXES, pairs)]
    unnamed x13 -> x11, local copies, waits for them, and re-layouts: 3.82 us -> 3.05 us
  transfers between devices with their start and end apart: 21 -> 22, of which waited for: 10 -> 10; matrix products, arithmetic and copies ran while one was open for 1% -> 1% of each run, Pallas kernels for 28% -> 27%
where the time goes in v3:
time: 108 us
  waiting for transfers between devices  50.2 us (46%)
  Pallas kernels  34.5 us (32%)
  starting transfers between devices  19.5 us (18%)
  local copies, waits for them, and re-layouts  3.23 us (3%)
    ppermute x22, waiting for transfers between devices, moved(): return lax.ppermute(x, AXES, pairs)  50.2 us
    pallas_call x8, Pallas kernels, add_labels(): pl.pallas_call(functools.partial(accumulate, spec), in_specs=[pl.BlockSpe...  28.3 us
    ppermute x22, starting transfers between devices, moved(): return lax.ppermute(x, AXES, pairs)  19.5 us
    pallas_call x2, Pallas kernels, packed_part(): pl.pallas_call(functools.partial(pack, (offset, rows, part_rows, groups))...  4.68 us
    unnamed x11, local copies, waits for them, and re-layouts  3.05 us
  transfers between devices with their start and end apart: 22, of which 10 were waited for; matrix products, arithmetic and copies ran while one was open for 1% of the time, Pallas kernels for 27%

profile of v3, /device:TPU:0, one launch (start us, length us, event | category | flops | bytes accessed | tf_op | source)
XLA Modules:
  0.0 108.2 jit_solution(938565879002497957)
XLA Ops:
  1.2 2.3 %shard_map.55 = bf16[136,1792]{1,0:T(8,128)(2,1)} custom-call(s32[6]{0:T(128)S(1)} %stack.27.table, bf16[512,1024]{1,0:T(8,128)(2,1)} %weight.3, bf16[512,768]{1,0:T(8,128)(2,1)} %embed.3, f32[1,512]{1,0:T(1,128)S(1)} %bitcast.7), custom_call_target="tpu_custom_call" | custom-call | tf_op jit(solution)/shard_map/pallas_call | solution.py:168
  3.6 2.6 %collective-permute-start = (bf16[136,1792]{1,0:T(8,128)(2,1)}, bf16[136,1792]{1,0:T(8,128)(2,1)}, u32[]{:S(2)}, u32[]{:S(2)}) collective-permute-start(bf16[136,1792]{1,0:T(8,128)(2,1)} %shard_map.55), channel_id=1, source_target_pairs={{0,4},{1,5},{2,6},{3,7},{4,8},{5,9},{6,10},{7,11},{8,12},{9,13},{1... | collective-permute-start | bytes 1462280 | tf_op jit(solution)/shard_map/ppermute | solution.py:197
  6.2 2.3 %shard_map.57 = bf16[128,1792]{1,0:T(8,128)(2,1)} custom-call(s32[6]{0:T(128)S(1)} %stack.27.table, bf16[512,1024]{1,0:T(8,128)(2,1)} %weight.3, bf16[512,768]{1,0:T(8,128)(2,1)} %embed.3, f32[1,512]{1,0:T(1,128)S(1)} %bitcast.8), custom_call_target="tpu_custom_call" | custom-call | flops 13200000000 | tf_op jit(solution)/shard_map/pallas_call | solution.py:168
  8.6 1.6 %collective-permute-start.6 = (bf16[128,1792]{1,0:T(8,128)(2,1)}, bf16[128,1792]{1,0:T(8,128)(2,1)}, u32[]{:S(2)}, u32[]{:S(2)}) collective-permute-start(bf16[128,1792]{1,0:T(8,128)(2,1)} %shard_map.57), channel_id=1, source_target_pairs={{0,4},{1,5},{2,6},{3,7},{4,8},{5,9},{6,10},{7,11},{8,12},{9,13},{1... | collective-permute-start | bytes 1376264 | tf_op jit(solution)/shard_map/ppermute | solution.py:197
  10.5 1.9 %collective-permute-done.2.refs_5_.refs_9_.refs_7_.refs_4_ = s32[1024,3]{1,0:T(8,128)S(1)} collective-permute-done((s32[1024,3]{1,0:T(8,128)S(1)}, s32[1024,3]{1,0:T(8,128)S(1)}, u32[]{:S(2)}, u32[]{:S(2)}) %collective-permute-start.2) | collective-permute-done | bytes 12320 | tf_op jit(solution)/shard_map/ppermute | solution.py:197
  15.2 4.8 %shard_map.56 = (f32[1024,768]{1,0:T(8,128)S(1)}, f32[1024,1]{1,0:T(8,128)S(1)}, f32[1024,768]{1,0:T(8,128)S(1)}, f32[1024,1]{1,0:T(8,128)S(1)}) custom-call(s32[6]{0:T(128)S(1)} %stack.27.table, f32[1,512]{1,0:T(1,128)S(1)} %bitcast.9, bf16[512,1024]{1,0:T(8,128)(2,1)S(1)} %copy-done.2, bf16[512,768]{1,0:T(8,128)(2,1)S(1)} %copy-done.3, ...), custom_call_target="tpu_custom_call" | custom-call | tf_op jit(solution)/shard_map/pallas_call | solution.py:108
  23.2 7.2 %collective-permute-done.6.refs_2_ = bf16[128,1792]{1,0:T(8,128)(2,1)} collective-permute-done((bf16[128,1792]{1,0:T(8,128)(2,1)}, bf16[128,1792]{1,0:T(8,128)(2,1)}, u32[]{:S(2)}, u32[]{:S(2)}) %collective-permute-start.6) | collective-permute-done | bytes 458784 | tf_op jit(solution)/shard_map/ppermute | solution.py:197
  30.4 1.6 %collective-permute-start.9 = (bf16[128,1792]{1,0:T(8,128)(2,1)}, bf16[128,1792]{1,0:T(8,128)(2,1)S(1)}, u32[]{:S(2)}, u32[]{:S(2)}) collective-permute-start(bf16[128,1792]{1,0:T(8,128)(2,1)} %collective-permute-done.6.refs_2_), channel_id=1, source_target_pairs={{0,16},{1,17},{2,18},{3,19},{4,20},{5,21},{6,22},{7,23},{8,24},{9,... | collective-permute-start | bytes 1376264 | tf_op jit(solution)/shard_map/ppermute | solution.py:197
  32.0 8.7 %collective-permute-done.3.refs_0_ = bf16[136,1792]{1,0:T(8,128)(2,1)S(1)} collective-permute-done((bf16[136,1792]{1,0:T(8,128)(2,1)}, bf16[136,1792]{1,0:T(8,128)(2,1)S(1)}, u32[]{:S(2)}, u32[]{:S(2)}) %collective-permute-start.3) | collective-permute-done | bytes 487456 | tf_op jit(solution)/shard_map/ppermute | solution.py:197
  40.7 1.6 %collective-permute-start.11 = (bf16[136,1792]{1,0:T(8,128)(2,1)S(1)}, bf16[136,1792]{1,0:T(8,128)(2,1)S(1)}, u32[]{:S(2)}, u32[]{:S(2)}) collective-permute-start(bf16[136,1792]{1,0:T(8,128)(2,1)S(1)} %collective-permute-done.3.refs_0_), channel_id=1, source_target_pairs={{0,16},{1,17},{2,18},{3,19},{4,20},{5,21},{6,22},{7,23},{8,24},{9,... | collective-permute-start | bytes 1462280 | tf_op jit(solution)/shard_map/ppermute | solution.py:197
  42.4 3.4 %collective-permute-done.9.refs_3_ = bf16[128,1792]{1,0:T(8,128)(2,1)S(1)} collective-permute-done((bf16[128,1792]{1,0:T(8,128)(2,1)}, bf16[128,1792]{1,0:T(8,128)(2,1)S(1)}, u32[]{:S(2)}, u32[]{:S(2)}) %collective-permute-start.9) | collective-permute-done | bytes 458784 | tf_op jit(solution)/shard_map/ppermute | solution.py:197
  45.7 6.4 %shard_map.58 = (f32[1024,768]{1,0:T(8,128)S(1)}, f32[1024,1]{1,0:T(8,128)S(1)}, f32[1024,768]{1,0:T(8,128)S(1)}, f32[1024,1]{1,0:T(8,128)S(1)}, f32[8,512]{1,0:T(8,128)}) custom-call(s32[6]{0:T(128)S(1)} %stack.27.table, f32[1,512]{1,0:T(1,128)S(1)} %bitcast.10, ...), custom_call_target="tpu_custom_call", output_to_operand_aliasing={{0}: (8, {}), {1}: (9, {}), {2}: (12, {}), {3}: (13, {})} | custom-call | tf_op jit(solution)/shard_map/pallas_call | solution.py:108
  53.9 7.1 %collective-permute-done.4.refs_0_ = bf16[136,1792]{1,0:T(8,128)(2,1)S(1)} collective-permute-done((bf16[136,1792]{1,0:T(8,128)(2,1)S(1)}, bf16[136,1792]{1,0:T(8,128)(2,1)S(1)}, u32[]{:S(2)}, u32[]{:S(2)}) %collective-permute-start.4) | collective-permute-done | bytes 487456 | tf_op jit(solution)/shard_map/ppermute | solution.py:197
  61.0 1.6 %collective-permute-start.5 = (bf16[136,1792]{1,0:T(8,128)(2,1)S(1)}, bf16[136,1792]{1,0:T(8,128)(2,1)S(1)}, u32[]{:S(2)}, u32[]{:S(2)}) collective-permute-start(bf16[136,1792]{1,0:T(8,128)(2,1)S(1)} %collective-permute-done.4.refs_0_), channel_id=1, source_target_pairs={{0,16},{1,17},{2,18},{3,19},{4,20},{5,21},{6,22},{7,23},{8,24},{9,... | collective-permute-start | bytes 1462280 | tf_op jit(solution)/shard_map/ppermute | solution.py:197
  62.6 3.4 %collective-permute-done.12.refs_3_ = bf16[128,1792]{1,0:T(8,128)(2,1)S(1)} collective-permute-done((bf16[128,1792]{1,0:T(8,128)(2,1)S(1)}, bf16[128,1792]{1,0:T(8,128)(2,1)S(1)}, u32[]{:S(2)}, u32[]{:S(2)}) %collective-permute-start.12) | collective-permute-done | bytes 458784 | tf_op jit(solution)/shard_map/ppermute | solution.py:197
  66.5 5.8 %shard_map.59 = (f32[1024,768]{1,0:T(8,128)S(1)}, f32[1024,1]{1,0:T(8,128)S(1)}, f32[1024,768]{1,0:T(8,128)S(1)}, f32[1024,1]{1,0:T(8,128)S(1)}, f32[8,512]{1,0:T(8,128)}) custom-call(s32[6]{0:T(128)S(1)} %stack.27.table, f32[1,512]{1,0:T(1,128)S(1)} %bitcast.11, ...), custom_call_target="tpu_custom_call", output_to_operand_aliasing={{0}: (8, {}), {1}: (9, {}), {2}: (12, {}), {3}: (13, {})} | custom-call | tf_op jit(solution)/shard_map/pallas_call | solution.py:108
  73.9 2.5 %collective-permute-done.5.refs_1_ = bf16[136,1792]{1,0:T(8,128)(2,1)S(1)} collective-permute-done((bf16[136,1792]{1,0:T(8,128)(2,1)S(1)}, bf16[136,1792]{1,0:T(8,128)(2,1)S(1)}, u32[]{:S(2)}, u32[]{:S(2)}) %collective-permute-start.5) | collective-permute-done | bytes 487456 | tf_op jit(solution)/shard_map/ppermute | solution.py:197
  76.5 4.4 %shard_map.60 = (f32[1024,768]{1,0:T(8,128)S(1)}, f32[1024,1]{1,0:T(8,128)S(1)}, f32[1024,768]{1,0:T(8,128)S(1)}, f32[1024,1]{1,0:T(8,128)S(1)}, f32[8,512]{1,0:T(8,128)S(1)}) custom-call(s32[6]{0:T(128)S(1)} %stack.27.table, f32[1,512]{1,0:T(1,128)S(1)} %bitcast.12, ...), custom_call_target="tpu_custom_call", output_to_operand_aliasing={{0}: (6, {}), {1}: (7, {}), {2}: (10, {}), {3}: (11, {})} | custom-call | tf_op jit(solution)/shard_map/pallas_call | solution.py:108
  80.9 1.8 %shard_map.62 = (bf16[512,768]{1,0:T(8,128)(2,1)S(1)}, f32[8,512]{1,0:T(8,128)S(1)}) custom-call(s32[6]{0:T(128)S(1)} %stack.27.table, f32[8,512]{1,0:T(8,128)S(1)} %get-tuple-element.77.bias_ref, bf16[128,1792]{1,0:T(8,128)(2,1)S(1)} %collective-permute-done.10.refs_0_, bf16[64,1792]{1,0:T(8,128)(2,1)S(1)} %collective-permute-done.13.refs_1_, ...), custom_call_target="tpu_custom_call" | custom-call | tf_op jit(solution)/shard_map/pallas_call | solution.py:108
  83.2 1.8 %collective-permute-done.16.refs_8_ = f32[8,512]{1,0:T(8,128)S(1)} collective-permute-done((f32[8,512]{1,0:T(8,128)S(1)}, f32[8,512]{1,0:T(8,128)S(1)}, u32[]{:S(2)}, u32[]{:S(2)}) %collective-permute-start.16) | collective-permute-done | bytes 16416 | tf_op jit(solution)/shard_map/ppermute | solution.py:197
  85.0 1.8 %shard_map.63 = (bf16[512,768]{1,0:T(8,128)(2,1)S(1)}, f32[8,512]{1,0:T(8,128)S(1)}) custom-call(s32[6]{0:T(128)S(1)} %stack.27.table, f32[8,512]{1,0:T(8,128)S(1)} %get-tuple-element.77.bias_ref, bf16[128,1792]{1,0:T(8,128)(2,1)S(1)} %collective-permute-done.10.refs_0_, bf16[64,1792]{1,0:T(8,128)(2,1)S(1)} %collective-permute-done.13.refs_1_, ...), custom_call_target="tpu_custom_call" | custom-call | tf_op jit(solution)/shard_map/pallas_call | solution.py:108
  88.4 1.8 %shard_map.64 = (bf16[512,768]{1,0:T(8,128)(2,1)S(1)}, f32[8,512]{1,0:T(8,128)S(1)}) custom-call(s32[6]{0:T(128)S(1)} %stack.27.table, f32[8,512]{1,0:T(8,128)S(1)} %get-tuple-element.77.bias_ref, bf16[128,1792]{1,0:T(8,128)(2,1)S(1)} %collective-permute-done.10.refs_0_, bf16[64,1792]{1,0:T(8,128)(2,1)S(1)} %collective-permute-done.13.refs_1_, ...), custom_call_target="tpu_custom_call" | custom-call | tf_op jit(solution)/shard_map/pallas_call | solution.py:108
  91.4 1.6 %shard_map.61 = (f32[512,768]{1,0:T(8,128)S(1)}, f32[512,1]{1,0:T(8,128)S(1)}) custom-call(s32[6]{0:T(128)S(1)} %stack.27.table, f32[8,512]{1,0:T(8,128)S(1)} %get-tuple-element.77.bias_ref, bf16[128,1792]{1,0:T(8,128)(2,1)S(1)} %collective-permute-done.10.refs_0_, bf16[64,1792]{1,0:T(8,128)(2,1)S(1)} %collective-permute-done.13.refs_1_, ...), custom_call_target="tpu_custom_call" | custom-call | tf_op jit(solution)/shard_map/pallas_call | solution.py:108
  93.0 13.8 %collective-permute-done.21.refs_4_ = f32[8,512]{1,0:T(8,128)S(1)} collective-permute-done((f32[8,512]{1,0:T(8,128)S(1)}, f32[8,512]{1,0:T(8,128)S(1)}, u32[]{:S(2)}, u32[]{:S(2)}) %collective-permute-start.21) | collective-permute-done | bytes 16416 | tf_op jit(solution)/shard_map/ppermute | solution.py:197
  (47 shorter events, 16.2 us)
Async XLA Ops:
  0.0 12.4 %collective-permute-start.1 = (bf16[1024,1024]{1,0:T(8,128)(2,1)}, bf16[1024,1024]{1,0:T(8,128)(2,1)S(1)}, u32[]{:S(2)}, u32[]{:S(2)}) collective-permute-start(bf16[1024,1024]{1,0:T(8,128)(2,1)} %refs_3_.5), channel_id=1, source_target_pairs={{0,2},{1,3},{2,0},{3,1},{4,6},{5,7},{6,4},{7,5},{8,10},{9,11},{10,... | collective-permute-start | bytes 6291464 | tf_op jit(solution)/shard_map/ppermute | solution.py:197
  3.6 8.8 %copy-start.3 = (bf16[512,768]{1,0:T(8,128)(2,1)S(1)}, bf16[512,768]{1,0:T(8,128)(2,1)}, u32[]{:S(2)}) copy-start(bf16[512,768]{1,0:T(8,128)(2,1)} %embed.3) | copy-start | bytes 2359300
  3.6 17.0 %collective-permute-start = (bf16[136,1792]{1,0:T(8,128)(2,1)}, bf16[136,1792]{1,0:T(8,128)(2,1)}, u32[]{:S(2)}, u32[]{:S(2)}) collective-permute-start(bf16[136,1792]{1,0:T(8,128)(2,1)} %shard_map.55), channel_id=1, source_target_pairs={{0,4},{1,5},{2,6},{3,7},{4,8},{5,9},{6,10},{7,11},{8,12},{9,13},{1... | collective-permute-start | bytes 1462280 | tf_op jit(solution)/shard_map/ppermute | solution.py:197
  8.6 21.8 %collective-permute-start.6 = (bf16[128,1792]{1,0:T(8,128)(2,1)}, bf16[128,1792]{1,0:T(8,128)(2,1)}, u32[]{:S(2)}, u32[]{:S(2)}) collective-permute-start(bf16[128,1792]{1,0:T(8,128)(2,1)} %shard_map.57), channel_id=1, source_target_pairs={{0,4},{1,5},{2,6},{3,7},{4,8},{5,9},{6,10},{7,11},{8,12},{9,13},{1... | collective-permute-start | bytes 1376264 | tf_op jit(solution)/shard_map/ppermute | solution.py:197
  10.4 2.0 %collective-permute-start.2 = (s32[1024,3]{1,0:T(8,128)S(1)}, s32[1024,3]{1,0:T(8,128)S(1)}, u32[]{:S(2)}, u32[]{:S(2)}) collective-permute-start(s32[1024,3]{1,0:T(8,128)S(1)} %copy.19.refs_3_.refs_5_.refs_4_), channel_id=1, source_target_pairs={{0,2},{1,3},{2,0},{3,1},{4,6},{5,7},{6,4},{7,5},{8,10},{9,11},{10,... | collective-permute-start | bytes 36872 | tf_op jit(solution)/shard_map/ppermute | solution.py:197
  15.2 30.5 %copy-start.1 = (bf16[1024,1024]{1,0:T(8,128)(2,1)S(1)}, bf16[1024,1024]{1,0:T(8,128)(2,1)}, u32[]{:S(2)}) copy-start(bf16[1024,1024]{1,0:T(8,128)(2,1)} %refs_3_.5) | copy-start | bytes 6291460
  20.6 20.2 %collective-permute-start.3 = (bf16[136,1792]{1,0:T(8,128)(2,1)}, bf16[136,1792]{1,0:T(8,128)(2,1)S(1)}, u32[]{:S(2)}, u32[]{:S(2)}) collective-permute-start(bf16[136,1792]{1,0:T(8,128)(2,1)} %collective-permute-done.refs_0_), channel_id=1, source_target_pairs={{0,4},{1,5},{2,6},{3,7},{4,8},{5,9},{6,10},{7,11},{8,12},{9,13},{1... | collective-permute-start | bytes 1462280 | tf_op jit(solution)/shard_map/ppermute | solution.py:197
  21.7 24.1 %collective-permute-start.8 = (bf16[136,1792]{1,0:T(8,128)(2,1)}, bf16[136,1792]{1,0:T(8,128)(2,1)S(1)}, u32[]{:S(2)}, u32[]{:S(2)}) collective-permute-start(bf16[136,1792]{1,0:T(8,128)(2,1)} %collective-permute-done.refs_0_), channel_id=1, source_target_pairs={{0,16},{1,17},{2,18},{3,19},{4,20},{5,21},{6,22},{7,23},{8,24},{9,... | collective-permute-start | bytes 1462280 | tf_op jit(solution)/shard_map/ppermute | solution.py:197
  30.4 15.3 %collective-permute-start.9 = (bf16[128,1792]{1,0:T(8,128)(2,1)}, bf16[128,1792]{1,0:T(8,128)(2,1)S(1)}, u32[]{:S(2)}, u32[]{:S(2)}) collective-permute-start(bf16[128,1792]{1,0:T(8,128)(2,1)} %collective-permute-done.6.refs_2_), channel_id=1, source_target_pairs={{0,16},{1,17},{2,18},{3,19},{4,20},{5,21},{6,22},{7,23},{8,24},{9,... | collective-permute-start | bytes 1376264 | tf_op jit(solution)/shard_map/ppermute | solution.py:197
  32.0 20.1 %collective-permute-start.7 = (bf16[128,1792]{1,0:T(8,128)(2,1)}, bf16[128,1792]{1,0:T(8,128)(2,1)S(1)}, u32[]{:S(2)}, u32[]{:S(2)}) collective-permute-start(bf16[128,1792]{1,0:T(8,128)(2,1)} %collective-permute-done.6.refs_2_), channel_id=1, source_target_pairs={{0,4},{1,5},{2,6},{3,7},{4,8},{5,9},{6,10},{7,11},{8,12},{9,13},{1... | collective-permute-start | bytes 1376264 | tf_op jit(solution)/shard_map/ppermute | solution.py:197
  40.7 20.3 %collective-permute-start.4 = (bf16[136,1792]{1,0:T(8,128)(2,1)S(1)}, bf16[136,1792]{1,0:T(8,128)(2,1)S(1)}, u32[]{:S(2)}, u32[]{:S(2)}) collective-permute-start(bf16[136,1792]{1,0:T(8,128)(2,1)S(1)} %collective-permute-done.3.refs_0_), channel_id=1, source_target_pairs={{0,4},{1,5},{2,6},{3,7},{4,8},{5,9},{6,10},{7,11},{8,12},{9,13},{1... | collective-permute-start | bytes 1462280 | tf_op jit(solution)/shard_map/ppermute | solution.py:197
  40.7 25.8 %collective-permute-start.11 = (bf16[136,1792]{1,0:T(8,128)(2,1)S(1)}, bf16[136,1792]{1,0:T(8,128)(2,1)S(1)}, u32[]{:S(2)}, u32[]{:S(2)}) collective-permute-start(bf16[136,1792]{1,0:T(8,128)(2,1)S(1)} %collective-permute-done.3.refs_0_), channel_id=1, source_target_pairs={{0,16},{1,17},{2,18},{3,19},{4,20},{5,21},{6,22},{7,23},{8,24},{9,... | collective-permute-start | bytes 1462280 | tf_op jit(solution)/shard_map/ppermute | solution.py:197
  52.1 13.9 %collective-permute-start.12 = (bf16[128,1792]{1,0:T(8,128)(2,1)S(1)}, bf16[128,1792]{1,0:T(8,128)(2,1)S(1)}, u32[]{:S(2)}, u32[]{:S(2)}) collective-permute-start(bf16[128,1792]{1,0:T(8,128)(2,1)S(1)} %collective-permute-done.7.refs_2_), channel_id=1, source_target_pairs={{0,16},{1,17},{2,18},{3,19},{4,20},{5,21},{6,22},{7,23},{8,24},{9,... | collective-permute-start | bytes 1376264 | tf_op jit(solution)/shard_map/ppermute | solution.py:197
  53.7 18.7 %collective-permute-start.10 = (bf16[128,1792]{1,0:T(8,128)(2,1)S(1)}, bf16[128,1792]{1,0:T(8,128)(2,1)S(1)}, u32[]{:S(2)}, u32[]{:S(2)}) collective-permute-start(bf16[128,1792]{1,0:T(8,128)(2,1)S(1)} %collective-permute-done.7.refs_2_), channel_id=1, source_target_pairs={{0,4},{1,5},{2,6},{3,7},{4,8},{5,9},{6,10},{7,11},{8,12},{9,13},{1... | collective-permute-start | bytes 1376264 | tf_op jit(solution)/shard_map/ppermute | solution.py:197
  61.0 15.5 %collective-permute-start.5 = (bf16[136,1792]{1,0:T(8,128)(2,1)S(1)}, bf16[136,1792]{1,0:T(8,128)(2,1)S(1)}, u32[]{:S(2)}, u32[]{:S(2)}) collective-permute-start(bf16[136,1792]{1,0:T(8,128)(2,1)S(1)} %collective-permute-done.4.refs_0_), channel_id=1, source_target_pairs={{0,16},{1,17},{2,18},{3,19},{4,20},{5,21},{6,22},{7,23},{8,24},{9,... | collective-permute-start | bytes 1462280 | tf_op jit(solution)/shard_map/ppermute | solution.py:197
  66.0 14.9 %collective-permute-start.14 = (bf16[64,1792]{1,0:T(8,128)(2,1)S(1)}, bf16[64,1792]{1,0:T(8,128)(2,1)S(1)}, u32[]{:S(2)}, u32[]{:S(2)}) collective-permute-start(bf16[64,1792]{1,0:T(8,128)(2,1)S(1)} %slice.16), channel_id=1, source_target_pairs={{0,4},{1,5},{2,6},{3,7},{4,8},{5,9},{6,10},{7,11},{8,12},{9,13},{1... | collective-permute-start | bytes 688136 | tf_op jit(solution)/shard_map/ppermute | solution.py:197
  72.3 8.6 %collective-permute-start.13 = (bf16[64,1792]{1,0:T(8,128)(2,1)S(1)}, bf16[64,1792]{1,0:T(8,128)(2,1)S(1)}, u32[]{:S(2)}, u32[]{:S(2)}) collective-permute-start(bf16[64,1792]{1,0:T(8,128)(2,1)S(1)} %slice.12), channel_id=1, source_target_pairs={{0,16},{1,17},{2,18},{3,19},{4,20},{5,21},{6,22},{7,23},{8,24},{9,... | collective-permute-start | bytes 688136 | tf_op jit(solution)/shard_map/ppermute | solution.py:197
  82.7 2.4 %collective-permute-start.15 = (bf16[512,768]{1,0:T(8,128)(2,1)S(1)}, bf16[512,768]{1,0:T(8,128)(2,1)S(1)}, u32[]{:S(2)}, u32[]{:S(2)}) collective-permute-start(bf16[512,768]{1,0:T(8,128)(2,1)S(1)} %get-tuple-element.85), channel_id=1, source_target_pairs={{0,2},{1,3},{2,0},{3,1},{4,6},{5,7},{6,4},{7,5},{8,10},{9,11},{10,... | collective-permute-start | bytes 2359304 | tf_op jit(solution)/shard_map/ppermute | solution.py:197
  82.7 2.3 %collective-permute-start.16 = (f32[8,512]{1,0:T(8,128)S(1)}, f32[8,512]{1,0:T(8,128)S(1)}, u32[]{:S(2)}, u32[]{:S(2)}) collective-permute-start(f32[8,512]{1,0:T(8,128)S(1)} %get-tuple-element.86), channel_id=1, source_target_pairs={{0,2},{1,3},{2,0},{3,1},{4,6},{5,7},{6,4},{7,5},{8,10},{9,11},{10,... | collective-permute-start | bytes 49160 | tf_op jit(solution)/shard_map/ppermute | solution.py:197
  86.8 20.0 %collective-permute-start.20 = (bf16[512,768]{1,0:T(8,128)(2,1)S(1)}, bf16[512,768]{1,0:T(8,128)(2,1)S(1)}, u32[]{:S(2)}, u32[]{:S(2)}) collective-permute-start(bf16[512,768]{1,0:T(8,128)(2,1)S(1)} %get-tuple-element.95), channel_id=1, source_target_pairs={{0,1},{1,0},{2,3},{3,2},{4,5},{5,4},{6,7},{7,6},{8,9},{9,8},{10,11... | collective-permute-start | bytes 2359304 | tf_op jit(solution)/shard_map/ppermute | solution.py:197
  90.2 16.6 %collective-permute-start.17 = (bf16[256,768]{1,0:T(8,128)(2,1)S(1)}, bf16[256,768]{1,0:T(8,128)(2,1)S(1)}, u32[]{:S(2)}, u32[]{:S(2)}) collective-permute-start(bf16[256,768]{1,0:T(8,128)(2,1)S(1)} %get-tuple-element.98), channel_id=1, source_target_pairs={{0,2},{1,3},{2,0},{3,1},{4,6},{5,7},{6,4},{7,5},{8,10},{9,11},{10,... | collective-permute-start | bytes 1179656 | tf_op jit(solution)/shard_map/ppermute | solution.py:197
  90.3 16.5 %collective-permute-start.18 = (bf16[256,768]{1,0:T(8,128)(2,1)S(1)}, bf16[256,768]{1,0:T(8,128)(2,1)S(1)}, u32[]{:S(2)}, u32[]{:S(2)}) collective-permute-start(bf16[256,768]{1,0:T(8,128)(2,1)S(1)} %get-tuple-element.97), channel_id=1, source_target_pairs={{0,2},{1,3},{2,0},{3,1},{4,6},{5,7},{6,4},{7,5},{8,10},{9,11},{10,... | collective-permute-start | bytes 1179656 | tf_op jit(solution)/shard_map/ppermute | solution.py:197
  90.8 2.2 %collective-permute-start.19 = (f32[8,512]{1,0:T(8,128)S(1)}, f32[8,512]{1,0:T(8,128)S(1)}, u32[]{:S(2)}, u32[]{:S(2)}) collective-permute-start(f32[8,512]{1,0:T(8,128)S(1)} %get-tuple-element.94), channel_id=1, source_target_pairs={{0,2},{1,3},{2,0},{3,1},{4,6},{5,7},{6,4},{7,5},{8,10},{9,11},{10,... | collective-permute-start | bytes 49160 | tf_op jit(solution)/shard_map/ppermute | solution.py:197
  90.9 15.9 %collective-permute-start.21 = (f32[8,512]{1,0:T(8,128)S(1)}, f32[8,512]{1,0:T(8,128)S(1)}, u32[]{:S(2)}, u32[]{:S(2)}) collective-permute-start(f32[8,512]{1,0:T(8,128)S(1)} %get-tuple-element.96), channel_id=1, source_target_pairs={{0,1},{1,0},{2,3},{3,2},{4,5},{5,4},{6,7},{7,6},{8,9},{9,8},{10,11... | collective-permute-start | bytes 49160 | tf_op jit(solution)/shard_map/ppermute | solution.py:197
  (3 other events, 9.4 us)

commit v4 on v3

--- a/solution.py
+++ b/solution.py
@@ -14,6 +14,8 @@
 TIES = {("first", 0): 1, ("mid", 1): 1, ("last", 1): 1}
 BIAS_ROWS = 8
 NEAR = 64
+HALVES = 2
+COST_PIECE = 8100000000
 COST_NEXT = 13200000000
 
 
@@ -26,7 +28,7 @@
 
 
 def accumulate(spec, table, bias_ref, *refs):
-    step, pieces, part_rows, sets, first, where, reps, received = spec
+    step, pieces, part_rows, sets, first, where, reps, received, narrow = spec
     count = max(2, len(pieces))
     labels, refs = refs[:count], refs[count:]
     if pieces:
@@ -42,7 +44,7 @@
                 row = lead[lead.shape[0] - BIAS_ROWS :, :part_rows].astype(jnp.float32)[:1]
             else:
                 row = bias_ref[:1, part * part_rows : (part + 1) * part_rows]
-            if where == "all" and offset == 0:
+            if where[0] == "all" and offset == 0:
                 refs[-1][:, part * part_rows : (part + 1) * part_rows] = jnp.broadcast_to(row, (8, part_rows))
             bias_rows.append(row[:, offset : offset + rows])
         bias = joined(bias_rows, 1)
@@ -50,24 +52,26 @@
     else:
         weight_rows, embed_rows, bias = labels[0][...], labels[1][...], bias_ref[...]
     block, rep = table[1 + step], table[table.shape[0] - 1]
-    per_set = 2 + (0 if first else 2) + (2 if received else 0)
+    per_set = 2 + (0 if first else 2) + (1 if received else 0)
+    kind, piece, count = where
+    outs = refs[sets * per_set :]
     for k in range(sets):
         docs_ref, ids_ref, *rest = refs[k * per_set : (k + 1) * per_set]
-        mix_out, sum_out = refs[sets * per_set + 2 * k : sets * per_set + 2 * k + 2]
-        held = docs_ref.shape[0] if where == "all" else docs_ref.shape[0] // reps
-        tile = min(DOC_TILE, held)
-        subs = held // tile
-
-        @pl.loop(0, mix_out.shape[0] // tile)
+        held = docs_ref.shape[0] // (1 if kind == "all" else reps)
+        tile = min(DOC_TILE, held) if kind == "all" else held // count
+        mix_out = outs[k if narrow else 2 * k]
+        spare = sum_rows(reps)
+        stride = tile + spare
+
+        @pl.loop(0, {"all": held // tile, "home": 1, "away": reps - 1}[kind])
         def _(i):
-            if where == "all":
-                source = i
-            elif where == "home":
-                source = rep * subs + i
+            if kind == "all":
+                start = i * tile
+            elif kind == "home":
+                start = rep * held + piece * tile
             else:
-                source = lax.rem(rep + 1 + i // subs, reps) * subs + lax.rem(i, subs)
-            from_rows = pl.ds(pl.multiple_of(source * tile, tile), tile)
-            to_rows = pl.ds(pl.multiple_of(i * tile, tile), tile)
+                start = lax.rem(rep + 1 + i, reps) * held + piece * tile
+            from_rows = pl.ds(pl.multiple_of(start, tile), tile)
             chosen = jnp.max((ids_ref[from_rows, :] == block).astype(jnp.float32), axis=1, keepdims=True)
             logits = lax.dot_general(
                 docs_ref[from_rows, :], weight_rows, (((1,), (1,)), ((), ())), preferred_element_type=jnp.float32
@@ -78,32 +82,58 @@
             if not first:
                 mix = mix + rest[0][from_rows, :]
                 sums = sums + rest[1][from_rows, :]
+            at = pl.multiple_of(i * stride, spare)
             if received:
-                mix = mix + rest[2][to_rows, :].astype(jnp.float32)
-                sums = sums + column(rest[3][:, to_rows])
-            mix_out[to_rows, :] = mix.astype(mix_out.dtype)
-            if sum_out.shape[0] == 8:
-                sum_out[:, to_rows] = jnp.transpose(jnp.broadcast_to(sums, (tile, 128)))[:8]
+                mix = mix + rest[2][pl.ds(at, tile), :].astype(jnp.float32)
+                sums = sums + sums_from(rest[2][pl.ds(at + tile, spare), :], tile)
+            if narrow:
+                mix_out[pl.ds(at, tile), :] = mix.astype(mix_out.dtype)
+                mix_out[pl.ds(at + tile, spare), :] = sums_to(sums, spare, mix_out.shape[1]).astype(mix_out.dtype)
             else:
-                sum_out[to_rows, :] = sums
-
-
-def add_labels(table, bias, labels, sets, *, step, pieces, parts, part_rows, reps, where="all", out=jnp.float32):
+                to_rows = pl.ds(pl.multiple_of(i * tile, tile), tile)
+                mix_out[to_rows, :] = mix
+                outs[2 * k + 1][to_rows, :] = sums
+
+
+def sum_rows(reps):
+    return 8 if reps == 2 else 16
+
+
+def sums_to(sums, spare, width):
+    rows = jnp.transpose(jnp.broadcast_to(sums, (sums.shape[0], 128)))[:spare]
+    high = rows.astype(jnp.bfloat16).astype(jnp.float32)
+    place = lax.broadcasted_iota(jnp.int32, rows.shape, 0)
+    rows = jnp.where(place == 0, high, jnp.where(place == 1, rows - high, 0.0))
+    if rows.shape[1] == width:
+        return rows
+    return jnp.concatenate([rows, jnp.zeros((spare, width - rows.shape[1]), jnp.float32)], axis=1)
+
+
+def sums_from(rows, count):
+    rows = rows.astype(jnp.float32)[:, :count]
+    return column(rows[:1] + rows[1:2])
+
+
+def add_labels(table, bias, labels, sets, *, step, pieces, parts, part_rows, reps, where=("all", 0, 1), narrow=False):
     embed_width = labels[0].shape[1] - sets[0][0].shape[1] if pieces else labels[1].shape[1]
     first, received = len(sets[0]) == 2, len(sets[0]) > 4
-    spec = (step, pieces, part_rows, len(sets), first, where, reps, received)
+    spec = (step, pieces, part_rows, len(sets), first, where, reps, received, narrow)
     operands = [bias, *labels]
     aliases, out_shape = {}, []
+    kind, _, count = where
     for k, one in enumerate(sets):
-        docs = one[0]
-        rows = {"all": docs.shape[0], "home": docs.shape[0] // reps, "away": docs.shape[0] // reps * (reps - 1)}[where]
-        if where == "all" and not first:
+        held = one[0].shape[0] // (1 if kind == "all" else reps)
+        if kind == "all" and not first:
             aliases[1 + len(operands) + 2] = 2 * k
             aliases[1 + len(operands) + 3] = 2 * k + 1
         operands += one
-        out_shape.append(jax.ShapeDtypeStruct((rows, embed_width), out))
-        out_shape.append(jax.ShapeDtypeStruct((rows, 1) if out == jnp.float32 else (8, rows), jnp.float32))
-    if pieces and where == "all":
+        if narrow:
+            rows = (held // count + sum_rows(reps)) * (reps - 1 if kind == "away" else 1)
+            out_shape.append(jax.ShapeDtypeStruct((rows, embed_width), jnp.bfloat16))
+        else:
+            out_shape.append(jax.ShapeDtypeStruct((held, embed_width), jnp.float32))
+            out_shape.append(jax.ShapeDtypeStruct((held, 1), jnp.float32))
+    if pieces and kind == "all":
         out_shape.append(jax.ShapeDtypeStruct((8, parts * part_rows), jnp.float32))
     outs = pl.pallas_call(
         functools.partial(accumulate, spec),
@@ -114,32 +144,50 @@
         compiler_params=pltpu.CompilerParams(vmem_limit_bytes=VMEM_LIMIT),
         cost_estimate=pl.CostEstimate(flops=0, bytes_accessed=0, transcendentals=0),
     )(table, *operands)
+    if narrow:
+        return outs[0]
     totals = [list(outs[2 * k : 2 * k + 2]) for k in range(len(sets))]
     return (totals, outs[-1]) if len(outs) > 2 * len(sets) else totals
 
 
-def combine(mix_ref, sum_ref, *refs):
-    out_ref, others = refs[-1], list(refs[:-1])
-    mix, sums = mix_ref[...], sum_ref[...]
-    while others:
-        parts, rows = [], 0
-        while rows < mix.shape[0]:
-            parts.append(others.pop(0)[...].astype(jnp.float32))
-            rows += parts[-1].shape[0]
-        mix = mix + joined(parts, 0)
-        sums = sums + column(others.pop(0)[...])
-    out_ref[...] = (mix / jnp.sqrt(1.0 + sums)).astype(out_ref.dtype)
-
-
-def combined(mix, sums, others):
-    return pl.pallas_call(
-        combine,
-        in_specs=[pl.BlockSpec(memory_space=pltpu.VMEM)] * (2 + len(others)),
-        out_specs=pl.BlockSpec(memory_space=pltpu.VMEM),
-        out_shape=jax.ShapeDtypeStruct(mix.shape, jnp.bfloat16),
-        compiler_params=pltpu.CompilerParams(vmem_limit_bytes=VMEM_LIMIT),
-        cost_estimate=pl.CostEstimate(flops=0, bytes_accessed=0, transcendentals=0),
-    )(mix, sums, *others)
+def combine(spec, mix_ref, sum_ref, *refs):
+    piece, count, shares = spec
+    out_ref, held, sem = refs[-3:]
+    rows = mix_ref.shape[0] // count
+    where = slice(piece * rows, (piece + 1) * rows)
+    mix, sums = mix_ref[where, :], sum_ref[where, :]
+    for arrays in shares:
+        parts, refs = refs[:arrays], refs[arrays:]
+        left = rows - sum(ref.shape[0] for ref in parts[:-1])
+        mix = mix + joined([ref[...].astype(jnp.float32) for ref in parts[:-1]] + [parts[-1][:left, :].astype(jnp.float32)], 0)
+        sums = sums + sums_from(parts[-1][left:, :], rows)
+    held[...] = (mix / jnp.sqrt(1.0 + sums)).astype(held.dtype)
+    copy = pltpu.make_async_copy(held, out_ref.at[pl.ds(piece * rows, rows), :], sem)
+    copy.start()
+    copy.wait()
+
+
+def combined(mix, sums, shares):
+    count, out = len(shares), None
+    for piece in range(count):
+        operands = [mix, sums, *sum(shares[piece], [])]
+        in_specs = [pl.BlockSpec(memory_space=pltpu.VMEM)] * len(operands)
+        aliases = {}
+        if out is not None:
+            operands.append(out)
+            in_specs.append(pl.BlockSpec(memory_space=pl.ANY))
+            aliases = {len(operands) - 1: 0}
+        out = pl.pallas_call(
+            functools.partial(combine, (piece, count, tuple(len(arrays) for arrays in shares[piece]))),
+            in_specs=in_specs,
+            out_specs=pl.BlockSpec(memory_space=pl.ANY),
+            out_shape=jax.ShapeDtypeStruct(mix.shape, jnp.bfloat16),
+            input_output_aliases=aliases,
+            scratch_shapes=[pltpu.VMEM((mix.shape[0] // count, mix.shape[1]), jnp.bfloat16), pltpu.SemaphoreType.DMA(())],
+            compiler_params=pltpu.CompilerParams(vmem_limit_bytes=VMEM_LIMIT),
+            cost_estimate=pl.CostEstimate(flops=COST_PIECE, bytes_accessed=0, transcendentals=0),
+        )(*operands)
+    return out
 
 
 def pack(spec, table, weight, embed, bias, out, sems):
@@ -255,24 +303,28 @@
     here = dict(step=chips - 1, pieces=tuple(place for place, _ in arrived[final]), **common)
     call = functools.partial(call, bias)
 
-    narrow = dict(out=jnp.bfloat16, **here)
     tile_docs = doc_count // reps
-    others = []
-    away = [held[0]]
+    halves = HALVES if tile_docs // HALVES >= 128 else 1
+    given = [None] * halves
     if cores == 2:
-        (share,) = call(labels, [held[1]], where="away", **narrow)
-        away = [held[0] + [other_core(x) for x in share]]
-    (away,) = call(labels, away, where="away", **narrow)
+        for h in range(halves):
+            given[h] = other_core(call(labels, [held[1]], where=("away", h, halves), narrow=True, **here))
+    shares = []
+    for h in range(halves):
+        one = held[0] + ([given[h]] if cores == 2 else [])
+        share = call(labels, [one], where=("away", h, halves), narrow=True, **here)
+        stride = share.shape[0] // (reps - 1)
+        if h == 0:
+            lead = share
+        shares.append([[other_rep(share if reps == 2 else share[k * stride - stride : k * stride], k)] for k in range(1, reps)])
     if cores == 2:
-        away, held[1] = lax.optimization_barrier((away, held[1]))
-        (share,) = call(labels, [held[1]], where="home", **narrow)
-        half = tile_docs // 2
-        others += [other_core(share[0][:half]), other_core(share[0][half:]), other_core(share[1])]
-    ((home_mix, home_sum),) = call(labels, [held[0]], where="home", **here)
-    for k in range(1, reps):
-        part = slice((k - 1) * tile_docs, k * tile_docs)
-        others += [other_rep(away[0][part], k), other_rep(away[1][:, part], k)]
-    return combined(home_mix, home_sum, others)
+        lead, held[1] = lax.optimization_barrier((lead, held[1]))
+        for h in range(halves):
+            share = call(labels, [held[1]], where=("home", h, halves), narrow=True, **here)
+            cut = tile_docs // halves // 2
+            shares[h].append([other_core(share[:cut]), other_core(share[cut:])])
+    ((home_mix, home_sum),) = call(labels, [held[0]], where=("home", 0, 1), **here)
+    return combined(home_mix, home_sum, shares)
 
 
 def solution(mesh):

time: 108 us -> 107 us (level)
  waiting for transfers between devices: 50.2 us -> 44.6 us
  Pallas kernels: 34.5 us -> 37.6 us
    ppermute x22 -> x23, waiting for transfers between devices: 50.2 us -> 44.6 us  [moved(): return lax.ppermute(x, AXES, pairs)]
    pallas_call x8 -> x11, Pallas kernels: 28.3 us -> 30.8 us  [add_labels(): pl.pallas_call(functools.partial(accumulate, spec), in_specs=[pl.BlockSpe...]
    ppermute x22 -> x23, starting transfers between devices: 19.5 us -> 20.2 us  [moved(): return lax.ppermute(x, AXES, pairs)]
  transfers between devices with their start and end apart: 22 -> 23, of which waited for: 10 -> 10; matrix products, arithmetic and copies ran while one was open for 1% -> 1% of each run, Pallas kernels for 27% -> 33%
where the time goes in v4:
time: 107 us
  waiting for transfers between devices  44.6 us (42%)
  Pallas kernels  37.6 us (35%)
  starting transfers between devices  20.2 us (19%)
  local copies, waits for them, and re-layouts  3.23 us (3%)
    ppermute x23, waiting for transfers between devices, moved(): return lax.ppermute(x, AXES, pairs)  44.6 us
    pallas_call x11, Pallas kernels, add_labels(): pl.pallas_call(functools.partial(accumulate, spec), in_specs=[pl.BlockSpe...  30.8 us
    ppermute x23, starting transfers between devices, moved(): return lax.ppermute(x, AXES, pairs)  20.2 us
    pallas_call x2, Pallas kernels, packed_part(): pl.pallas_call(functools.partial(pack, (offset, rows, part_rows, groups))...  4.68 us
    unnamed x11, local copies, waits for them, and re-layouts  3.05 us
  transfers between devices with their start and end apart: 23, of which 10 were waited for; matrix products, arithmetic and copies ran while one was open for 1% of the time, Pallas kernels for 33%

profile of v4, /device:TPU:0, one launch (start us, length us, event | category | flops | bytes accessed | tf_op | source)
XLA Modules:
  0.0 106.7 jit_solution(683704977057281929)
XLA Ops:
  1.2 2.3 %shard_map.55 = bf16[136,1792]{1,0:T(8,128)(2,1)} custom-call(s32[6]{0:T(128)S(1)} %stack.27.table, bf16[512,1024]{1,0:T(8,128)(2,1)} %weight.3, bf16[512,768]{1,0:T(8,128)(2,1)} %embed.3, f32[1,512]{1,0:T(1,128)S(1)} %bitcast.7), custom_call_target="tpu_custom_call" | custom-call | tf_op jit(solution)/shard_map/pallas_call | solution.py:216
  3.6 2.6 %collective-permute-start = (bf16[136,1792]{1,0:T(8,128)(2,1)}, bf16[136,1792]{1,0:T(8,128)(2,1)}, u32[]{:S(2)}, u32[]{:S(2)}) collective-permute-start(bf16[136,1792]{1,0:T(8,128)(2,1)} %shard_map.55), channel_id=1, source_target_pairs={{0,4},{1,5},{2,6},{3,7},{4,8},{5,9},{6,10},{7,11},{8,12},{9,13},{1... | collective-permute-start | bytes 1462280 | tf_op jit(solution)/shard_map/ppermute | solution.py:245
  6.2 2.3 %shard_map.57 = bf16[128,1792]{1,0:T(8,128)(2,1)} custom-call(s32[6]{0:T(128)S(1)} %stack.27.table, bf16[512,1024]{1,0:T(8,128)(2,1)} %weight.3, bf16[512,768]{1,0:T(8,128)(2,1)} %embed.3, f32[1,512]{1,0:T(1,128)S(1)} %bitcast.8), custom_call_target="tpu_custom_call" | custom-call | flops 13200000000 | tf_op jit(solution)/shard_map/pallas_call | solution.py:216
  8.6 1.6 %collective-permute-start.6 = (bf16[128,1792]{1,0:T(8,128)(2,1)}, bf16[128,1792]{1,0:T(8,128)(2,1)}, u32[]{:S(2)}, u32[]{:S(2)}) collective-permute-start(bf16[128,1792]{1,0:T(8,128)(2,1)} %shard_map.57), channel_id=1, source_target_pairs={{0,4},{1,5},{2,6},{3,7},{4,8},{5,9},{6,10},{7,11},{8,12},{9,13},{1... | collective-permute-start | bytes 1376264 | tf_op jit(solution)/shard_map/ppermute | solution.py:245
  10.5 1.9 %collective-permute-done.2.refs_5_.refs_9_.refs_7_.refs_4_ = s32[1024,3]{1,0:T(8,128)S(1)} collective-permute-done((s32[1024,3]{1,0:T(8,128)S(1)}, s32[1024,3]{1,0:T(8,128)S(1)}, u32[]{:S(2)}, u32[]{:S(2)}) %collective-permute-start.2) | collective-permute-done | bytes 12320 | tf_op jit(solution)/shard_map/ppermute | solution.py:245
  12.4 1.6 %copy-done = bf16[1024,1024]{1,0:T(8,128)(2,1)S(1)} copy-done((bf16[1024,1024]{1,0:T(8,128)(2,1)S(1)}, bf16[1024,1024]{1,0:T(8,128)(2,1)}, u32[]{:S(2)}) %copy-start) | copy-done | bytes 2097176
  15.2 4.8 %shard_map.56 = (f32[1024,768]{1,0:T(8,128)S(1)}, f32[1024,1]{1,0:T(8,128)S(1)}, f32[1024,768]{1,0:T(8,128)S(1)}, f32[1024,1]{1,0:T(8,128)S(1)}) custom-call(s32[6]{0:T(128)S(1)} %stack.27.table, f32[1,512]{1,0:T(1,128)S(1)} %bitcast.9, bf16[512,1024]{1,0:T(8,128)(2,1)S(1)} %copy-done.2, bf16[512,768]{1,0:T(8,128)(2,1)S(1)} %copy-done.3, ...), custom_call_target="tpu_custom_call" | custom-call | tf_op jit(solution)/shard_map/pallas_call | solution.py:138
  23.2 7.2 %collective-permute-done.6.refs_2_ = bf16[128,1792]{1,0:T(8,128)(2,1)} collective-permute-done((bf16[128,1792]{1,0:T(8,128)(2,1)}, bf16[128,1792]{1,0:T(8,128)(2,1)}, u32[]{:S(2)}, u32[]{:S(2)}) %collective-permute-start.6) | collective-permute-done | bytes 458784 | tf_op jit(solution)/shard_map/ppermute | solution.py:245
  30.4 1.6 %collective-permute-start.9 = (bf16[128,1792]{1,0:T(8,128)(2,1)}, bf16[128,1792]{1,0:T(8,128)(2,1)S(1)}, u32[]{:S(2)}, u32[]{:S(2)}) collective-permute-start(bf16[128,1792]{1,0:T(8,128)(2,1)} %collective-permute-done.6.refs_2_), channel_id=1, source_target_pairs={{0,16},{1,17},{2,18},{3,19},{4,20},{5,21},{6,22},{7,23},{8,24},{9,... | collective-permute-start | bytes 1376264 | tf_op jit(solution)/shard_map/ppermute | solution.py:245
  32.0 8.7 %collective-permute-done.3.refs_0_ = bf16[136,1792]{1,0:T(8,128)(2,1)S(1)} collective-permute-done((bf16[136,1792]{1,0:T(8,128)(2,1)}, bf16[136,1792]{1,0:T(8,128)(2,1)S(1)}, u32[]{:S(2)}, u32[]{:S(2)}) %collective-permute-start.3) | collective-permute-done | bytes 487456 | tf_op jit(solution)/shard_map/ppermute | solution.py:245
  40.7 1.6 %collective-permute-start.11 = (bf16[136,1792]{1,0:T(8,128)(2,1)S(1)}, bf16[136,1792]{1,0:T(8,128)(2,1)S(1)}, u32[]{:S(2)}, u32[]{:S(2)}) collective-permute-start(bf16[136,1792]{1,0:T(8,128)(2,1)S(1)} %collective-permute-done.3.refs_0_), channel_id=1, source_target_pairs={{0,16},{1,17},{2,18},{3,19},{4,20},{5,21},{6,22},{7,23},{8,24},{9,... | collective-permute-start | bytes 1462280 | tf_op jit(solution)/shard_map/ppermute | solution.py:245
  42.4 3.4 %collective-permute-done.9.refs_3_ = bf16[128,1792]{1,0:T(8,128)(2,1)S(1)} collective-permute-done((bf16[128,1792]{1,0:T(8,128)(2,1)}, bf16[128,1792]{1,0:T(8,128)(2,1)S(1)}, u32[]{:S(2)}, u32[]{:S(2)}) %collective-permute-start.9) | collective-permute-done | bytes 458784 | tf_op jit(solution)/shard_map/ppermute | solution.py:245
  45.7 6.4 %shard_map.58 = (f32[1024,768]{1,0:T(8,128)S(1)}, f32[1024,1]{1,0:T(8,128)S(1)}, f32[1024,768]{1,0:T(8,128)S(1)}, f32[1024,1]{1,0:T(8,128)S(1)}, f32[8,512]{1,0:T(8,128)}) custom-call(s32[6]{0:T(128)S(1)} %stack.27.table, f32[1,512]{1,0:T(1,128)S(1)} %bitcast.10, ...), custom_call_target="tpu_custom_call", output_to_operand_aliasing={{0}: (8, {}), {1}: (9, {}), {2}: (12, {}), {3}: (13, {})} | custom-call | tf_op jit(solution)/shard_map/pallas_call | solution.py:138
  54.0 7.0 %collective-permute-done.4.refs_0_ = bf16[136,1792]{1,0:T(8,128)(2,1)S(1)} collective-permute-done((bf16[136,1792]{1,0:T(8,128)(2,1)S(1)}, bf16[136,1792]{1,0:T(8,128)(2,1)S(1)}, u32[]{:S(2)}, u32[]{:S(2)}) %collective-permute-start.4) | collective-permute-done | bytes 487456 | tf_op jit(solution)/shard_map/ppermute | solution.py:245
  61.0 1.6 %collective-permute-start.5 = (bf16[136,1792]{1,0:T(8,128)(2,1)S(1)}, bf16[136,1792]{1,0:T(8,128)(2,1)S(1)}, u32[]{:S(2)}, u32[]{:S(2)}) collective-permute-start(bf16[136,1792]{1,0:T(8,128)(2,1)S(1)} %collective-permute-done.4.refs_0_), channel_id=1, source_target_pairs={{0,16},{1,17},{2,18},{3,19},{4,20},{5,21},{6,22},{7,23},{8,24},{9,... | collective-permute-start | bytes 1462280 | tf_op jit(solution)/shard_map/ppermute | solution.py:245
  62.6 3.4 %collective-permute-done.12.refs_3_ = bf16[128,1792]{1,0:T(8,128)(2,1)S(1)} collective-permute-done((bf16[128,1792]{1,0:T(8,128)(2,1)S(1)}, bf16[128,1792]{1,0:T(8,128)(2,1)S(1)}, u32[]{:S(2)}, u32[]{:S(2)}) %collective-permute-start.12) | collective-permute-done | bytes 458784 | tf_op jit(solution)/shard_map/ppermute | solution.py:245
  66.6 5.8 %shard_map.59 = (f32[1024,768]{1,0:T(8,128)S(1)}, f32[1024,1]{1,0:T(8,128)S(1)}, f32[1024,768]{1,0:T(8,128)S(1)}, f32[1024,1]{1,0:T(8,128)S(1)}, f32[8,512]{1,0:T(8,128)}) custom-call(s32[6]{0:T(128)S(1)} %stack.27.table, f32[1,512]{1,0:T(1,128)S(1)} %bitcast.11, ...), custom_call_target="tpu_custom_call", output_to_operand_aliasing={{0}: (8, {}), {1}: (9, {}), {2}: (12, {}), {3}: (13, {})} | custom-call | tf_op jit(solution)/shard_map/pallas_call | solution.py:138
  72.3 1.6 %collective-permute-start.13 = (bf16[64,1792]{1,0:T(8,128)(2,1)S(1)}, bf16[64,1792]{1,0:T(8,128)(2,1)S(1)}, u32[]{:S(2)}, u32[]{:S(2)}) collective-permute-start(bf16[64,1792]{1,0:T(8,128)(2,1)S(1)} %slice.18), channel_id=1, source_target_pairs={{0,16},{1,17},{2,18},{3,19},{4,20},{5,21},{6,22},{7,23},{8,24},{9,... | collective-permute-start | bytes 688136 | tf_op jit(solution)/shard_map/ppermute | solution.py:245
  73.9 2.5 %collective-permute-done.5.refs_1_ = bf16[136,1792]{1,0:T(8,128)(2,1)S(1)} collective-permute-done((bf16[136,1792]{1,0:T(8,128)(2,1)S(1)}, bf16[136,1792]{1,0:T(8,128)(2,1)S(1)}, u32[]{:S(2)}, u32[]{:S(2)}) %collective-permute-start.5) | collective-permute-done | bytes 487456 | tf_op jit(solution)/shard_map/ppermute | solution.py:245
  76.5 4.4 %shard_map.60 = (f32[1024,768]{1,0:T(8,128)S(1)}, f32[1024,1]{1,0:T(8,128)S(1)}, f32[1024,768]{1,0:T(8,128)S(1)}, f32[1024,1]{1,0:T(8,128)S(1)}, f32[8,512]{1,0:T(8,128)S(1)}) custom-call(s32[6]{0:T(128)S(1)} %stack.27.table, f32[1,512]{1,0:T(1,128)S(1)} %bitcast.12, ...), custom_call_target="tpu_custom_call", output_to_operand_aliasing={{0}: (6, {}), {1}: (7, {}), {2}: (10, {}), {3}: (11, {})} | custom-call | tf_op jit(solution)/shard_map/pallas_call | solution.py:138
  85.4 1.6 %collective-permute-start.20 = (bf16[264,768]{1,0:T(8,128)(2,1)S(1)}, bf16[264,768]{1,0:T(8,128)(2,1)S(1)}, u32[]{:S(2)}, u32[]{:S(2)}) collective-permute-start(bf16[264,768]{1,0:T(8,128)(2,1)S(1)} %shard_map.65), channel_id=1, source_target_pairs={{0,1},{1,0},{2,3},{3,2},{4,5},{5,4},{6,7},{7,6},{8,9},{9,8},{10,11... | collective-permute-start | bytes 1216520 | tf_op jit(solution)/shard_map/ppermute | solution.py:245
  89.0 1.6 %shard_map.61 = (f32[512,768]{1,0:T(8,128)S(1)}, f32[512,1]{1,0:T(8,128)S(1)}) custom-call(s32[6]{0:T(128)S(1)} %stack.27.table, f32[8,512]{1,0:T(8,128)S(1)} %get-tuple-element.69.bias_ref, bf16[128,1792]{1,0:T(8,128)(2,1)S(1)} %collective-permute-done.10.refs_0_, bf16[64,1792]{1,0:T(8,128)(2,1)S(1)} %collective-permute-done.13.refs_1_, ...), custom_call_target="tpu_custom_call" | custom-call | tf_op jit(solution)/shard_map/pallas_call | solution.py:138
  94.4 2.6 %collective-permute-done.20.refs_0_ = bf16[264,768]{1,0:T(8,128)(2,1)S(1)} collective-permute-done((bf16[264,768]{1,0:T(8,128)(2,1)S(1)}, bf16[264,768]{1,0:T(8,128)(2,1)S(1)}, u32[]{:S(2)}, u32[]{:S(2)}) %collective-permute-start.20) | collective-permute-done | bytes 405536 | tf_op jit(solution)/shard_map/ppermute | solution.py:245
  98.1 7.4 %collective-permute-done.16.refs_0_ = bf16[264,768]{1,0:T(8,128)(2,1)S(1)} collective-permute-done((bf16[264,768]{1,0:T(8,128)(2,1)S(1)}, bf16[264,768]{1,0:T(8,128)(2,1)S(1)}, u32[]{:S(2)}, u32[]{:S(2)}) %collective-permute-start.16) | collective-permute-done | bytes 405536 | tf_op jit(solution)/shard_map/ppermute | solution.py:245
  (56 shorter events, 20.7 us)
Async XLA Ops:
  0.0 12.4 %collective-permute-start.1 = (bf16[1024,1024]{1,0:T(8,128)(2,1)}, bf16[1024,1024]{1,0:T(8,128)(2,1)S(1)}, u32[]{:S(2)}, u32[]{:S(2)}) collective-permute-start(bf16[1024,1024]{1,0:T(8,128)(2,1)} %refs_3_.7), channel_id=1, source_target_pairs={{0,2},{1,3},{2,0},{3,1},{4,6},{5,7},{6,4},{7,5},{8,10},{9,11},{10,... | collective-permute-start | bytes 6291464 | tf_op jit(solution)/shard_map/ppermute | solution.py:245
  3.6 17.0 %collective-permute-start = (bf16[136,1792]{1,0:T(8,128)(2,1)}, bf16[136,1792]{1,0:T(8,128)(2,1)}, u32[]{:S(2)}, u32[]{:S(2)}) collective-permute-start(bf16[136,1792]{1,0:T(8,128)(2,1)} %shard_map.55), channel_id=1, source_target_pairs={{0,4},{1,5},{2,6},{3,7},{4,8},{5,9},{6,10},{7,11},{8,12},{9,13},{1... | collective-permute-start | bytes 1462280 | tf_op jit(solution)/shard_map/ppermute | solution.py:245
  8.6 21.8 %collective-permute-start.6 = (bf16[128,1792]{1,0:T(8,128)(2,1)}, bf16[128,1792]{1,0:T(8,128)(2,1)}, u32[]{:S(2)}, u32[]{:S(2)}) collective-permute-start(bf16[128,1792]{1,0:T(8,128)(2,1)} %shard_map.57), channel_id=1, source_target_pairs={{0,4},{1,5},{2,6},{3,7},{4,8},{5,9},{6,10},{7,11},{8,12},{9,13},{1... | collective-permute-start | bytes 1376264 | tf_op jit(solution)/shard_map/ppermute | solution.py:245
  10.4 2.0 %collective-permute-start.2 = (s32[1024,3]{1,0:T(8,128)S(1)}, s32[1024,3]{1,0:T(8,128)S(1)}, u32[]{:S(2)}, u32[]{:S(2)}) collective-permute-start(s32[1024,3]{1,0:T(8,128)S(1)} %copy.20.refs_3_.refs_5_.refs_4_), channel_id=1, source_target_pairs={{0,2},{1,3},{2,0},{3,1},{4,6},{5,7},{6,4},{7,5},{8,10},{9,11},{10,... | collective-permute-start | bytes 36872 | tf_op jit(solution)/shard_map/ppermute | solution.py:245
  15.2 30.5 %copy-start.1 = (bf16[1024,1024]{1,0:T(8,128)(2,1)S(1)}, bf16[1024,1024]{1,0:T(8,128)(2,1)}, u32[]{:S(2)}) copy-start(bf16[1024,1024]{1,0:T(8,128)(2,1)} %refs_3_.7) | copy-start | bytes 6291460
  20.6 20.2 %collective-permute-start.3 = (bf16[136,1792]{1,0:T(8,128)(2,1)}, bf16[136,1792]{1,0:T(8,128)(2,1)S(1)}, u32[]{:S(2)}, u32[]{:S(2)}) collective-permute-start(bf16[136,1792]{1,0:T(8,128)(2,1)} %collective-permute-done.refs_0_), channel_id=1, source_target_pairs={{0,4},{1,5},{2,6},{3,7},{4,8},{5,9},{6,10},{7,11},{8,12},{9,13},{1... | collective-permute-start | bytes 1462280 | tf_op jit(solution)/shard_map/ppermute | solution.py:245
  21.7 24.1 %collective-permute-start.8 = (bf16[136,1792]{1,0:T(8,128)(2,1)}, bf16[136,1792]{1,0:T(8,128)(2,1)S(1)}, u32[]{:S(2)}, u32[]{:S(2)}) collective-permute-start(bf16[136,1792]{1,0:T(8,128)(2,1)} %collective-permute-done.refs_0_), channel_id=1, source_target_pairs={{0,16},{1,17},{2,18},{3,19},{4,20},{5,21},{6,22},{7,23},{8,24},{9,... | collective-permute-start | bytes 1462280 | tf_op jit(solution)/shard_map/ppermute | solution.py:245
  30.4 15.4 %collective-permute-start.9 = (bf16[128,1792]{1,0:T(8,128)(2,1)}, bf16[128,1792]{1,0:T(8,128)(2,1)S(1)}, u32[]{:S(2)}, u32[]{:S(2)}) collective-permute-start(bf16[128,1792]{1,0:T(8,128)(2,1)} %collective-permute-done.6.refs_2_), channel_id=1, source_target_pairs={{0,16},{1,17},{2,18},{3,19},{4,20},{5,21},{6,22},{7,23},{8,24},{9,... | collective-permute-start | bytes 1376264 | tf_op jit(solution)/shard_map/ppermute | solution.py:245
  32.0 20.1 %collective-permute-start.7 = (bf16[128,1792]{1,0:T(8,128)(2,1)}, bf16[128,1792]{1,0:T(8,128)(2,1)S(1)}, u32[]{:S(2)}, u32[]{:S(2)}) collective-permute-start(bf16[128,1792]{1,0:T(8,128)(2,1)} %collective-permute-done.6.refs_2_), channel_id=1, source_target_pairs={{0,4},{1,5},{2,6},{3,7},{4,8},{5,9},{6,10},{7,11},{8,12},{9,13},{1... | collective-permute-start | bytes 1376264 | tf_op jit(solution)/shard_map/ppermute | solution.py:245
  40.7 20.3 %collective-permute-start.4 = (bf16[136,1792]{1,0:T(8,128)(2,1)S(1)}, bf16[136,1792]{1,0:T(8,128)(2,1)S(1)}, u32[]{:S(2)}, u32[]{:S(2)}) collective-permute-start(bf16[136,1792]{1,0:T(8,128)(2,1)S(1)} %collective-permute-done.3.refs_0_), channel_id=1, source_target_pairs={{0,4},{1,5},{2,6},{3,7},{4,8},{5,9},{6,10},{7,11},{8,12},{9,13},{1... | collective-permute-start | bytes 1462280 | tf_op jit(solution)/shard_map/ppermute | solution.py:245
  40.7 25.8 %collective-permute-start.11 = (bf16[136,1792]{1,0:T(8,128)(2,1)S(1)}, bf16[136,1792]{1,0:T(8,128)(2,1)S(1)}, u32[]{:S(2)}, u32[]{:S(2)}) collective-permute-start(bf16[136,1792]{1,0:T(8,128)(2,1)S(1)} %collective-permute-done.3.refs_0_), channel_id=1, source_target_pairs={{0,16},{1,17},{2,18},{3,19},{4,20},{5,21},{6,22},{7,23},{8,24},{9,... | collective-permute-start | bytes 1462280 | tf_op jit(solution)/shard_map/ppermute | solution.py:245
  52.2 13.9 %collective-permute-start.12 = (bf16[128,1792]{1,0:T(8,128)(2,1)S(1)}, bf16[128,1792]{1,0:T(8,128)(2,1)S(1)}, u32[]{:S(2)}, u32[]{:S(2)}) collective-permute-start(bf16[128,1792]{1,0:T(8,128)(2,1)S(1)} %collective-permute-done.7.refs_2_), channel_id=1, source_target_pairs={{0,16},{1,17},{2,18},{3,19},{4,20},{5,21},{6,22},{7,23},{8,24},{9,... | collective-permute-start | bytes 1376264 | tf_op jit(solution)/shard_map/ppermute | solution.py:245
  53.7 18.7 %collective-permute-start.10 = (bf16[128,1792]{1,0:T(8,128)(2,1)S(1)}, bf16[128,1792]{1,0:T(8,128)(2,1)S(1)}, u32[]{:S(2)}, u32[]{:S(2)}) collective-permute-start(bf16[128,1792]{1,0:T(8,128)(2,1)S(1)} %collective-permute-done.7.refs_2_), channel_id=1, source_target_pairs={{0,4},{1,5},{2,6},{3,7},{4,8},{5,9},{6,10},{7,11},{8,12},{9,13},{1... | collective-permute-start | bytes 1376264 | tf_op jit(solution)/shard_map/ppermute | solution.py:245
  61.0 15.5 %collective-permute-start.5 = (bf16[136,1792]{1,0:T(8,128)(2,1)S(1)}, bf16[136,1792]{1,0:T(8,128)(2,1)S(1)}, u32[]{:S(2)}, u32[]{:S(2)}) collective-permute-start(bf16[136,1792]{1,0:T(8,128)(2,1)S(1)} %collective-permute-done.4.refs_0_), channel_id=1, source_target_pairs={{0,16},{1,17},{2,18},{3,19},{4,20},{5,21},{6,22},{7,23},{8,24},{9,... | collective-permute-start | bytes 1462280 | tf_op jit(solution)/shard_map/ppermute | solution.py:245
  66.0 14.9 %collective-permute-start.14 = (bf16[64,1792]{1,0:T(8,128)(2,1)S(1)}, bf16[64,1792]{1,0:T(8,128)(2,1)S(1)}, u32[]{:S(2)}, u32[]{:S(2)}) collective-permute-start(bf16[64,1792]{1,0:T(8,128)(2,1)S(1)} %slice.24), channel_id=1, source_target_pairs={{0,4},{1,5},{2,6},{3,7},{4,8},{5,9},{6,10},{7,11},{8,12},{9,13},{1... | collective-permute-start | bytes 688136 | tf_op jit(solution)/shard_map/ppermute | solution.py:245
  72.3 8.6 %collective-permute-start.13 = (bf16[64,1792]{1,0:T(8,128)(2,1)S(1)}, bf16[64,1792]{1,0:T(8,128)(2,1)S(1)}, u32[]{:S(2)}, u32[]{:S(2)}) collective-permute-start(bf16[64,1792]{1,0:T(8,128)(2,1)S(1)} %slice.18), channel_id=1, source_target_pairs={{0,16},{1,17},{2,18},{3,19},{4,20},{5,21},{6,22},{7,23},{8,24},{9,... | collective-permute-start | bytes 688136 | tf_op jit(solution)/shard_map/ppermute | solution.py:245
  82.2 1.9 %collective-permute-start.17 = (bf16[264,768]{1,0:T(8,128)(2,1)S(1)}, bf16[264,768]{1,0:T(8,128)(2,1)S(1)}, u32[]{:S(2)}, u32[]{:S(2)}) collective-permute-start(bf16[264,768]{1,0:T(8,128)(2,1)S(1)} %shard_map.64), channel_id=1, source_target_pairs={{0,2},{1,3},{2,0},{3,1},{4,6},{5,7},{6,4},{7,5},{8,10},{9,11},{10,... | collective-permute-start | bytes 1216520 | tf_op jit(solution)/shard_map/ppermute | solution.py:245
  83.6 8.4 %collective-permute-start.15 = (bf16[264,768]{1,0:T(8,128)(2,1)S(1)}, bf16[264,768]{1,0:T(8,128)(2,1)S(1)}, u32[]{:S(2)}, u32[]{:S(2)}) collective-permute-start(bf16[264,768]{1,0:T(8,128)(2,1)S(1)} %shard_map.62), channel_id=1, source_target_pairs={{0,2},{1,3},{2,0},{3,1},{4,6},{5,7},{6,4},{7,5},{8,10},{9,11},{10,... | collective-permute-start | bytes 1216520 | tf_op jit(solution)/shard_map/ppermute | solution.py:245
  85.4 11.6 %collective-permute-start.20 = (bf16[264,768]{1,0:T(8,128)(2,1)S(1)}, bf16[264,768]{1,0:T(8,128)(2,1)S(1)}, u32[]{:S(2)}, u32[]{:S(2)}) collective-permute-start(bf16[264,768]{1,0:T(8,128)(2,1)S(1)} %shard_map.65), channel_id=1, source_target_pairs={{0,1},{1,0},{2,3},{3,2},{4,5},{5,4},{6,7},{7,6},{8,9},{9,8},{10,11... | collective-permute-start | bytes 1216520 | tf_op jit(solution)/shard_map/ppermute | solution.py:245
  88.3 6.1 %collective-permute-start.22 = (bf16[136,768]{1,0:T(8,128)(2,1)S(1)}, bf16[136,768]{1,0:T(8,128)(2,1)S(1)}, u32[]{:S(2)}, u32[]{:S(2)}) collective-permute-start(bf16[136,768]{1,0:T(8,128)(2,1)S(1)} %slice.28), channel_id=1, source_target_pairs={{0,2},{1,3},{2,0},{3,1},{4,6},{5,7},{6,4},{7,5},{8,10},{9,11},{10,... | collective-permute-start | bytes 626696 | tf_op jit(solution)/shard_map/ppermute | solution.py:245
  88.4 5.4 %collective-permute-start.21 = (bf16[128,768]{1,0:T(8,128)(2,1)S(1)}, bf16[128,768]{1,0:T(8,128)(2,1)S(1)}, u32[]{:S(2)}, u32[]{:S(2)}) collective-permute-start(bf16[128,768]{1,0:T(8,128)(2,1)S(1)} %slice.27), channel_id=1, source_target_pairs={{0,2},{1,3},{2,0},{3,1},{4,6},{5,7},{6,4},{7,5},{8,10},{9,11},{10,... | collective-permute-start | bytes 589832 | tf_op jit(solution)/shard_map/ppermute | solution.py:245
  91.9 6.2 %collective-permute-start.19 = (bf16[136,768]{1,0:T(8,128)(2,1)S(1)}, bf16[136,768]{1,0:T(8,128)(2,1)S(1)}, u32[]{:S(2)}, u32[]{:S(2)}) collective-permute-start(bf16[136,768]{1,0:T(8,128)(2,1)S(1)} %slice.26), channel_id=1, source_target_pairs={{0,2},{1,3},{2,0},{3,1},{4,6},{5,7},{6,4},{7,5},{8,10},{9,11},{10,... | collective-permute-start | bytes 626696 | tf_op jit(solution)/shard_map/ppermute | solution.py:245
  92.0 6.1 %collective-permute-start.18 = (bf16[128,768]{1,0:T(8,128)(2,1)S(1)}, bf16[128,768]{1,0:T(8,128)(2,1)S(1)}, u32[]{:S(2)}, u32[]{:S(2)}) collective-permute-start(bf16[128,768]{1,0:T(8,128)(2,1)S(1)} %slice.25), channel_id=1, source_target_pairs={{0,2},{1,3},{2,0},{3,1},{4,6},{5,7},{6,4},{7,5},{8,10},{9,11},{10,... | collective-permute-start | bytes 589832 | tf_op jit(solution)/shard_map/ppermute | solution.py:245
  93.8 11.7 %collective-permute-start.16 = (bf16[264,768]{1,0:T(8,128)(2,1)S(1)}, bf16[264,768]{1,0:T(8,128)(2,1)S(1)}, u32[]{:S(2)}, u32[]{:S(2)}) collective-permute-start(bf16[264,768]{1,0:T(8,128)(2,1)S(1)} %shard_map.63), channel_id=1, source_target_pairs={{0,1},{1,0},{2,3},{3,2},{4,5},{5,4},{6,7},{7,6},{8,9},{9,8},{10,11... | collective-permute-start | bytes 1216520 | tf_op jit(solution)/shard_map/ppermute | solution.py:245
  (4 other events, 18.3 us)

commit v5 on v4

--- a/solution.py
+++ b/solution.py
@@ -50,7 +50,7 @@
         bias = joined(bias_rows, 1)
         weight_rows, embed_rows = joined(weight_rows, 0), joined(embed_rows, 0)
     else:
-        weight_rows, embed_rows, bias = labels[0][...], labels[1][...], bias_ref[...]
+        weight_rows, embed_rows, bias = labels[0][...], labels[1][...], bias_ref[...].astype(jnp.float32)
     block, rep = table[1 + step], table[table.shape[0] - 1]
     per_set = 2 + (0 if first else 2) + (1 if received else 0)
     kind, piece, count = where
@@ -202,9 +202,10 @@
     for copy in copies:
         copy.start()
     if offset == 0:
-        row = bias[:, :part_rows]
+        every = bias[...].astype(jnp.float32)
+        row = every[:, :part_rows]
         for other in range(1, groups):
-            row = jnp.where(group == other, bias[:, other * part_rows : (other + 1) * part_rows], row)
+            row = jnp.where(group == other, every[:, other * part_rows : (other + 1) * part_rows], row)
         out[rows:, :part_rows] = jnp.broadcast_to(row, (BIAS_ROWS, part_rows)).astype(out.dtype)
         out[rows:, part_rows:] = jnp.zeros((BIAS_ROWS, out.shape[1] - part_rows), out.dtype)
     for copy in copies:
@@ -259,14 +260,26 @@
     total = sum(SHARES)
     cuts = [part_rows * sum(SHARES[:k]) // total // 16 * 16 for k in range(len(SHARES))] + [part_rows]
     chunks = [(a, b - a) for a, b in zip(cuts, cuts[1:])]
-    bias = label_bias.astype(jnp.float32)[None, :]
+    bias = label_bias[None, :]
+    sets = [[documents, block_ids]]
+    later = table
+    if cores == 2:
+        sets.append([other_core(documents), other_core(block_ids)])
+        later, sets[1][1] = lax.optimization_barrier((table, sets[1][1]))
     flying = [
-        packed_part(table, label_weight, label_embed, bias, offset, rows, part_rows, groups, COST_NEXT if offset else 0)
+        packed_part(
+            later if offset else table,
+            label_weight,
+            label_embed,
+            bias,
+            offset,
+            rows,
+            part_rows,
+            groups,
+            COST_NEXT if offset else 0,
+        )
         for offset, rows in chunks
     ]
-    sets = [[documents, block_ids]]
-    if cores == 2:
-        sets.append([other_core(documents), other_core(block_ids)])
     call = functools.partial(add_labels, table)
     common = dict(parts=groups, part_rows=part_rows, reps=reps)
     history = [call(bias, [label_weight, label_embed], sets, step=0, pieces=(), **common)]

time: 107 us -> 105 us (0.981)
  Pallas kernels: 37.6 us -> 35.4 us
  starting transfers between devices: 20.2 us -> 22 us
  local copies, waits for them, and re-layouts: 3.23 us -> 1.81 us
    unnamed x11 -> x7, local copies, waits for them, and re-layouts: 3.05 us -> 0.95 us
    ppermute x23, starting transfers between devices: 20.2 us -> 22 us  [moved(): return lax.ppermute(x, AXES, pairs)]
    pallas_call x2, Pallas kernels: 4.68 us -> 3.14 us  [packed_part(): pl.pallas_call(functools.partial(pack, (offset, rows, part_rows, groups))...]
  transfers between devices with their start and end apart: 23 -> 23, of which waited for: 10 -> 9; matrix products, arithmetic and copies ran while one was open for 1% -> 2% of each run, Pallas kernels for 33% -> 32%
where the time goes in v5:
time: 105 us; the launch traced here: 104 us
  waiting for transfers between devices  44.7 us (43%)
  Pallas kernels  35.4 us (34%)
  starting transfers between devices  22 us (21%)
  local copies, waits for them, and re-layouts  1.81 us (2%)
    ppermute x23, waiting for transfers between devices, moved(): return lax.ppermute(x, AXES, pairs)  44.7 us
    pallas_call x11, Pallas kernels, add_labels(): pl.pallas_call(functools.partial(accumulate, spec), in_specs=[pl.BlockSpe...  30.1 us
    ppermute x23, starting transfers between devices, moved(): return lax.ppermute(x, AXES, pairs)  22 us
    pallas_call x2, Pallas kernels, packed_part(): pl.pallas_call(functools.partial(pack, (offset, rows, part_rows, groups))...  3.14 us
    pallas_call x2, Pallas kernels, combined(): pl.pallas_call(functools.partial(combine, (piece, count, tuple((len(array...  2.13 us
  transfers between devices with their start and end apart: 23, of which 9 were waited for; matrix products, arithmetic and copies ran while one was open for 2% of the time, Pallas kernels for 32%

profile of v5, /device:TPU:0, one launch (start us, length us, event | category | flops | bytes accessed | tf_op | source)
XLA Modules:
  0.0 104.3 jit_solution(17819802357398584079)
XLA Ops:
  2.3 1.6 %shard_map.55 = bf16[136,1792]{1,0:T(8,128)(2,1)S(1)} custom-call(s32[6]{0:T(128)S(1)} %stack.27.table, bf16[512,1024]{1,0:T(8,128)(2,1)} %weight.3, bf16[512,768]{1,0:T(8,128)(2,1)} %embed.3, bf16[1,512]{1,0:T(2,128)(2,1)S(1)} %broadcast_in_dim.3.bias.bias_ref), custom_call_target="tpu_custom_call" | custom-call | tf_op jit(solution)/shard_map/pallas_call | solution.py:217
  3.9 3.0 %collective-permute-start = (bf16[136,1792]{1,0:T(8,128)(2,1)S(1)}, bf16[136,1792]{1,0:T(8,128)(2,1)S(1)}, u32[]{:S(2)}, u32[]{:S(2)}) collective-permute-start(bf16[136,1792]{1,0:T(8,128)(2,1)S(1)} %shard_map.55), channel_id=1, source_target_pairs={{0,4},{1,5},{2,6},{3,7},{4,8},{5,9},{6,10},{7,11},{8,12},{9,13},{1... | collective-permute-start | bytes 1462280 | tf_op jit(solution)/shard_map/ppermute | solution.py:246
  7.0 1.6 %shard_map.57 = bf16[128,1792]{1,0:T(8,128)(2,1)S(1)} custom-call(s32[6]{0:T(128)S(1)} %stack.27.table, bf16[512,1024]{1,0:T(8,128)(2,1)} %weight.3, bf16[512,768]{1,0:T(8,128)(2,1)} %embed.3, bf16[1,512]{1,0:T(2,128)(2,1)S(1)} %broadcast_in_dim.3.bias.bias_ref), custom_call_target="tpu_custom_call" | custom-call | flops 13200000000 | tf_op jit(solution)/shard_map/pallas_call | solution.py:217
  8.5 1.6 %collective-permute-start.6 = (bf16[128,1792]{1,0:T(8,128)(2,1)S(1)}, bf16[128,1792]{1,0:T(8,128)(2,1)S(1)}, u32[]{:S(2)}, u32[]{:S(2)}) collective-permute-start(bf16[128,1792]{1,0:T(8,128)(2,1)S(1)} %shard_map.57), channel_id=1, source_target_pairs={{0,4},{1,5},{2,6},{3,7},{4,8},{5,9},{6,10},{7,11},{8,12},{9,13},{1... | collective-permute-start | bytes 1376264 | tf_op jit(solution)/shard_map/ppermute | solution.py:246
  10.2 4.8 %shard_map.56 = (f32[1024,768]{1,0:T(8,128)S(1)}, f32[1024,1]{1,0:T(8,128)S(1)}, f32[1024,768]{1,0:T(8,128)S(1)}, f32[1024,1]{1,0:T(8,128)S(1)}) custom-call(s32[6]{0:T(128)S(1)} %stack.27.table, bf16[1,512]{1,0:T(2,128)(2,1)S(1)} %broadcast_in_dim.3.bias.bias_ref, bf16[512,1024]{1,0:T(8,128)(2,1)S(1)} %copy-done.1, bf16[512,768]{1,0:T(8,128)(2,1)S(1)} %copy-done.2, ...), custom_call_target="tpu_custom_call" | custom-call | tf_op jit(solution)/shard_map/pallas_call | solution.py:138
  15.0 5.9 %collective-permute-done.refs_0_ = bf16[136,1792]{1,0:T(8,128)(2,1)S(1)} collective-permute-done((bf16[136,1792]{1,0:T(8,128)(2,1)S(1)}, bf16[136,1792]{1,0:T(8,128)(2,1)S(1)}, u32[]{:S(2)}, u32[]{:S(2)}) %collective-permute-start) | collective-permute-done | bytes 487456 | tf_op jit(solution)/shard_map/ppermute | solution.py:246
  21.0 1.7 %collective-permute-start.8 = (bf16[136,1792]{1,0:T(8,128)(2,1)S(1)}, bf16[136,1792]{1,0:T(8,128)(2,1)S(1)}, u32[]{:S(2)}, u32[]{:S(2)}) collective-permute-start(bf16[136,1792]{1,0:T(8,128)(2,1)S(1)} %collective-permute-done.refs_0_), channel_id=1, source_target_pairs={{0,16},{1,17},{2,18},{3,19},{4,20},{5,21},{6,22},{7,23},{8,24},{9,... | collective-permute-start | bytes 1462280 | tf_op jit(solution)/shard_map/ppermute | solution.py:246
  22.7 8.1 %collective-permute-done.6.refs_2_ = bf16[128,1792]{1,0:T(8,128)(2,1)S(1)} collective-permute-done((bf16[128,1792]{1,0:T(8,128)(2,1)S(1)}, bf16[128,1792]{1,0:T(8,128)(2,1)S(1)}, u32[]{:S(2)}, u32[]{:S(2)}) %collective-permute-start.6) | collective-permute-done | bytes 458784 | tf_op jit(solution)/shard_map/ppermute | solution.py:246
  30.8 1.8 %collective-permute-start.9 = (bf16[128,1792]{1,0:T(8,128)(2,1)S(1)}, bf16[128,1792]{1,0:T(8,128)(2,1)S(1)}, u32[]{:S(2)}, u32[]{:S(2)}) collective-permute-start(bf16[128,1792]{1,0:T(8,128)(2,1)S(1)} %collective-permute-done.6.refs_2_), channel_id=1, source_target_pairs={{0,16},{1,17},{2,18},{3,19},{4,20},{5,21},{6,22},{7,23},{8,24},{9,... | collective-permute-start | bytes 1376264 | tf_op jit(solution)/shard_map/ppermute | solution.py:246
  32.5 8.7 %collective-permute-done.3.refs_0_ = bf16[136,1792]{1,0:T(8,128)(2,1)S(1)} collective-permute-done((bf16[136,1792]{1,0:T(8,128)(2,1)S(1)}, bf16[136,1792]{1,0:T(8,128)(2,1)S(1)}, u32[]{:S(2)}, u32[]{:S(2)}) %collective-permute-start.3) | collective-permute-done | bytes 487456 | tf_op jit(solution)/shard_map/ppermute | solution.py:246
  41.2 1.7 %collective-permute-start.11 = (bf16[136,1792]{1,0:T(8,128)(2,1)S(1)}, bf16[136,1792]{1,0:T(8,128)(2,1)S(1)}, u32[]{:S(2)}, u32[]{:S(2)}) collective-permute-start(bf16[136,1792]{1,0:T(8,128)(2,1)S(1)} %collective-permute-done.3.refs_0_), channel_id=1, source_target_pairs={{0,16},{1,17},{2,18},{3,19},{4,20},{5,21},{6,22},{7,23},{8,24},{9,... | collective-permute-start | bytes 1462280 | tf_op jit(solution)/shard_map/ppermute | solution.py:246
  43.0 5.8 %shard_map.58 = (f32[1024,768]{1,0:T(8,128)S(1)}, f32[1024,1]{1,0:T(8,128)S(1)}, f32[1024,768]{1,0:T(8,128)S(1)}, f32[1024,1]{1,0:T(8,128)S(1)}, f32[8,512]{1,0:T(8,128)}) custom-call(s32[6]{0:T(128)S(1)} %stack.27.table, ...), custom_call_target="tpu_custom_call", output_to_operand_aliasing={{0}: (8, {}), {1}: (9, {}), {2}: (12, {}), {3}: (13, {})} | custom-call | tf_op jit(solution)/shard_map/pallas_call | solution.py:138
  48.8 2.3 %collective-permute-done.7.refs_2_ = bf16[128,1792]{1,0:T(8,128)(2,1)S(1)} collective-permute-done((bf16[128,1792]{1,0:T(8,128)(2,1)S(1)}, bf16[128,1792]{1,0:T(8,128)(2,1)S(1)}, u32[]{:S(2)}, u32[]{:S(2)}) %collective-permute-start.7) | collective-permute-done | bytes 458784 | tf_op jit(solution)/shard_map/ppermute | solution.py:246
  51.0 1.8 %collective-permute-start.12 = (bf16[128,1792]{1,0:T(8,128)(2,1)S(1)}, bf16[128,1792]{1,0:T(8,128)(2,1)S(1)}, u32[]{:S(2)}, u32[]{:S(2)}) collective-permute-start(bf16[128,1792]{1,0:T(8,128)(2,1)S(1)} %collective-permute-done.7.refs_2_), channel_id=1, source_target_pairs={{0,16},{1,17},{2,18},{3,19},{4,20},{5,21},{6,22},{7,23},{8,24},{9,... | collective-permute-start | bytes 1376264 | tf_op jit(solution)/shard_map/ppermute | solution.py:246
  52.8 8.7 %collective-permute-done.4.refs_0_ = bf16[136,1792]{1,0:T(8,128)(2,1)S(1)} collective-permute-done((bf16[136,1792]{1,0:T(8,128)(2,1)S(1)}, bf16[136,1792]{1,0:T(8,128)(2,1)S(1)}, u32[]{:S(2)}, u32[]{:S(2)}) %collective-permute-start.4) | collective-permute-done | bytes 487456 | tf_op jit(solution)/shard_map/ppermute | solution.py:246
  61.5 1.8 %collective-permute-start.5 = (bf16[136,1792]{1,0:T(8,128)(2,1)S(1)}, bf16[136,1792]{1,0:T(8,128)(2,1)S(1)}, u32[]{:S(2)}, u32[]{:S(2)}) collective-permute-start(bf16[136,1792]{1,0:T(8,128)(2,1)S(1)} %collective-permute-done.4.refs_0_), channel_id=1, source_target_pairs={{0,16},{1,17},{2,18},{3,19},{4,20},{5,21},{6,22},{7,23},{8,24},{9,... | collective-permute-start | bytes 1462280 | tf_op jit(solution)/shard_map/ppermute | solution.py:246
  63.3 2.0 %collective-permute-start.14 = (bf16[64,1792]{1,0:T(8,128)(2,1)S(1)}, bf16[64,1792]{1,0:T(8,128)(2,1)S(1)}, u32[]{:S(2)}, u32[]{:S(2)}) collective-permute-start(bf16[64,1792]{1,0:T(8,128)(2,1)S(1)} %slice.24), channel_id=1, source_target_pairs={{0,4},{1,5},{2,6},{3,7},{4,8},{5,9},{6,10},{7,11},{8,12},{9,13},{1... | collective-permute-start | bytes 688136 | tf_op jit(solution)/shard_map/ppermute | solution.py:246
  65.3 5.8 %shard_map.59 = (f32[1024,768]{1,0:T(8,128)S(1)}, f32[1024,1]{1,0:T(8,128)S(1)}, f32[1024,768]{1,0:T(8,128)S(1)}, f32[1024,1]{1,0:T(8,128)S(1)}, f32[8,512]{1,0:T(8,128)}) custom-call(s32[6]{0:T(128)S(1)} %stack.27.table, ...), custom_call_target="tpu_custom_call", output_to_operand_aliasing={{0}: (8, {}), {1}: (9, {}), {2}: (12, {}), {3}: (13, {})} | custom-call | tf_op jit(solution)/shard_map/pallas_call | solution.py:138
  71.3 1.8 %collective-permute-start.13 = (bf16[64,1792]{1,0:T(8,128)(2,1)S(1)}, bf16[64,1792]{1,0:T(8,128)(2,1)S(1)}, u32[]{:S(2)}, u32[]{:S(2)}) collective-permute-start(bf16[64,1792]{1,0:T(8,128)(2,1)S(1)} %slice.18), channel_id=1, source_target_pairs={{0,16},{1,17},{2,18},{3,19},{4,20},{5,21},{6,22},{7,23},{8,24},{9,... | collective-permute-start | bytes 688136 | tf_op jit(solution)/shard_map/ppermute | solution.py:246
  74.0 4.4 %shard_map.60 = (f32[1024,768]{1,0:T(8,128)S(1)}, f32[1024,1]{1,0:T(8,128)S(1)}, f32[1024,768]{1,0:T(8,128)S(1)}, f32[1024,1]{1,0:T(8,128)S(1)}, f32[8,512]{1,0:T(8,128)S(1)}) custom-call(s32[6]{0:T(128)S(1)} %stack.27.table, ...), custom_call_target="tpu_custom_call", output_to_operand_aliasing={{0}: (6, {}), {1}: (7, {}), {2}: (10, {}), {3}: (11, {})} | custom-call | tf_op jit(solution)/shard_map/pallas_call | solution.py:138
  83.0 1.3 %collective-permute-start.20 = (bf16[264,768]{1,0:T(8,128)(2,1)S(1)}, bf16[264,768]{1,0:T(8,128)(2,1)S(1)}, u32[]{:S(2)}, u32[]{:S(2)}) collective-permute-start(bf16[264,768]{1,0:T(8,128)(2,1)S(1)} %shard_map.65), channel_id=1, source_target_pairs={{0,1},{1,0},{2,3},{3,2},{4,5},{5,4},{6,7},{7,6},{8,9},{9,8},{10,11... | collective-permute-start | bytes 1216520 | tf_op jit(solution)/shard_map/ppermute | solution.py:246
  86.3 1.6 %shard_map.61 = (f32[512,768]{1,0:T(8,128)S(1)}, f32[512,1]{1,0:T(8,128)S(1)}) custom-call(s32[6]{0:T(128)S(1)} %stack.27.table, f32[8,512]{1,0:T(8,128)S(1)} %get-tuple-element.73.bias_ref, bf16[128,1792]{1,0:T(8,128)(2,1)S(1)} %collective-permute-done.10.refs_0_, bf16[64,1792]{1,0:T(8,128)(2,1)S(1)} %collective-permute-done.13.refs_1_, ...), custom_call_target="tpu_custom_call" | custom-call | tf_op jit(solution)/shard_map/pallas_call | solution.py:138
  92.0 2.9 %collective-permute-done.20.refs_0_ = bf16[264,768]{1,0:T(8,128)(2,1)S(1)} collective-permute-done((bf16[264,768]{1,0:T(8,128)(2,1)S(1)}, bf16[264,768]{1,0:T(8,128)(2,1)S(1)}, u32[]{:S(2)}, u32[]{:S(2)}) %collective-permute-start.20) | collective-permute-done | bytes 405536 | tf_op jit(solution)/shard_map/ppermute | solution.py:246
  96.0 7.1 %collective-permute-done.16.refs_0_ = bf16[264,768]{1,0:T(8,128)(2,1)S(1)} collective-permute-done((bf16[264,768]{1,0:T(8,128)(2,1)S(1)}, bf16[264,768]{1,0:T(8,128)(2,1)S(1)}, u32[]{:S(2)}, u32[]{:S(2)}) %collective-permute-start.16) | collective-permute-done | bytes 405536 | tf_op jit(solution)/shard_map/ppermute | solution.py:246
  (52 shorter events, 16.2 us)
Async XLA Ops:
  0.0 10.2 %collective-permute-start.1 = (bf16[1024,1024]{1,0:T(8,128)(2,1)}, bf16[1024,1024]{1,0:T(8,128)(2,1)S(1)}, u32[]{:S(2)}, u32[]{:S(2)}) collective-permute-start(bf16[1024,1024]{1,0:T(8,128)(2,1)} %refs_3_.7), channel_id=1, source_target_pairs={{0,2},{1,3},{2,0},{3,1},{4,6},{5,7},{6,4},{7,5},{8,10},{9,11},{10,... | collective-permute-start | bytes 6291464 | tf_op jit(solution)/shard_map/ppermute | solution.py:246
  1.4 5.6 %collective-permute-start.2 = (s32[1024,3]{1,0:T(8,128)S(1)}, s32[1024,3]{1,0:T(8,128)S(1)}, u32[]{:S(2)}, u32[]{:S(2)}) collective-permute-start(s32[1024,3]{1,0:T(8,128)S(1)} %copy.20.refs_3_.refs_5_.refs_4_), channel_id=1, source_target_pairs={{0,2},{1,3},{2,0},{3,1},{4,6},{5,7},{6,4},{7,5},{8,10},{9,11},{10,... | collective-permute-start | bytes 36872 | tf_op jit(solution)/shard_map/ppermute | solution.py:246
  3.9 6.3 %copy-start = (bf16[1024,1024]{1,0:T(8,128)(2,1)S(1)}, bf16[1024,1024]{1,0:T(8,128)(2,1)}, u32[]{:S(2)}) copy-start(bf16[1024,1024]{1,0:T(8,128)(2,1)} %refs_3_.7) | copy-start | bytes 6291460
  3.9 17.0 %collective-permute-start = (bf16[136,1792]{1,0:T(8,128)(2,1)S(1)}, bf16[136,1792]{1,0:T(8,128)(2,1)S(1)}, u32[]{:S(2)}, u32[]{:S(2)}) collective-permute-start(bf16[136,1792]{1,0:T(8,128)(2,1)S(1)} %shard_map.55), channel_id=1, source_target_pairs={{0,4},{1,5},{2,6},{3,7},{4,8},{5,9},{6,10},{7,11},{8,12},{9,13},{1... | collective-permute-start | bytes 1462280 | tf_op jit(solution)/shard_map/ppermute | solution.py:246
  8.5 22.2 %collective-permute-start.6 = (bf16[128,1792]{1,0:T(8,128)(2,1)S(1)}, bf16[128,1792]{1,0:T(8,128)(2,1)S(1)}, u32[]{:S(2)}, u32[]{:S(2)}) collective-permute-start(bf16[128,1792]{1,0:T(8,128)(2,1)S(1)} %shard_map.57), channel_id=1, source_target_pairs={{0,4},{1,5},{2,6},{3,7},{4,8},{5,9},{6,10},{7,11},{8,12},{9,13},{1... | collective-permute-start | bytes 1376264 | tf_op jit(solution)/shard_map/ppermute | solution.py:246
  20.9 20.3 %collective-permute-start.3 = (bf16[136,1792]{1,0:T(8,128)(2,1)S(1)}, bf16[136,1792]{1,0:T(8,128)(2,1)S(1)}, u32[]{:S(2)}, u32[]{:S(2)}) collective-permute-start(bf16[136,1792]{1,0:T(8,128)(2,1)S(1)} %collective-permute-done.refs_0_), channel_id=1, source_target_pairs={{0,4},{1,5},{2,6},{3,7},{4,8},{5,9},{6,10},{7,11},{8,12},{9,13},{1... | collective-permute-start | bytes 1462280 | tf_op jit(solution)/shard_map/ppermute | solution.py:246
  21.0 22.0 %collective-permute-start.8 = (bf16[136,1792]{1,0:T(8,128)(2,1)S(1)}, bf16[136,1792]{1,0:T(8,128)(2,1)S(1)}, u32[]{:S(2)}, u32[]{:S(2)}) collective-permute-start(bf16[136,1792]{1,0:T(8,128)(2,1)S(1)} %collective-permute-done.refs_0_), channel_id=1, source_target_pairs={{0,16},{1,17},{2,18},{3,19},{4,20},{5,21},{6,22},{7,23},{8,24},{9,... | collective-permute-start | bytes 1462280 | tf_op jit(solution)/shard_map/ppermute | solution.py:246
  30.8 12.2 %collective-permute-start.9 = (bf16[128,1792]{1,0:T(8,128)(2,1)S(1)}, bf16[128,1792]{1,0:T(8,128)(2,1)S(1)}, u32[]{:S(2)}, u32[]{:S(2)}) collective-permute-start(bf16[128,1792]{1,0:T(8,128)(2,1)S(1)} %collective-permute-done.6.refs_2_), channel_id=1, source_target_pairs={{0,16},{1,17},{2,18},{3,19},{4,20},{5,21},{6,22},{7,23},{8,24},{9,... | collective-permute-start | bytes 1376264 | tf_op jit(solution)/shard_map/ppermute | solution.py:246
  32.5 18.5 %collective-permute-start.7 = (bf16[128,1792]{1,0:T(8,128)(2,1)S(1)}, bf16[128,1792]{1,0:T(8,128)(2,1)S(1)}, u32[]{:S(2)}, u32[]{:S(2)}) collective-permute-start(bf16[128,1792]{1,0:T(8,128)(2,1)S(1)} %collective-permute-done.6.refs_2_), channel_id=1, source_target_pairs={{0,4},{1,5},{2,6},{3,7},{4,8},{5,9},{6,10},{7,11},{8,12},{9,13},{1... | collective-permute-start | bytes 1376264 | tf_op jit(solution)/shard_map/ppermute | solution.py:246
  41.2 20.3 %collective-permute-start.4 = (bf16[136,1792]{1,0:T(8,128)(2,1)S(1)}, bf16[136,1792]{1,0:T(8,128)(2,1)S(1)}, u32[]{:S(2)}, u32[]{:S(2)}) collective-permute-start(bf16[136,1792]{1,0:T(8,128)(2,1)S(1)} %collective-permute-done.3.refs_0_), channel_id=1, source_target_pairs={{0,4},{1,5},{2,6},{3,7},{4,8},{5,9},{6,10},{7,11},{8,12},{9,13},{1... | collective-permute-start | bytes 1462280 | tf_op jit(solution)/shard_map/ppermute | solution.py:246
  41.2 24.1 %collective-permute-start.11 = (bf16[136,1792]{1,0:T(8,128)(2,1)S(1)}, bf16[136,1792]{1,0:T(8,128)(2,1)S(1)}, u32[]{:S(2)}, u32[]{:S(2)}) collective-permute-start(bf16[136,1792]{1,0:T(8,128)(2,1)S(1)} %collective-permute-done.3.refs_0_), channel_id=1, source_target_pairs={{0,16},{1,17},{2,18},{3,19},{4,20},{5,21},{6,22},{7,23},{8,24},{9,... | collective-permute-start | bytes 1462280 | tf_op jit(solution)/shard_map/ppermute | solution.py:246
  51.0 12.2 %collective-permute-start.12 = (bf16[128,1792]{1,0:T(8,128)(2,1)S(1)}, bf16[128,1792]{1,0:T(8,128)(2,1)S(1)}, u32[]{:S(2)}, u32[]{:S(2)}) collective-permute-start(bf16[128,1792]{1,0:T(8,128)(2,1)S(1)} %collective-permute-done.7.refs_2_), channel_id=1, source_target_pairs={{0,16},{1,17},{2,18},{3,19},{4,20},{5,21},{6,22},{7,23},{8,24},{9,... | collective-permute-start | bytes 1376264 | tf_op jit(solution)/shard_map/ppermute | solution.py:246
  52.8 18.5 %collective-permute-start.10 = (bf16[128,1792]{1,0:T(8,128)(2,1)S(1)}, bf16[128,1792]{1,0:T(8,128)(2,1)S(1)}, u32[]{:S(2)}, u32[]{:S(2)}) collective-permute-start(bf16[128,1792]{1,0:T(8,128)(2,1)S(1)} %collective-permute-done.7.refs_2_), channel_id=1, source_target_pairs={{0,4},{1,5},{2,6},{3,7},{4,8},{5,9},{6,10},{7,11},{8,12},{9,13},{1... | collective-permute-start | bytes 1376264 | tf_op jit(solution)/shard_map/ppermute | solution.py:246
  61.5 12.6 %collective-permute-start.5 = (bf16[136,1792]{1,0:T(8,128)(2,1)S(1)}, bf16[136,1792]{1,0:T(8,128)(2,1)S(1)}, u32[]{:S(2)}, u32[]{:S(2)}) collective-permute-start(bf16[136,1792]{1,0:T(8,128)(2,1)S(1)} %collective-permute-done.4.refs_0_), channel_id=1, source_target_pairs={{0,16},{1,17},{2,18},{3,19},{4,20},{5,21},{6,22},{7,23},{8,24},{9,... | collective-permute-start | bytes 1462280 | tf_op jit(solution)/shard_map/ppermute | solution.py:246
  63.3 15.2 %collective-permute-start.14 = (bf16[64,1792]{1,0:T(8,128)(2,1)S(1)}, bf16[64,1792]{1,0:T(8,128)(2,1)S(1)}, u32[]{:S(2)}, u32[]{:S(2)}) collective-permute-start(bf16[64,1792]{1,0:T(8,128)(2,1)S(1)} %slice.24), channel_id=1, source_target_pairs={{0,4},{1,5},{2,6},{3,7},{4,8},{5,9},{6,10},{7,11},{8,12},{9,13},{1... | collective-permute-start | bytes 688136 | tf_op jit(solution)/shard_map/ppermute | solution.py:246
  71.3 7.2 %collective-permute-start.13 = (bf16[64,1792]{1,0:T(8,128)(2,1)S(1)}, bf16[64,1792]{1,0:T(8,128)(2,1)S(1)}, u32[]{:S(2)}, u32[]{:S(2)}) collective-permute-start(bf16[64,1792]{1,0:T(8,128)(2,1)S(1)} %slice.18), channel_id=1, source_target_pairs={{0,16},{1,17},{2,18},{3,19},{4,20},{5,21},{6,22},{7,23},{8,24},{9,... | collective-permute-start | bytes 688136 | tf_op jit(solution)/shard_map/ppermute | solution.py:246
  79.8 1.9 %collective-permute-start.17 = (bf16[264,768]{1,0:T(8,128)(2,1)S(1)}, bf16[264,768]{1,0:T(8,128)(2,1)S(1)}, u32[]{:S(2)}, u32[]{:S(2)}) collective-permute-start(bf16[264,768]{1,0:T(8,128)(2,1)S(1)} %shard_map.64), channel_id=1, source_target_pairs={{0,2},{1,3},{2,0},{3,1},{4,6},{5,7},{6,4},{7,5},{8,10},{9,11},{10,... | collective-permute-start | bytes 1216520 | tf_op jit(solution)/shard_map/ppermute | solution.py:246
  81.2 8.2 %collective-permute-start.15 = (bf16[264,768]{1,0:T(8,128)(2,1)S(1)}, bf16[264,768]{1,0:T(8,128)(2,1)S(1)}, u32[]{:S(2)}, u32[]{:S(2)}) collective-permute-start(bf16[264,768]{1,0:T(8,128)(2,1)S(1)} %shard_map.62), channel_id=1, source_target_pairs={{0,2},{1,3},{2,0},{3,1},{4,6},{5,7},{6,4},{7,5},{8,10},{9,11},{10,... | collective-permute-start | bytes 1216520 | tf_op jit(solution)/shard_map/ppermute | solution.py:246
  83.0 11.8 %collective-permute-start.20 = (bf16[264,768]{1,0:T(8,128)(2,1)S(1)}, bf16[264,768]{1,0:T(8,128)(2,1)S(1)}, u32[]{:S(2)}, u32[]{:S(2)}) collective-permute-start(bf16[264,768]{1,0:T(8,128)(2,1)S(1)} %shard_map.65), channel_id=1, source_target_pairs={{0,1},{1,0},{2,3},{3,2},{4,5},{5,4},{6,7},{7,6},{8,9},{9,8},{10,11... | collective-permute-start | bytes 1216520 | tf_op jit(solution)/shard_map/ppermute | solution.py:246
  85.7 6.3 %collective-permute-start.22 = (bf16[136,768]{1,0:T(8,128)(2,1)S(1)}, bf16[136,768]{1,0:T(8,128)(2,1)S(1)}, u32[]{:S(2)}, u32[]{:S(2)}) collective-permute-start(bf16[136,768]{1,0:T(8,128)(2,1)S(1)} %slice.28), channel_id=1, source_target_pairs={{0,2},{1,3},{2,0},{3,1},{4,6},{5,7},{6,4},{7,5},{8,10},{9,11},{10,... | collective-permute-start | bytes 626696 | tf_op jit(solution)/shard_map/ppermute | solution.py:246
  85.8 5.4 %collective-permute-start.21 = (bf16[128,768]{1,0:T(8,128)(2,1)S(1)}, bf16[128,768]{1,0:T(8,128)(2,1)S(1)}, u32[]{:S(2)}, u32[]{:S(2)}) collective-permute-start(bf16[128,768]{1,0:T(8,128)(2,1)S(1)} %slice.27), channel_id=1, source_target_pairs={{0,2},{1,3},{2,0},{3,1},{4,6},{5,7},{6,4},{7,5},{8,10},{9,11},{10,... | collective-permute-start | bytes 589832 | tf_op jit(solution)/shard_map/ppermute | solution.py:246
  89.3 6.7 %collective-permute-start.19 = (bf16[136,768]{1,0:T(8,128)(2,1)S(1)}, bf16[136,768]{1,0:T(8,128)(2,1)S(1)}, u32[]{:S(2)}, u32[]{:S(2)}) collective-permute-start(bf16[136,768]{1,0:T(8,128)(2,1)S(1)} %slice.26), channel_id=1, source_target_pairs={{0,2},{1,3},{2,0},{3,1},{4,6},{5,7},{6,4},{7,5},{8,10},{9,11},{10,... | collective-permute-start | bytes 626696 | tf_op jit(solution)/shard_map/ppermute | solution.py:246
  89.3 6.6 %collective-permute-start.18 = (bf16[128,768]{1,0:T(8,128)(2,1)S(1)}, bf16[128,768]{1,0:T(8,128)(2,1)S(1)}, u32[]{:S(2)}, u32[]{:S(2)}) collective-permute-start(bf16[128,768]{1,0:T(8,128)(2,1)S(1)} %slice.25), channel_id=1, source_target_pairs={{0,2},{1,3},{2,0},{3,1},{4,6},{5,7},{6,4},{7,5},{8,10},{9,11},{10,... | collective-permute-start | bytes 589832 | tf_op jit(solution)/shard_map/ppermute | solution.py:246
  91.1 12.0 %collective-permute-start.16 = (bf16[264,768]{1,0:T(8,128)(2,1)S(1)}, bf16[264,768]{1,0:T(8,128)(2,1)S(1)}, u32[]{:S(2)}, u32[]{:S(2)}) collective-permute-start(bf16[264,768]{1,0:T(8,128)(2,1)S(1)} %shard_map.63), channel_id=1, source_target_pairs={{0,1},{1,0},{2,3},{3,2},{4,5},{5,4},{6,7},{7,6},{8,9},{9,8},{10,11... | collective-permute-start | bytes 1216520 | tf_op jit(solution)/shard_map/ppermute | solution.py:246
  (2 other events, 12.5 us)

commit v6 on v5

--- a/solution.py
+++ b/solution.py
@@ -21,6 +21,11 @@
 
 def joined(xs, axis):
     return xs[0] if len(xs) == 1 else jnp.concatenate(xs, axis=axis)
+
+
+def in_one_row(ref):
+    rows = ref[...].astype(jnp.float32)
+    return joined([rows[k : k + 1, :] for k in range(rows.shape[0])], 1)
 
 
 def column(row):
@@ -50,7 +55,7 @@
         bias = joined(bias_rows, 1)
         weight_rows, embed_rows = joined(weight_rows, 0), joined(embed_rows, 0)
     else:
-        weight_rows, embed_rows, bias = labels[0][...], labels[1][...], bias_ref[...].astype(jnp.float32)
+        weight_rows, embed_rows, bias = labels[0][...], labels[1][...], in_one_row(bias_ref)
     block, rep = table[1 + step], table[table.shape[0] - 1]
     per_set = 2 + (0 if first else 2) + (1 if received else 0)
     kind, piece, count = where
@@ -190,7 +195,7 @@
     return out
 
 
-def pack(spec, table, weight, embed, bias, out, sems):
+def pack(spec, table, weight, embed, bias, out, near, sems):
     offset, rows, part_rows, groups = spec
     width = weight.shape[1]
     group = table[0]
@@ -202,7 +207,10 @@
     for copy in copies:
         copy.start()
     if offset == 0:
-        every = bias[...].astype(jnp.float32)
+        copy = pltpu.make_async_copy(bias, near, sems.at[2])
+        copy.start()
+        copy.wait()
+        every = in_one_row(near)
         row = every[:, :part_rows]
         for other in range(1, groups):
             row = jnp.where(group == other, every[:, other * part_rows : (other + 1) * part_rows], row)
@@ -217,14 +225,13 @@
     return pl.pallas_call(
         functools.partial(pack, (offset, rows, part_rows, groups)),
         in_specs=[pl.BlockSpec(memory_space=pltpu.SMEM)]
-        + [pl.BlockSpec(memory_space=pl.ANY)] * 2
-        + [pl.BlockSpec(memory_space=pltpu.VMEM)],
+        + [pl.BlockSpec(memory_space=pl.ANY)] * 3,
         out_specs=pl.BlockSpec(memory_space=pltpu.VMEM),
         out_shape=jax.ShapeDtypeStruct((rows + (0 if offset else BIAS_ROWS), width), weight.dtype),
-        scratch_shapes=[pltpu.SemaphoreType.DMA((2,))],
+        scratch_shapes=[pltpu.VMEM(bias.shape, bias.dtype), pltpu.SemaphoreType.DMA((3,))],
         compiler_params=pltpu.CompilerParams(vmem_limit_bytes=VMEM_LIMIT),
         cost_estimate=pl.CostEstimate(flops=cost, bytes_accessed=0, transcendentals=0),
-    )(table, *[pltpu.with_memory_space_constraint(x, pltpu.HBM) for x in (weight, embed)], bias)
+    )(table, *[pltpu.with_memory_space_constraint(x, pltpu.HBM) for x in (weight, embed, bias)])
 
 
 def per_device(sizes, documents, block_ids, label_weight, label_bias, label_embed):
@@ -260,7 +267,7 @@
     total = sum(SHARES)
     cuts = [part_rows * sum(SHARES[:k]) // total // 16 * 16 for k in range(len(SHARES))] + [part_rows]
     chunks = [(a, b - a) for a, b in zip(cuts, cuts[1:])]
-    bias = label_bias[None, :]
+    bias = label_bias.reshape(-1, 128)
     sets = [[documents, block_ids]]
     later = table
     if cores == 2:

time: 105 us -> 104 us (level)
  transfers between devices with their start and end apart: 23 -> 23, of which waited for: 9 -> 9; matrix products, arithmetic and copies ran while one was open for 2% -> 1% of each run, Pallas kernels for 32% -> 32%
where the time goes in v6:
time: 104 us
  waiting for transfers between devices  44.7 us (43%)
  Pallas kernels  35.4 us (34%)
  starting transfers between devices  22 us (21%)
  local copies, waits for them, and re-layouts  1.13 us (1%)
    ppermute x23, waiting for transfers between devices, moved(): return lax.ppermute(x, AXES, pairs)  44.7 us
    pallas_call x11, Pallas kernels, add_labels(): pl.pallas_call(functools.partial(accumulate, spec), in_specs=[pl.BlockSpe...  30.1 us
    ppermute x23, starting transfers between devices, moved(): return lax.ppermute(x, AXES, pairs)  22 us
    pallas_call x2, Pallas kernels, packed_part(): pl.pallas_call(functools.partial(pack, (offset, rows, part_rows, groups))...  3.15 us
    pallas_call x2, Pallas kernels, combined(): pl.pallas_call(functools.partial(combine, (piece, count, tuple((len(array...  2.13 us
  transfers between devices with their start and end apart: 23, of which 9 were waited for; matrix products, arithmetic and copies ran while one was open for 1% of the time, Pallas kernels for 32%

profile of v6, /device:TPU:0, one launch (start us, length us, event | category | flops | bytes accessed | tf_op | source)
XLA Modules:
  0.0 103.6 jit_solution(10157423266269004769)
XLA Ops:
  1.6 1.6 %shard_map.55 = bf16[136,1792]{1,0:T(8,128)(2,1)S(1)} custom-call(s32[6]{0:T(128)S(1)} %stack.27.table, bf16[512,1024]{1,0:T(8,128)(2,1)} %weight.3, bf16[512,768]{1,0:T(8,128)(2,1)} %embed.3, bf16[4,128]{1,0:T(4,128)(2,1)} %bitcast.7), custom_call_target="tpu_custom_call" | custom-call | tf_op jit(solution)/shard_map/pallas_call | solution.py:225
  3.3 3.0 %collective-permute-start = (bf16[136,1792]{1,0:T(8,128)(2,1)S(1)}, bf16[136,1792]{1,0:T(8,128)(2,1)S(1)}, u32[]{:S(2)}, u32[]{:S(2)}) collective-permute-start(bf16[136,1792]{1,0:T(8,128)(2,1)S(1)} %shard_map.55), channel_id=1, source_target_pairs={{0,4},{1,5},{2,6},{3,7},{4,8},{5,9},{6,10},{7,11},{8,12},{9,13},{1... | collective-permute-start | bytes 1462280 | tf_op jit(solution)/shard_map/ppermute | solution.py:253
  6.3 1.6 %shard_map.57 = bf16[128,1792]{1,0:T(8,128)(2,1)S(1)} custom-call(s32[6]{0:T(128)S(1)} %stack.27.table, bf16[512,1024]{1,0:T(8,128)(2,1)} %weight.3, bf16[512,768]{1,0:T(8,128)(2,1)} %embed.3, bf16[4,128]{1,0:T(4,128)(2,1)} %bitcast.8), custom_call_target="tpu_custom_call" | custom-call | flops 13200000000 | tf_op jit(solution)/shard_map/pallas_call | solution.py:225
  7.9 1.7 %collective-permute-start.6 = (bf16[128,1792]{1,0:T(8,128)(2,1)S(1)}, bf16[128,1792]{1,0:T(8,128)(2,1)S(1)}, u32[]{:S(2)}, u32[]{:S(2)}) collective-permute-start(bf16[128,1792]{1,0:T(8,128)(2,1)S(1)} %shard_map.57), channel_id=1, source_target_pairs={{0,4},{1,5},{2,6},{3,7},{4,8},{5,9},{6,10},{7,11},{8,12},{9,13},{1... | collective-permute-start | bytes 1376264 | tf_op jit(solution)/shard_map/ppermute | solution.py:253
  9.6 4.8 %shard_map.56 = (f32[1024,768]{1,0:T(8,128)S(1)}, f32[1024,1]{1,0:T(8,128)S(1)}, f32[1024,768]{1,0:T(8,128)S(1)}, f32[1024,1]{1,0:T(8,128)S(1)}) custom-call(s32[6]{0:T(128)S(1)} %stack.27.table, bf16[4,128]{1,0:T(4,128)(2,1)S(1)} %bitcast.9, bf16[512,1024]{1,0:T(8,128)(2,1)S(1)} %copy-done.1, bf16[512,768]{1,0:T(8,128)(2,1)S(1)} %copy-done.2, ...), custom_call_target="tpu_custom_call" | custom-call | tf_op jit(solution)/shard_map/pallas_call | solution.py:143
  14.4 5.8 %collective-permute-done.refs_0_ = bf16[136,1792]{1,0:T(8,128)(2,1)S(1)} collective-permute-done((bf16[136,1792]{1,0:T(8,128)(2,1)S(1)}, bf16[136,1792]{1,0:T(8,128)(2,1)S(1)}, u32[]{:S(2)}, u32[]{:S(2)}) %collective-permute-start) | collective-permute-done | bytes 487456 | tf_op jit(solution)/shard_map/ppermute | solution.py:253
  20.3 1.7 %collective-permute-start.8 = (bf16[136,1792]{1,0:T(8,128)(2,1)S(1)}, bf16[136,1792]{1,0:T(8,128)(2,1)S(1)}, u32[]{:S(2)}, u32[]{:S(2)}) collective-permute-start(bf16[136,1792]{1,0:T(8,128)(2,1)S(1)} %collective-permute-done.refs_0_), channel_id=1, source_target_pairs={{0,16},{1,17},{2,18},{3,19},{4,20},{5,21},{6,22},{7,23},{8,24},{9,... | collective-permute-start | bytes 1462280 | tf_op jit(solution)/shard_map/ppermute | solution.py:253
  22.0 8.1 %collective-permute-done.6.refs_2_ = bf16[128,1792]{1,0:T(8,128)(2,1)S(1)} collective-permute-done((bf16[128,1792]{1,0:T(8,128)(2,1)S(1)}, bf16[128,1792]{1,0:T(8,128)(2,1)S(1)}, u32[]{:S(2)}, u32[]{:S(2)}) %collective-permute-start.6) | collective-permute-done | bytes 458784 | tf_op jit(solution)/shard_map/ppermute | solution.py:253
  30.1 1.8 %collective-permute-start.9 = (bf16[128,1792]{1,0:T(8,128)(2,1)S(1)}, bf16[128,1792]{1,0:T(8,128)(2,1)S(1)}, u32[]{:S(2)}, u32[]{:S(2)}) collective-permute-start(bf16[128,1792]{1,0:T(8,128)(2,1)S(1)} %collective-permute-done.6.refs_2_), channel_id=1, source_target_pairs={{0,16},{1,17},{2,18},{3,19},{4,20},{5,21},{6,22},{7,23},{8,24},{9,... | collective-permute-start | bytes 1376264 | tf_op jit(solution)/shard_map/ppermute | solution.py:253
  31.9 8.7 %collective-permute-done.3.refs_0_ = bf16[136,1792]{1,0:T(8,128)(2,1)S(1)} collective-permute-done((bf16[136,1792]{1,0:T(8,128)(2,1)S(1)}, bf16[136,1792]{1,0:T(8,128)(2,1)S(1)}, u32[]{:S(2)}, u32[]{:S(2)}) %collective-permute-start.3) | collective-permute-done | bytes 487456 | tf_op jit(solution)/shard_map/ppermute | solution.py:253
  40.6 1.7 %collective-permute-start.11 = (bf16[136,1792]{1,0:T(8,128)(2,1)S(1)}, bf16[136,1792]{1,0:T(8,128)(2,1)S(1)}, u32[]{:S(2)}, u32[]{:S(2)}) collective-permute-start(bf16[136,1792]{1,0:T(8,128)(2,1)S(1)} %collective-permute-done.3.refs_0_), channel_id=1, source_target_pairs={{0,16},{1,17},{2,18},{3,19},{4,20},{5,21},{6,22},{7,23},{8,24},{9,... | collective-permute-start | bytes 1462280 | tf_op jit(solution)/shard_map/ppermute | solution.py:253
  42.3 5.8 %shard_map.58 = (f32[1024,768]{1,0:T(8,128)S(1)}, f32[1024,1]{1,0:T(8,128)S(1)}, f32[1024,768]{1,0:T(8,128)S(1)}, f32[1024,1]{1,0:T(8,128)S(1)}, f32[8,512]{1,0:T(8,128)}) custom-call(s32[6]{0:T(128)S(1)} %stack.27.table, bf16[4,128]{1,0:T(4,128)(2,1)S(1)} %bitcast.10, ...), custom_call_target="tpu_custom_call", output_to_operand_aliasing={{0}: (8, {}), {1}: (9, {}), {2}: (12, {}), {3}: (13, {})} | custom-call | tf_op jit(solution)/shard_map/pallas_call | solution.py:143
  48.1 2.3 %collective-permute-done.7.refs_2_ = bf16[128,1792]{1,0:T(8,128)(2,1)S(1)} collective-permute-done((bf16[128,1792]{1,0:T(8,128)(2,1)S(1)}, bf16[128,1792]{1,0:T(8,128)(2,1)S(1)}, u32[]{:S(2)}, u32[]{:S(2)}) %collective-permute-start.7) | collective-permute-done | bytes 458784 | tf_op jit(solution)/shard_map/ppermute | solution.py:253
  50.4 1.8 %collective-permute-start.12 = (bf16[128,1792]{1,0:T(8,128)(2,1)S(1)}, bf16[128,1792]{1,0:T(8,128)(2,1)S(1)}, u32[]{:S(2)}, u32[]{:S(2)}) collective-permute-start(bf16[128,1792]{1,0:T(8,128)(2,1)S(1)} %collective-permute-done.7.refs_2_), channel_id=1, source_target_pairs={{0,16},{1,17},{2,18},{3,19},{4,20},{5,21},{6,22},{7,23},{8,24},{9,... | collective-permute-start | bytes 1376264 | tf_op jit(solution)/shard_map/ppermute | solution.py:253
  52.1 8.7 %collective-permute-done.4.refs_0_ = bf16[136,1792]{1,0:T(8,128)(2,1)S(1)} collective-permute-done((bf16[136,1792]{1,0:T(8,128)(2,1)S(1)}, bf16[136,1792]{1,0:T(8,128)(2,1)S(1)}, u32[]{:S(2)}, u32[]{:S(2)}) %collective-permute-start.4) | collective-permute-done | bytes 487456 | tf_op jit(solution)/shard_map/ppermute | solution.py:253
  60.8 1.8 %collective-permute-start.5 = (bf16[136,1792]{1,0:T(8,128)(2,1)S(1)}, bf16[136,1792]{1,0:T(8,128)(2,1)S(1)}, u32[]{:S(2)}, u32[]{:S(2)}) collective-permute-start(bf16[136,1792]{1,0:T(8,128)(2,1)S(1)} %collective-permute-done.4.refs_0_), channel_id=1, source_target_pairs={{0,16},{1,17},{2,18},{3,19},{4,20},{5,21},{6,22},{7,23},{8,24},{9,... | collective-permute-start | bytes 1462280 | tf_op jit(solution)/shard_map/ppermute | solution.py:253
  62.6 2.0 %collective-permute-start.14 = (bf16[64,1792]{1,0:T(8,128)(2,1)S(1)}, bf16[64,1792]{1,0:T(8,128)(2,1)S(1)}, u32[]{:S(2)}, u32[]{:S(2)}) collective-permute-start(bf16[64,1792]{1,0:T(8,128)(2,1)S(1)} %slice.24), channel_id=1, source_target_pairs={{0,4},{1,5},{2,6},{3,7},{4,8},{5,9},{6,10},{7,11},{8,12},{9,13},{1... | collective-permute-start | bytes 688136 | tf_op jit(solution)/shard_map/ppermute | solution.py:253
  64.6 5.8 %shard_map.59 = (f32[1024,768]{1,0:T(8,128)S(1)}, f32[1024,1]{1,0:T(8,128)S(1)}, f32[1024,768]{1,0:T(8,128)S(1)}, f32[1024,1]{1,0:T(8,128)S(1)}, f32[8,512]{1,0:T(8,128)}) custom-call(s32[6]{0:T(128)S(1)} %stack.27.table, bf16[4,128]{1,0:T(4,128)(2,1)S(1)} %bitcast.11, ...), custom_call_target="tpu_custom_call", output_to_operand_aliasing={{0}: (8, {}), {1}: (9, {}), {2}: (12, {}), {3}: (13, {})} | custom-call | tf_op jit(solution)/shard_map/pallas_call | solution.py:143
  70.7 1.8 %collective-permute-start.13 = (bf16[64,1792]{1,0:T(8,128)(2,1)S(1)}, bf16[64,1792]{1,0:T(8,128)(2,1)S(1)}, u32[]{:S(2)}, u32[]{:S(2)}) collective-permute-start(bf16[64,1792]{1,0:T(8,128)(2,1)S(1)} %slice.18), channel_id=1, source_target_pairs={{0,16},{1,17},{2,18},{3,19},{4,20},{5,21},{6,22},{7,23},{8,24},{9,... | collective-permute-start | bytes 688136 | tf_op jit(solution)/shard_map/ppermute | solution.py:253
  73.4 4.4 %shard_map.60 = (f32[1024,768]{1,0:T(8,128)S(1)}, f32[1024,1]{1,0:T(8,128)S(1)}, f32[1024,768]{1,0:T(8,128)S(1)}, f32[1024,1]{1,0:T(8,128)S(1)}, f32[8,512]{1,0:T(8,128)S(1)}) custom-call(s32[6]{0:T(128)S(1)} %stack.27.table, bf16[4,128]{1,0:T(4,128)(2,1)S(1)} %bitcast.12, ...), custom_call_target="tpu_custom_call", output_to_operand_aliasing={{0}: (6, {}), {1}: (7, {}), {2}: (10, {}), {3}: (11, {})} | custom-call | tf_op jit(solution)/shard_map/pallas_call | solution.py:143
  82.4 1.3 %collective-permute-start.20 = (bf16[264,768]{1,0:T(8,128)(2,1)S(1)}, bf16[264,768]{1,0:T(8,128)(2,1)S(1)}, u32[]{:S(2)}, u32[]{:S(2)}) collective-permute-start(bf16[264,768]{1,0:T(8,128)(2,1)S(1)} %shard_map.65), channel_id=1, source_target_pairs={{0,1},{1,0},{2,3},{3,2},{4,5},{5,4},{6,7},{7,6},{8,9},{9,8},{10,11... | collective-permute-start | bytes 1216520 | tf_op jit(solution)/shard_map/ppermute | solution.py:253
  85.6 1.6 %shard_map.61 = (f32[512,768]{1,0:T(8,128)S(1)}, f32[512,1]{1,0:T(8,128)S(1)}) custom-call(s32[6]{0:T(128)S(1)} %stack.27.table, f32[8,512]{1,0:T(8,128)S(1)} %get-tuple-element.73.bias_ref, bf16[128,1792]{1,0:T(8,128)(2,1)S(1)} %collective-permute-done.10.refs_0_, bf16[64,1792]{1,0:T(8,128)(2,1)S(1)} %collective-permute-done.13.refs_1_, ...), custom_call_target="tpu_custom_call" | custom-call | tf_op jit(solution)/shard_map/pallas_call | solution.py:143
  91.3 2.9 %collective-permute-done.20.refs_0_ = bf16[264,768]{1,0:T(8,128)(2,1)S(1)} collective-permute-done((bf16[264,768]{1,0:T(8,128)(2,1)S(1)}, bf16[264,768]{1,0:T(8,128)(2,1)S(1)}, u32[]{:S(2)}, u32[]{:S(2)}) %collective-permute-start.20) | collective-permute-done | bytes 405536 | tf_op jit(solution)/shard_map/ppermute | solution.py:253
  95.3 7.1 %collective-permute-done.16.refs_0_ = bf16[264,768]{1,0:T(8,128)(2,1)S(1)} collective-permute-done((bf16[264,768]{1,0:T(8,128)(2,1)S(1)}, bf16[264,768]{1,0:T(8,128)(2,1)S(1)}, u32[]{:S(2)}, u32[]{:S(2)}) %collective-permute-start.16) | collective-permute-done | bytes 405536 | tf_op jit(solution)/shard_map/ppermute | solution.py:253
  (53 shorter events, 15.5 us)
Async XLA Ops:
  0.0 9.6 %collective-permute-start.1 = (bf16[1024,1024]{1,0:T(8,128)(2,1)}, bf16[1024,1024]{1,0:T(8,128)(2,1)S(1)}, u32[]{:S(2)}, u32[]{:S(2)}) collective-permute-start(bf16[1024,1024]{1,0:T(8,128)(2,1)} %refs_3_.7), channel_id=1, source_target_pairs={{0,2},{1,3},{2,0},{3,1},{4,6},{5,7},{6,4},{7,5},{8,10},{9,11},{10,... | collective-permute-start | bytes 6291464 | tf_op jit(solution)/shard_map/ppermute | solution.py:253
  1.4 4.9 %collective-permute-start.2 = (s32[1024,3]{1,0:T(8,128)S(1)}, s32[1024,3]{1,0:T(8,128)S(1)}, u32[]{:S(2)}, u32[]{:S(2)}) collective-permute-start(s32[1024,3]{1,0:T(8,128)S(1)} %copy.20.refs_3_.refs_5_.refs_4_), channel_id=1, source_target_pairs={{0,2},{1,3},{2,0},{3,1},{4,6},{5,7},{6,4},{7,5},{8,10},{9,11},{10,... | collective-permute-start | bytes 36872 | tf_op jit(solution)/shard_map/ppermute | solution.py:253
  3.2 6.3 %copy-start = (bf16[1024,1024]{1,0:T(8,128)(2,1)S(1)}, bf16[1024,1024]{1,0:T(8,128)(2,1)}, u32[]{:S(2)}) copy-start(bf16[1024,1024]{1,0:T(8,128)(2,1)} %refs_3_.7) | copy-start | bytes 6291460
  3.3 17.0 %collective-permute-start = (bf16[136,1792]{1,0:T(8,128)(2,1)S(1)}, bf16[136,1792]{1,0:T(8,128)(2,1)S(1)}, u32[]{:S(2)}, u32[]{:S(2)}) collective-permute-start(bf16[136,1792]{1,0:T(8,128)(2,1)S(1)} %shard_map.55), channel_id=1, source_target_pairs={{0,4},{1,5},{2,6},{3,7},{4,8},{5,9},{6,10},{7,11},{8,12},{9,13},{1... | collective-permute-start | bytes 1462280 | tf_op jit(solution)/shard_map/ppermute | solution.py:253
  7.9 22.2 %collective-permute-start.6 = (bf16[128,1792]{1,0:T(8,128)(2,1)S(1)}, bf16[128,1792]{1,0:T(8,128)(2,1)S(1)}, u32[]{:S(2)}, u32[]{:S(2)}) collective-permute-start(bf16[128,1792]{1,0:T(8,128)(2,1)S(1)} %shard_map.57), channel_id=1, source_target_pairs={{0,4},{1,5},{2,6},{3,7},{4,8},{5,9},{6,10},{7,11},{8,12},{9,13},{1... | collective-permute-start | bytes 1376264 | tf_op jit(solution)/shard_map/ppermute | solution.py:253
  20.3 20.3 %collective-permute-start.3 = (bf16[136,1792]{1,0:T(8,128)(2,1)S(1)}, bf16[136,1792]{1,0:T(8,128)(2,1)S(1)}, u32[]{:S(2)}, u32[]{:S(2)}) collective-permute-start(bf16[136,1792]{1,0:T(8,128)(2,1)S(1)} %collective-permute-done.refs_0_), channel_id=1, source_target_pairs={{0,4},{1,5},{2,6},{3,7},{4,8},{5,9},{6,10},{7,11},{8,12},{9,13},{1... | collective-permute-start | bytes 1462280 | tf_op jit(solution)/shard_map/ppermute | solution.py:253
  20.3 22.0 %collective-permute-start.8 = (bf16[136,1792]{1,0:T(8,128)(2,1)S(1)}, bf16[136,1792]{1,0:T(8,128)(2,1)S(1)}, u32[]{:S(2)}, u32[]{:S(2)}) collective-permute-start(bf16[136,1792]{1,0:T(8,128)(2,1)S(1)} %collective-permute-done.refs_0_), channel_id=1, source_target_pairs={{0,16},{1,17},{2,18},{3,19},{4,20},{5,21},{6,22},{7,23},{8,24},{9,... | collective-permute-start | bytes 1462280 | tf_op jit(solution)/shard_map/ppermute | solution.py:253
  30.1 12.2 %collective-permute-start.9 = (bf16[128,1792]{1,0:T(8,128)(2,1)S(1)}, bf16[128,1792]{1,0:T(8,128)(2,1)S(1)}, u32[]{:S(2)}, u32[]{:S(2)}) collective-permute-start(bf16[128,1792]{1,0:T(8,128)(2,1)S(1)} %collective-permute-done.6.refs_2_), channel_id=1, source_target_pairs={{0,16},{1,17},{2,18},{3,19},{4,20},{5,21},{6,22},{7,23},{8,24},{9,... | collective-permute-start | bytes 1376264 | tf_op jit(solution)/shard_map/ppermute | solution.py:253
  31.9 18.5 %collective-permute-start.7 = (bf16[128,1792]{1,0:T(8,128)(2,1)S(1)}, bf16[128,1792]{1,0:T(8,128)(2,1)S(1)}, u32[]{:S(2)}, u32[]{:S(2)}) collective-permute-start(bf16[128,1792]{1,0:T(8,128)(2,1)S(1)} %collective-permute-done.6.refs_2_), channel_id=1, source_target_pairs={{0,4},{1,5},{2,6},{3,7},{4,8},{5,9},{6,10},{7,11},{8,12},{9,13},{1... | collective-permute-start | bytes 1376264 | tf_op jit(solution)/shard_map/ppermute | solution.py:253
  40.5 20.3 %collective-permute-start.4 = (bf16[136,1792]{1,0:T(8,128)(2,1)S(1)}, bf16[136,1792]{1,0:T(8,128)(2,1)S(1)}, u32[]{:S(2)}, u32[]{:S(2)}) collective-permute-start(bf16[136,1792]{1,0:T(8,128)(2,1)S(1)} %collective-permute-done.3.refs_0_), channel_id=1, source_target_pairs={{0,4},{1,5},{2,6},{3,7},{4,8},{5,9},{6,10},{7,11},{8,12},{9,13},{1... | collective-permute-start | bytes 1462280 | tf_op jit(solution)/shard_map/ppermute | solution.py:253
  40.6 24.1 %collective-permute-start.11 = (bf16[136,1792]{1,0:T(8,128)(2,1)S(1)}, bf16[136,1792]{1,0:T(8,128)(2,1)S(1)}, u32[]{:S(2)}, u32[]{:S(2)}) collective-permute-start(bf16[136,1792]{1,0:T(8,128)(2,1)S(1)} %collective-permute-done.3.refs_0_), channel_id=1, source_target_pairs={{0,16},{1,17},{2,18},{3,19},{4,20},{5,21},{6,22},{7,23},{8,24},{9,... | collective-permute-start | bytes 1462280 | tf_op jit(solution)/shard_map/ppermute | solution.py:253
  50.4 12.2 %collective-permute-start.12 = (bf16[128,1792]{1,0:T(8,128)(2,1)S(1)}, bf16[128,1792]{1,0:T(8,128)(2,1)S(1)}, u32[]{:S(2)}, u32[]{:S(2)}) collective-permute-start(bf16[128,1792]{1,0:T(8,128)(2,1)S(1)} %collective-permute-done.7.refs_2_), channel_id=1, source_target_pairs={{0,16},{1,17},{2,18},{3,19},{4,20},{5,21},{6,22},{7,23},{8,24},{9,... | collective-permute-start | bytes 1376264 | tf_op jit(solution)/shard_map/ppermute | solution.py:253
  52.1 18.5 %collective-permute-start.10 = (bf16[128,1792]{1,0:T(8,128)(2,1)S(1)}, bf16[128,1792]{1,0:T(8,128)(2,1)S(1)}, u32[]{:S(2)}, u32[]{:S(2)}) collective-permute-start(bf16[128,1792]{1,0:T(8,128)(2,1)S(1)} %collective-permute-done.7.refs_2_), channel_id=1, source_target_pairs={{0,4},{1,5},{2,6},{3,7},{4,8},{5,9},{6,10},{7,11},{8,12},{9,13},{1... | collective-permute-start | bytes 1376264 | tf_op jit(solution)/shard_map/ppermute | solution.py:253
  60.8 12.6 %collective-permute-start.5 = (bf16[136,1792]{1,0:T(8,128)(2,1)S(1)}, bf16[136,1792]{1,0:T(8,128)(2,1)S(1)}, u32[]{:S(2)}, u32[]{:S(2)}) collective-permute-start(bf16[136,1792]{1,0:T(8,128)(2,1)S(1)} %collective-permute-done.4.refs_0_), channel_id=1, source_target_pairs={{0,16},{1,17},{2,18},{3,19},{4,20},{5,21},{6,22},{7,23},{8,24},{9,... | collective-permute-start | bytes 1462280 | tf_op jit(solution)/shard_map/ppermute | solution.py:253
  62.6 15.2 %collective-permute-start.14 = (bf16[64,1792]{1,0:T(8,128)(2,1)S(1)}, bf16[64,1792]{1,0:T(8,128)(2,1)S(1)}, u32[]{:S(2)}, u32[]{:S(2)}) collective-permute-start(bf16[64,1792]{1,0:T(8,128)(2,1)S(1)} %slice.24), channel_id=1, source_target_pairs={{0,4},{1,5},{2,6},{3,7},{4,8},{5,9},{6,10},{7,11},{8,12},{9,13},{1... | collective-permute-start | bytes 688136 | tf_op jit(solution)/shard_map/ppermute | solution.py:253
  70.7 7.2 %collective-permute-start.13 = (bf16[64,1792]{1,0:T(8,128)(2,1)S(1)}, bf16[64,1792]{1,0:T(8,128)(2,1)S(1)}, u32[]{:S(2)}, u32[]{:S(2)}) collective-permute-start(bf16[64,1792]{1,0:T(8,128)(2,1)S(1)} %slice.18), channel_id=1, source_target_pairs={{0,16},{1,17},{2,18},{3,19},{4,20},{5,21},{6,22},{7,23},{8,24},{9,... | collective-permute-start | bytes 688136 | tf_op jit(solution)/shard_map/ppermute | solution.py:253
  79.1 1.9 %collective-permute-start.17 = (bf16[264,768]{1,0:T(8,128)(2,1)S(1)}, bf16[264,768]{1,0:T(8,128)(2,1)S(1)}, u32[]{:S(2)}, u32[]{:S(2)}) collective-permute-start(bf16[264,768]{1,0:T(8,128)(2,1)S(1)} %shard_map.64), channel_id=1, source_target_pairs={{0,2},{1,3},{2,0},{3,1},{4,6},{5,7},{6,4},{7,5},{8,10},{9,11},{10,... | collective-permute-start | bytes 1216520 | tf_op jit(solution)/shard_map/ppermute | solution.py:253
  80.5 8.2 %collective-permute-start.15 = (bf16[264,768]{1,0:T(8,128)(2,1)S(1)}, bf16[264,768]{1,0:T(8,128)(2,1)S(1)}, u32[]{:S(2)}, u32[]{:S(2)}) collective-permute-start(bf16[264,768]{1,0:T(8,128)(2,1)S(1)} %shard_map.62), channel_id=1, source_target_pairs={{0,2},{1,3},{2,0},{3,1},{4,6},{5,7},{6,4},{7,5},{8,10},{9,11},{10,... | collective-permute-start | bytes 1216520 | tf_op jit(solution)/shard_map/ppermute | solution.py:253
  82.4 11.8 %collective-permute-start.20 = (bf16[264,768]{1,0:T(8,128)(2,1)S(1)}, bf16[264,768]{1,0:T(8,128)(2,1)S(1)}, u32[]{:S(2)}, u32[]{:S(2)}) collective-permute-start(bf16[264,768]{1,0:T(8,128)(2,1)S(1)} %shard_map.65), channel_id=1, source_target_pairs={{0,1},{1,0},{2,3},{3,2},{4,5},{5,4},{6,7},{7,6},{8,9},{9,8},{10,11... | collective-permute-start | bytes 1216520 | tf_op jit(solution)/shard_map/ppermute | solution.py:253
  85.0 6.3 %collective-permute-start.22 = (bf16[136,768]{1,0:T(8,128)(2,1)S(1)}, bf16[136,768]{1,0:T(8,128)(2,1)S(1)}, u32[]{:S(2)}, u32[]{:S(2)}) collective-permute-start(bf16[136,768]{1,0:T(8,128)(2,1)S(1)} %slice.28), channel_id=1, source_target_pairs={{0,2},{1,3},{2,0},{3,1},{4,6},{5,7},{6,4},{7,5},{8,10},{9,11},{10,... | collective-permute-start | bytes 626696 | tf_op jit(solution)/shard_map/ppermute | solution.py:253
  85.1 5.4 %collective-permute-start.21 = (bf16[128,768]{1,0:T(8,128)(2,1)S(1)}, bf16[128,768]{1,0:T(8,128)(2,1)S(1)}, u32[]{:S(2)}, u32[]{:S(2)}) collective-permute-start(bf16[128,768]{1,0:T(8,128)(2,1)S(1)} %slice.27), channel_id=1, source_target_pairs={{0,2},{1,3},{2,0},{3,1},{4,6},{5,7},{6,4},{7,5},{8,10},{9,11},{10,... | collective-permute-start | bytes 589832 | tf_op jit(solution)/shard_map/ppermute | solution.py:253
  88.6 6.7 %collective-permute-start.19 = (bf16[136,768]{1,0:T(8,128)(2,1)S(1)}, bf16[136,768]{1,0:T(8,128)(2,1)S(1)}, u32[]{:S(2)}, u32[]{:S(2)}) collective-permute-start(bf16[136,768]{1,0:T(8,128)(2,1)S(1)} %slice.26), channel_id=1, source_target_pairs={{0,2},{1,3},{2,0},{3,1},{4,6},{5,7},{6,4},{7,5},{8,10},{9,11},{10,... | collective-permute-start | bytes 626696 | tf_op jit(solution)/shard_map/ppermute | solution.py:253
  88.7 6.6 %collective-permute-start.18 = (bf16[128,768]{1,0:T(8,128)(2,1)S(1)}, bf16[128,768]{1,0:T(8,128)(2,1)S(1)}, u32[]{:S(2)}, u32[]{:S(2)}) collective-permute-start(bf16[128,768]{1,0:T(8,128)(2,1)S(1)} %slice.25), channel_id=1, source_target_pairs={{0,2},{1,3},{2,0},{3,1},{4,6},{5,7},{6,4},{7,5},{8,10},{9,11},{10,... | collective-permute-start | bytes 589832 | tf_op jit(solution)/shard_map/ppermute | solution.py:253
  90.5 12.0 %collective-permute-start.16 = (bf16[264,768]{1,0:T(8,128)(2,1)S(1)}, bf16[264,768]{1,0:T(8,128)(2,1)S(1)}, u32[]{:S(2)}, u32[]{:S(2)}) collective-permute-start(bf16[264,768]{1,0:T(8,128)(2,1)S(1)} %shard_map.63), channel_id=1, source_target_pairs={{0,1},{1,0},{2,3},{3,2},{4,5},{5,4},{6,7},{7,6},{8,9},{9,8},{10,11... | collective-permute-start | bytes 1216520 | tf_op jit(solution)/shard_map/ppermute | solution.py:253
  (3 other events, 19.0 us)
